TPU v7x, 32 devices: a whole 2x2x4 slice. The times are simulated.
32 devices in a mesh: dp: 16 (over z, y, x), head: 2 (over core).
Axes of the slice: x: 2, y: 2, z: 4, core: 2. Of those that a mesh axis runs over, the one named last changes fastest.
Arguments:
- tokens: bfloat16 [65536, 512], P('dp', 'head'), may hold values from -6 to 6
- cotangent: bfloat16 [65536, 512], P('dp', 'head'), may hold values from -6 to 6
- lengths: int32 [32], P('dp'), may hold values from 128 to 2048, as said below
- owners: int32 [5], replicated, may hold values from 0 to 15
- w_qkv: float32 [512, 3, 512], P(None, None, 'head'), may hold values from -0.25 to 0.25
- w_out: float32 [512, 512], P('head'), may hold values from -1 to 1
- w_up: float32 [512, 2048], P(None, 'head'), may hold values from -0.25 to 0.25
- w_down: float32 [2048, 512], P('head'), may hold values from -0.125 to 0.125
- ln_params: float32 [4, 512], replicated
- m_qkv: float32 [512, 3, 512], P(None, None, 'head'), may hold values from -768 to 768
- m_out: float32 [512, 512], P('head'), may hold values from -384 to 384
- m_up: float32 [512, 2048], P(None, 'head'), may hold values from -384 to 384
- m_down: float32 [2048, 512], P('head'), may hold values from -768 to 768
- m_ln: float32 [4, 512], replicated, may hold values from -768 to 768
- v_qkv: float32 [512, 3, 512], P(None, None, 'head'), may hold values from 16384 to 65536
- v_out: float32 [512, 512], P('head'), may hold values from 4096 to 16384
- v_up: float32 [512, 2048], P(None, 'head'), may hold values from 4096 to 16384
- v_down: float32 [2048, 512], P('head'), may hold values from 16384 to 65536
- v_ln: float32 [4, 512], replicated, may hold values from 16384 to 65536
Outputs:
- output: bfloat16 [65536, 512], P('dp', 'head')
- grad_tokens: bfloat16 [65536, 512], P('dp', 'head')
- owned_qkv: float32 [16, 512, 3, 512], P('dp', None, None, 'head')
- owned_out: float32 [16, 512, 512], P('dp', 'head')
- owned_up: float32 [16, 512, 2048], P('dp', None, 'head')
- owned_down: float32 [16, 2048, 512], P('dp', 'head')
- owned_ln: float32 [16, 4, 512], P('dp')
- new_qkv: float32 [512, 3, 512], P(None, None, 'head')
- new_out: float32 [512, 512], P('head')
- new_up: float32 [512, 2048], P(None, 'head')
- new_down: float32 [2048, 512], P('head')
- new_ln: float32 [4, 512], replicated
- first_qkv: float32 [512, 3, 512], P(None, None, 'head')
- first_out: float32 [512, 512], P('head')
- first_up: float32 [512, 2048], P(None, 'head')
- first_down: float32 [2048, 512], P('head')
- first_ln: float32 [4, 512], replicated
- second_qkv: float32 [512, 3, 512], P(None, None, 'head')
- second_out: float32 [512, 512], P('head')
- second_up: float32 [512, 2048], P(None, 'head')
- second_down: float32 [2048, 512], P('head')
- second_ln: float32 [4, 512], replicated
- copy_qkv: bfloat16 [512, 3, 512], P(None, None, 'head')
- copy_out: bfloat16 [512, 512], P('head')
- copy_up: bfloat16 [512, 2048], P(None, 'head')
- copy_down: bfloat16 [2048, 512], P('head')
Inputs may be any that keep to these rules, and one draw needn't show every extreme that they name: `lengths`: each length is a multiple of 128; tokens at or past it are padding, which the layer leaves unchanged.
All inputs are finite; a program needn't handle non-finite values.
Results may differ from a plain program's by a relative error of at most 0.025.
Values may be sent and summed in bfloat16 or wider, within the bound.
A program may use at most 320 MiB of HBM per device.

v0:
```python
import jax
import jax.numpy as jnp
from jax import lax
from jax.sharding import PartitionSpec as P

D = 512
HEAD_DIM = 64
FF = 2048
SPAN = 128
SEQ = 2048
STEP = 5
ROWS = 16


epsilon_norm = 1e-05
epsilon_adam = 1e-08
beta_one = 0.5
beta_two = 0.5
decay_rate = 0.1
masked_score = -1e30


def layer_norm(values, gain_vec, bias_vec):
    row_mean = jnp.mean(values, axis=-1, keepdims=True)
    centered = values - row_mean
    row_var = jnp.mean(centered * centered, axis=-1, keepdims=True)
    return centered * lax.rsqrt(row_var + epsilon_norm) * gain_vec + bias_vec


def score_bias():
    row_ids = jnp.arange(ROWS)
    col_ids = jnp.arange(SPAN)
    direct_ok = jnp.broadcast_to((col_ids[None, :] <= col_ids[:, None])[None], (ROWS, SPAN, SPAN))
    summary_ok = jnp.broadcast_to((row_ids >= 1)[:, None, None], (ROWS, SPAN, SPAN))
    allowed = jnp.concatenate([direct_ok, summary_ok], axis=2)
    log_count = jnp.log(jnp.maximum(row_ids, 1).astype(jnp.float32))
    shift = jnp.concatenate(
        [
            jnp.zeros((ROWS, SPAN, SPAN), jnp.float32),
            jnp.broadcast_to(log_count[:, None, None], (ROWS, SPAN, SPAN)),
        ],
        axis=2,
    )
    return (allowed[:, None], shift[:, None])


def adam_step(gradient, weight, moment_one, moment_two, step_rate):
    first_new = beta_one * moment_one + (1.0 - beta_one) * gradient
    second_new = beta_two * moment_two + (1.0 - beta_two) * gradient * gradient
    first_hat = first_new / (1.0 - beta_one**STEP)
    second_hat = second_new / (1.0 - beta_two**STEP)
    weight_new = weight - step_rate * (
        first_hat / (jnp.sqrt(second_hat) + epsilon_adam) + decay_rate * weight
    )
    return (weight_new, first_new, second_new)


def row_divisor():
    return jnp.maximum(jnp.arange(ROWS), 1).astype(jnp.float32)[:, None, None, None]


def split_heads(seq_qkv):
    local_heads = seq_qkv.shape[2] // HEAD_DIM
    split_rows = seq_qkv.reshape(ROWS, SPAN, 3, local_heads, HEAD_DIM)
    query_part = split_rows[:, :, 0]
    key_part = split_rows[:, :, 1]
    value_part = split_rows[:, :, 2]
    key_float = key_part.astype(jnp.float32)
    value_float = value_part.astype(jnp.float32)
    key_mean = ((jnp.cumsum(key_float, axis=0) - key_float) / row_divisor()).astype(jnp.bfloat16)
    value_mean = ((jnp.cumsum(value_float, axis=0) - value_float) / row_divisor()).astype(
        jnp.bfloat16
    )
    all_keys = jnp.concatenate([key_part, key_mean], axis=1)
    all_values = jnp.concatenate([value_part, value_mean], axis=1)
    allowed, shift = score_bias()
    raw_scores = jnp.einsum(
        "rqhe,rkhe->rhqk", query_part, all_keys, preferred_element_type=jnp.float32
    )
    scores = jnp.where(allowed, raw_scores * float(HEAD_DIM) ** (-0.5) + shift, masked_score)
    return (query_part, all_keys, all_values, scores, local_heads)


def attend(seq_qkv):
    query_part, all_keys, all_values, scores, local_heads = split_heads(seq_qkv)
    row_max = jnp.max(scores, axis=-1, keepdims=True)
    expo = jnp.exp(scores - row_max)
    row_total = jnp.sum(expo, axis=-1, keepdims=True)
    prob_rows = expo / row_total
    log_total = row_max + jnp.log(row_total)
    context = jnp.einsum(
        "rhqk,rkhe->rqhe",
        prob_rows.astype(jnp.bfloat16),
        all_values,
        preferred_element_type=jnp.float32,
    )
    return (context.astype(jnp.bfloat16).reshape(SEQ, local_heads * HEAD_DIM), log_total)


def spread_back(grad_mean):
    scaled = grad_mean / row_divisor()
    return jnp.sum(scaled, axis=0, keepdims=True) - jnp.cumsum(scaled, axis=0)


def attend_back(packed):
    seq_qkv, log_total, grad_context = packed
    query_part, all_keys, all_values, scores, local_heads = split_heads(seq_qkv)
    scale_factor = float(HEAD_DIM) ** (-0.5)
    prob_rows = jnp.exp(scores - log_total)
    grad_ctx_rows = grad_context.reshape(ROWS, SPAN, local_heads, HEAD_DIM)
    grad_prob = jnp.einsum(
        "rqhe,rkhe->rhqk", grad_ctx_rows, all_values, preferred_element_type=jnp.float32
    )
    delta_rows = jnp.sum(grad_prob * prob_rows, axis=-1, keepdims=True)
    grad_scores = (prob_rows * (grad_prob - delta_rows)).astype(jnp.bfloat16)
    grad_query = (
        jnp.einsum("rhqk,rkhe->rqhe", grad_scores, all_keys, preferred_element_type=jnp.float32)
        * scale_factor
    )
    grad_keys = (
        jnp.einsum("rhqk,rqhe->rkhe", grad_scores, query_part, preferred_element_type=jnp.float32)
        * scale_factor
    )
    grad_values = jnp.einsum(
        "rhqk,rqhe->rkhe",
        prob_rows.astype(jnp.bfloat16),
        grad_ctx_rows,
        preferred_element_type=jnp.float32,
    )
    grad_key = grad_keys[:, :SPAN] + spread_back(grad_keys[:, SPAN:])
    grad_value = grad_values[:, :SPAN] + spread_back(grad_values[:, SPAN:])
    stacked = jnp.stack([grad_query, grad_key, grad_value], axis=2).astype(jnp.bfloat16)
    return stacked.reshape(SEQ, 3, local_heads * HEAD_DIM)


def body(
    tokens,
    cotangent,
    lengths,
    owners,
    w_qkv,
    w_out,
    w_up,
    w_down,
    ln_params,
    m_qkv,
    m_out,
    m_up,
    m_down,
    m_ln,
    v_qkv,
    v_out,
    v_up,
    v_down,
    v_ln,
):
    token_full, cot_full = (
        lax.all_gather(tokens, "head", axis=1, tiled=True),
        lax.all_gather(cotangent, "head", axis=1, tiled=True),
    )
    token_rows = token_full.astype(jnp.float32)
    cot_rows = cot_full.astype(jnp.float32)
    seq_count = lengths.shape[0]
    positions = jnp.arange(SEQ, dtype=jnp.int32)
    valid_rows = (
        (positions[None, :] < lengths[:, None]).astype(jnp.float32).reshape(seq_count * SEQ, 1)
    )
    qkv_low = w_qkv.astype(jnp.bfloat16)
    out_low = w_out.astype(jnp.bfloat16)
    up_low = w_up.astype(jnp.bfloat16)
    down_low = w_down.astype(jnp.bfloat16)
    normed_one, norm_back_one = jax.vjp(layer_norm, token_rows, ln_params[0], ln_params[1])
    normed_one_low = normed_one.astype(jnp.bfloat16)
    projected = jnp.einsum(
        "sd,dce->sce", normed_one_low, qkv_low, preferred_element_type=jnp.float32
    ).astype(jnp.bfloat16)
    width_local = projected.shape[2]
    seq_qkv = projected.reshape(seq_count, SEQ, 3, width_local)
    contexts, log_totals = lax.map(attend, seq_qkv)
    context = contexts.reshape(seq_count * SEQ, width_local)
    attn_part = jnp.dot(context, out_low, preferred_element_type=jnp.float32)
    attn_out = lax.psum(attn_part.astype(jnp.bfloat16), "head").astype(jnp.float32)
    residual = token_rows + valid_rows * attn_out
    normed_two, norm_back_two = jax.vjp(layer_norm, residual, ln_params[2], ln_params[3])
    normed_two_low = normed_two.astype(jnp.bfloat16)
    up_proj = jnp.dot(normed_two_low, up_low, preferred_element_type=jnp.float32)
    hidden_float, gelu_back = jax.vjp(lambda inner: jax.nn.gelu(inner, approximate=False), up_proj)
    hidden = hidden_float.astype(jnp.bfloat16)
    mlp_part = jnp.dot(hidden, down_low, preferred_element_type=jnp.float32)
    mlp_cols = lax.psum_scatter(
        mlp_part.astype(jnp.bfloat16), "head", scatter_dimension=1, tiled=True
    ).astype(jnp.float32)
    col_width = mlp_cols.shape[1]
    col_start = lax.axis_index("head") * col_width
    residual_cols = lax.dynamic_slice_in_dim(residual, col_start, col_width, 1)
    output_rows = (residual_cols + valid_rows * mlp_cols).astype(jnp.bfloat16)
    grad_mlp = (valid_rows * cot_rows).astype(jnp.bfloat16)
    grad_down = jnp.einsum("sf,sd->fd", hidden, grad_mlp, preferred_element_type=jnp.float32)
    grad_hidden = jnp.einsum("sd,fd->sf", grad_mlp, down_low, preferred_element_type=jnp.float32)
    grad_up_proj = gelu_back(grad_hidden)[0].astype(jnp.bfloat16)
    grad_up = jnp.einsum(
        "sd,sf->df", normed_two_low, grad_up_proj, preferred_element_type=jnp.float32
    )
    grad_normed_two = lax.psum(
        jnp.einsum("sf,df->sd", grad_up_proj, up_low, preferred_element_type=jnp.float32).astype(
            jnp.bfloat16
        ),
        "head",
    ).astype(jnp.float32)
    grad_res_norm, grad_gain_two, grad_bias_two = norm_back_two(grad_normed_two)
    grad_residual = cot_rows + grad_res_norm
    grad_attn = (valid_rows * grad_residual).astype(jnp.bfloat16)
    grad_out = jnp.einsum("sh,sd->hd", context, grad_attn, preferred_element_type=jnp.float32)
    grad_context = jnp.einsum(
        "sd,hd->sh", grad_attn, out_low, preferred_element_type=jnp.float32
    ).astype(jnp.bfloat16)
    grad_seq = lax.map(
        attend_back, (seq_qkv, log_totals, grad_context.reshape(seq_count, SEQ, width_local))
    )
    grad_projected = grad_seq.reshape(seq_count * SEQ, 3, width_local)
    grad_qkv = jnp.einsum(
        "sd,sce->dce", normed_one_low, grad_projected, preferred_element_type=jnp.float32
    )
    grad_normed_one = lax.psum(
        jnp.einsum(
            "sce,dce->sd", grad_projected, qkv_low, preferred_element_type=jnp.float32
        ).astype(jnp.bfloat16),
        "head",
    ).astype(jnp.float32)
    grad_tok_norm, grad_gain_one, grad_bias_one = norm_back_one(grad_normed_one)
    grad_token_rows = grad_residual + grad_tok_norm
    grad_input = lax.dynamic_slice_in_dim(grad_token_rows, col_start, col_width, 1).astype(
        jnp.bfloat16
    )
    grad_ln = jnp.stack([grad_gain_one, grad_bias_one, grad_gain_two, grad_bias_two])
    masters = (w_qkv, w_out, w_up, w_down, ln_params)
    firsts = (m_qkv, m_out, m_up, m_down, m_ln)
    seconds = (v_qkv, v_out, v_up, v_down, v_ln)
    rates = (
        float(D) ** (-0.5),
        4.0 * float(D) ** (-0.5),
        float(D) ** (-0.5),
        float(FF) ** (-0.5),
        0.7,
    )
    summed = lax.psum((grad_qkv, grad_out, grad_up, grad_down, grad_ln), "dp")
    updated = [
        adam_step(
            summed[kind_index],
            masters[kind_index],
            firsts[kind_index],
            seconds[kind_index],
            rates[kind_index],
        )
        for kind_index in range(5)
    ]
    new_weights = tuple((entry[0] for entry in updated))
    new_firsts = tuple((entry[1] for entry in updated))
    new_seconds = tuple((entry[2] for entry in updated))
    device_index = lax.axis_index("dp")
    owned_grads = tuple(
        (
            jnp.where(owners[kind_index] == device_index, summed[kind_index], 0.0)[None]
            for kind_index in range(5)
        )
    )
    copies = tuple((new_weights[kind_index].astype(jnp.bfloat16) for kind_index in range(4)))
    return (
        (output_rows, grad_input)
        + owned_grads
        + tuple(new_weights)
        + tuple(new_firsts)
        + tuple(new_seconds)
        + copies
    )


def solution(mesh):
    placed = (
        P("dp", "head"),
        P("dp", "head"),
        P("dp"),
        P(),
        P(None, None, "head"),
        P("head", None),
        P(None, "head"),
        P("head", None),
        P(),
        P(None, None, "head"),
        P("head", None),
        P(None, "head"),
        P("head", None),
        P(),
        P(None, None, "head"),
        P("head", None),
        P(None, "head"),
        P("head", None),
        P(),
    )
    return jax.shard_map(
        body,
        mesh=mesh,
        in_specs=placed,
        out_specs=(
            P("dp", "head"),
            P("dp", "head"),
            P("dp", None, None, "head"),
            P("dp", "head", None),
            P("dp", None, "head"),
            P("dp", "head", None),
            P("dp", None, None),
            P(None, None, "head"),
            P("head", None),
            P(None, "head"),
            P("head", None),
            P(),
            P(None, None, "head"),
            P("head", None),
            P(None, "head"),
            P("head", None),
            P(),
            P(None, None, "head"),
            P("head", None),
            P(None, "head"),
            P("head", None),
            P(),
            P(None, None, "head"),
            P("head", None),
            P(None, "head"),
            P("head", None),
        ),
        check_vma=False,
    )
```

profile of v0, /device:TPU:0, one launch (start us, length us, event | category | flops | bytes accessed | tf_op | source)
XLA Modules:
  0.0 655.5 jit_solution(235247026467546465)
XLA Ops:
  9.4 15.8 %all-gather.3.cloned.1.call-done = bf16[4096,512]{1,0:T(8,128)(2,1)} async-done(((bf16[4096,256]{1,0:T(8,128)(2,1)}), bf16[4096,512]{1,0:T(8,128)(2,1)}) %all-gather.3.cloned.1.call-update) | async-done | bytes 4194320 | tf_op jit(solution)/shard_map/all_gather | solution.py:158
  25.3 3.0 convert_reduce_fusion.2
  31.2 6.1 convolution_convert_fusion
  37.3 8.7 %copy.78 = bf16[2,2048,3,256]{1,3,2,0:T(8,128)(2,1)} copy(bf16[2,2048,3,256]{3,1,0,2:T(8,128)(2,1)} %bitcast.193) | data formatting | bytes 12582912 | tf_op jit(solution)/shard_map/while | solution.py:179
  46.0 41.1 %while.22 = (s32[]{:T(128)}, bf16[2,2048,256]{2,1,0:T(8,128)(2,1)}, f32[2,16,4,128,1]{3,2,1,4,0:T(4,128)S(1)}, bf16[2,2048,3,256]{1,3,2,0:T(8,128)(2,1)}, s32[]{:T(128)}, /*index=5*/f32[]{:T(128)}) while((s32[]{:T(128)}, bf16[2,2048,256]{2,1,0:T(8,128)(2,1)}, f32[2,16,4,128,1]{3,2,1,4,0:T(4,128)S(1)}, bf16[2,2048,3,256]{1,3,2,0:T(8,128)(2,1)}, ...), condition=%wide.region_7.8_spmd, body=%wide.region_2.7_spmd.sunk | while | flops 598745216 | bytes 78938552 | solution.py:179
  54.9 3.5 fusion.177
  58.4 4.4 fusion.179
  75.5 3.5 fusion.177
  78.9 4.4 fusion.179
  87.2 4.9 convolution_convert_fusion.3
  93.2 28.6 %all-reduce.8.cloned.1.call-done = bf16[4096,512]{1,0:T(8,128)(2,1)} async-done(((bf16[4096,512]{1,0:T(8,128)(2,1)}), bf16[4096,512]{1,0:T(8,128)(2,1)}) %all-reduce.8.cloned.1.call-update) | async-done | bytes 4194320 | tf_op jit(solution)/shard_map/psum | solution.py:182
  121.9 4.6 fusion.127
  130.4 8.9 %fusion.103 = f32[4096,1024]{1,0:T(8,128)} fusion(f32[512,1024]{1,0:T(8,128)S(1)} %copy-done.16, f32[4096,512]{1,0:T(8,128)S(1)} %get-tuple-element.160, f32[512]{0:T(512)S(1)} %bitcast.215, f32[512]{0:T(512)S(1)} %bitcast.200, f32[4096]{0:T(1024)S(1)} %fusion.111, f32[4096]{0:T(1024)S(1)} %broadcast_multiply_fusion), kind=kOutput, calls=%fused_computation.176 | convolution fusion | flops 4305977344 | bytes 27299840 | tf_op jit(solution)/shard_map/dot_general | solution.py:186
  139.3 46.6 %add_convert_fusion = (bf16[4096,1024]{1,0:T(8,128)(2,1)S(1)}, f32[4096,1024]{1,0:T(8,128)}) fusion(f32[4096,1024]{1,0:T(8,128)} %fusion.103, f32[1024,512]{1,0:T(8,128)} %param.30, bf16[4096,512]{1,0:T(8,128)(2,1)} %all-gather.5.cloned.1.call-done, f32[4096]{0:T(1024)S(1)} %bitcast.195), kind=kOutput, calls=%fused_computation.92 | convolution fusion | flops 4603772928 | bytes 48250880 | tf_op jit(solution)/shard_map/sd,fd->sf/dot_general | solution.py:199
  185.9 3.3 copy-done.63
  189.1 6.6 %convolution_convert_fusion.1 = bf16[4096,512]{1,0:T(8,128)(2,1)} fusion(bf16[4096,1024]{1,0:T(8,128)(2,1)S(1)} %get-tuple-element.157, f32[512,1024]{1,0:T(8,128)S(1)} %copy-done.16), kind=kOutput, calls=%fused_computation.141 | convolution fusion | flops 4297588736 | bytes 14680064 | tf_op jit(solution)/shard_map/sf,df->sd/dot_general | solution.py:205
  195.9 29.7 %all-reduce.10.cloned.1.call-done = bf16[4096,512]{1,0:T(8,128)(2,1)} async-done(((bf16[4096,512]{1,0:T(8,128)(2,1)}), bf16[4096,512]{1,0:T(8,128)(2,1)}) %all-reduce.10.cloned.1.call-update) | async-done | bytes 4194320 | tf_op jit(solution)/shard_map/psum | solution.py:204
  225.6 5.8 fusion.81
  231.5 7.9 %fusion.85 = (f32[512]{0:T(512)}, f32[4096]{0:T(1024)S(1)}, f32[512]{0:T(512)}) fusion(bf16[4096,512]{1,0:T(8,128)(2,1)S(1)} %copy-done.9, f32[4096,512]{1,0:T(8,128)} %copy-done.2, f32[4096]{0:T(1024)S(1)} %copy-done.39, f32[4096]{0:T(1024)S(1)} %copy-done.32, f32[4096]{0:T(1024)S(1)} %multiply_multiply_fusion.10, f32[512]{0:T(512)S(1)} %bitcast.202), kind=kLoop, calls=%fused_computation.134 | loop fusion | flops 25160704 | bytes 12654592 | tf_op jit(solution)/shard_map/transpose(jvp())/reduce_sum | solution.py:27
  239.4 4.4 convert_add_fusion.1
  247.1 101.1 %while.23 = (s32[]{:T(128)}, bf16[2,2048,3,256]{3,1,0,2:T(8,128)(2,1)}, bf16[2,2048,3,256]{1,3,2,0:T(8,128)(2,1)}, f32[2,16,4,128,1]{3,2,1,4,0:T(4,128)S(1)}, bf...) while((s32[]{:T(128)}, bf16[2,2048,3,256]{3,1,0,2:T(8,128)(2,1)}, ...), condition=%wide.region_23.24_spmd, body=%wide.region_15.23_spmd.sunk | while | flops 1424433280 | bytes 232457040 | solution.py:217
  267.9 4.0 subtract_exponential_fusion.3
  279.4 2.8 multiply_bitcast_fusion.2
  284.1 2.9 fusion.192
  295.4 2.9 copy.180
  298.3 3.9 constant_dynamic-update-slice_fusion.5
  313.4 4.0 subtract_exponential_fusion.3
  324.9 2.8 multiply_bitcast_fusion.2
  329.7 2.9 fusion.192
  341.0 2.9 copy.180
  343.9 3.9 constant_dynamic-update-slice_fusion.5
  348.2 8.7 %bitcast_convert_fusion = bf16[4096,512]{1,0:T(8,128)(2,1)} fusion(bf16[4096,3,256]{2,0,1:T(8,128)(2,1)} %bitcast.217, f32[512,3,256]{2,0,1:T(8,128)} %param.27), kind=kOutput, calls=%fused_computation.136 | convolution fusion | flops 3223715840 | bytes 12058624 | tf_op jit(solution)/shard_map/sce,dce->sd/dot_general | solution.py:225
  356.9 13.9 %multiply_convert_fusion.2 = bf16[4096,1024]{1,0:T(8,128)(2,1)S(1)} fusion(f32[4096,1024]{1,0:T(8,128)} %get-tuple-element.158, f32[4096,1024]{1,0:T(8,128)} %fusion.103), kind=kLoop, calls=%fused_computation.93 | loop fusion | flops 12582912 | bytes 41943040 | tf_op jit(solution)/shard_map/convert_element_type | solution.py:188
  370.8 3.3 copy-done.12
  374.1 6.2 convolution_convert_fusion.2
  381.1 11.6 %fusion.91 = f32[1024,512]{1,0:T(8,128)} fusion(bf16[4096,1024]{1,0:T(8,128)(2,1)} %copy-done.12, bf16[4096,512]{1,0:T(8,128)(2,1)} %all-gather.5.cloned.1.call-done, f32[4096]{0:T(1024)S(1)} %bitcast.197), kind=kOutput, calls=%fused_computation.162 | convolution fusion | flops 4301258752 | bytes 14696448 | tf_op jit(solution)/shard_map/sf,sd->fd/dot_general | solution.py:198
  392.7 13.4 %fusion.115 = f32[512,1024]{1,0:T(8,128)} fusion(bf16[4096,1024]{1,0:T(8,128)(2,1)} %copy-done.63, f32[4096,512]{1,0:T(8,128)} %copy-done.2, f32[512]{0:T(512)S(1)} %bitcast.216, f32[512]{0:T(512)S(1)} %bitcast.204, f32[4096]{0:T(1024)S(1)} %copy-done.40, f32[4096]{0:T(1024)S(1)} %copy-done.33), kind=kOutput, calls=%fused_computation.202 | convolution fusion | flops 4305453056 | bytes 18911232 | tf_op jit(solution)/shard_map/sd,sf->df/dot_general | solution.py:201
  408.6 5.4 fusion.96
  418.5 6.0 fusion.86
  424.6 45.5 %psum.63 = f32[4,512]{1,0:T(4,128)S(1)} all-reduce(f32[4,512]{1,0:T(4,128)S(1)} %pad_maximum_fusion.4), channel_id=1, replica_groups=mesh['dp'=16,'head'=2] {'dp'}, use_global_device_ids=true, to_apply=%region_35.36 | all-reduce | flops 2048 | bytes 16384 | tf_op jit(solution)/shard_map/psum | solution.py:246
  470.2 6.2 fusion.125
  477.1 3.6 fusion.88
  480.6 4.9 add_convert_fusion.2
  485.6 143.7 %all-reduce.14.cloned.1.call-done = (f32[512,3,256]{2,0,1:T(8,128)}, f32[256,512]{1,0:T(8,128)}, f32[512,1024]{1,0:T(8,128)}, f32[1024,512]{1,0:T(8,128)}) async-done(((f32[512,3,256]{2,0,1:T(8,128)}, f32[256,512]{1,0:T(8,128)}, f32[512,1024]{1,0:T(8,128)}, f32[1024,512]{1,0:T(8,128)}), (f32[512,3,256]{2,0,1:T(8,128)}, f32[256,512]{1,0:T(8,128)}, f32[512,1024]{1,0:T(8,128)}, ...) | async-done | bytes 6291472 | tf_op jit(solution)/shard_map/psum | solution.py:246
  629.3 3.0 fusion.120
  632.4 5.9 fusion.122
  638.4 5.1 fusion.118
  643.6 4.9 fusion.116
  (295 shorter events, 101.5 us)
Async XLA Ops:
  7.2 18.1 %all-gather.3.cloned.1.call-start = ((), (), s32[]{:S(2)}) async-start(), calls=%async_computation.1 | async-start | bytes 6291456 | tf_op jit(solution)/shard_map/all_gather | solution.py:158
  7.9 113.9 %all-reduce.8.cloned.1.call-start = ((), (), s32[]{:S(2)}) async-start(), calls=%async_computation.2 | async-start | bytes 8388608 | tf_op jit(solution)/shard_map/psum | solution.py:182
  9.4 21.7 %copy-start.51 = (f32[1,512]{1,0:T(1,128)}, f32[1,512]{1,0:T(1,128)S(1)}, u32[]{:S(2)}) copy-start(f32[1,512]{1,0:T(1,128)S(1)} %get-tuple-element.182) | copy-start | bytes 6148
  9.4 21.8 %copy-start.58 = (f32[1,512]{1,0:T(1,128)}, f32[1,512]{1,0:T(1,128)S(1)}, u32[]{:S(2)}) copy-start(f32[1,512]{1,0:T(1,128)S(1)} %get-tuple-element.181) | copy-start | bytes 6148
  25.3 5.9 copy-start.25
  28.7 8.6 %copy-start.36 = (f32[4096]{0:T(1024)}, f32[4096]{0:T(1024)S(1)}, u32[]{:S(2)}) copy-start(f32[4096]{0:T(1024)S(1)} %broadcast_multiply_fusion.1) | copy-start | bytes 49156
  31.2 6.2 copy-start.45
  92.1 47.2 %all-gather.5.cloned.1.call-start = ((), (), s32[]{:S(2)}) async-start(), calls=%async_computation.4 | async-start | bytes 6291456 | tf_op jit(solution)/shard_map/all_gather | solution.py:159
  92.8 132.7 %all-reduce.10.cloned.1.call-start = ((), (), s32[]{:S(2)}) async-start(), calls=%async_computation.5 | async-start | bytes 8388608 | tf_op jit(solution)/shard_map/psum | solution.py:204
  93.2 150.6 %copy-start.28 = (f32[1,16,2,128]{3,1,2,0:T(8,128)}, f32[1,16,2,128]{3,1,2,0:T(8,128)S(1)}, u32[]{:S(2)}) copy-start(f32[1,16,2,128]{3,1,2,0:T(8,128)S(1)} %copy.103) | copy-start | bytes 49156
  128.2 11.1 %copy-start.43 = (f32[4096]{0:T(1024)}, f32[4096]{0:T(1024)S(1)}, u32[]{:S(2)}) copy-start(f32[4096]{0:T(1024)S(1)} %multiply_reduce_fusion.1) | copy-start | bytes 49156
  128.3 11.0 %copy-start.38 = (f32[4096]{0:T(1024)}, f32[4096]{0:T(1024)S(1)}, u32[]{:S(2)}) copy-start(f32[4096]{0:T(1024)S(1)} %fusion.111) | copy-start | bytes 49156
  195.7 29.8 %copy-start.32 = (f32[4096]{0:T(1024)S(1)}, f32[4096]{0:T(1024)}, u32[]{:S(2)}) copy-start(f32[4096]{0:T(1024)} %copy-done.31) | copy-start | bytes 49156
  195.7 29.8 %copy-start.49 = (f32[1,512]{1,0:T(1,128)S(1)}, f32[1,512]{1,0:T(1,128)}, u32[]{:S(2)}) copy-start(f32[1,512]{1,0:T(1,128)} %get-tuple-element.180) | copy-start | bytes 6148
  195.8 222.7 %all-reduce.12.cloned.1.call-start = ((), (), s32[]{:S(2)}) async-start(), calls=%async_computation.6 | async-start | bytes 8388608 | tf_op jit(solution)/shard_map/psum | solution.py:224
  195.8 35.6 %copy-start.44 = (f32[4096]{0:T(1024)S(1)}, f32[4096]{0:T(1024)}, u32[]{:S(2)}) copy-start(f32[4096]{0:T(1024)} %copy-done.43) | copy-start | bytes 49156
  195.8 35.6 %copy-start.39 = (f32[4096]{0:T(1024)S(1)}, f32[4096]{0:T(1024)}, u32[]{:S(2)}) copy-start(f32[4096]{0:T(1024)} %copy-done.38) | copy-start | bytes 49156
  225.6 5.9 copy-start.9
  225.6 13.8 %slice-start = ((s8[8388608]{0:T(1024)(128)(4,1)}), s8[4194304]{0:T(1024)(128)(4,1)S(1)}, s32[]{:S(2)}) async-start(s8[8388608]{0:T(1024)(128)(4,1)} %bitcast.186), calls=%async_computation.8 | async-start | bytes 8388608
  231.5 7.9 %slice-start.1 = ((s8[8388608]{0:T(1024)(128)(4,1)}), s8[4194304]{0:T(1024)(128)(4,1)S(1)}, s32[]{:S(2)}) async-start(s8[8388608]{0:T(1024)(128)(4,1)} %bitcast.186), calls=%async_computation.9 | async-start | bytes 8388608
  231.5 7.9 %copy-start.15 = (bf16[4096,512]{1,0:T(8,128)(2,1)S(1)}, bf16[4096,512]{1,0:T(8,128)(2,1)}, u32[]{:S(2)}) copy-start(bf16[4096,512]{1,0:T(8,128)(2,1)} %all-gather.5.cloned.1.call-done) | copy-start | bytes 12582916
  356.9 123.8 %reduce-scatter.2.cloned.1.call-start = ((), (), s32[]{:S(2)}) async-start(), calls=%async_computation.3 | async-start | bytes 6291456 | tf_op jit(solution)/shard_map/reduce_scatter | solution.py:190
  356.9 17.2 %copy-start.20 = (f32[1024,512]{1,0:T(8,128)S(1)}, f32[1024,512]{1,0:T(8,128)}, u32[]{:S(2)}) copy-start(f32[1024,512]{1,0:T(8,128)} %param.30) | copy-start | bytes 6291460
  380.4 12.3 %copy-start.33 = (f32[4096]{0:T(1024)S(1)}, f32[4096]{0:T(1024)}, u32[]{:S(2)}) copy-start(f32[4096]{0:T(1024)} %copy-done.31) | copy-start | bytes 49156
  380.4 12.3 %copy-start.40 = (f32[4096]{0:T(1024)S(1)}, f32[4096]{0:T(1024)}, u32[]{:S(2)}) copy-start(f32[4096]{0:T(1024)} %copy-done.38) | copy-start | bytes 49156
  380.4 12.3 %copy-start.50 = (f32[1,512]{1,0:T(1,128)S(1)}, f32[1,512]{1,0:T(1,128)}, u32[]{:S(2)}) copy-start(f32[1,512]{1,0:T(1,128)} %get-tuple-element.180) | copy-start | bytes 6148
  380.4 12.3 %copy-start.61 = (f32[1,512]{1,0:T(1,128)S(1)}, f32[1,512]{1,0:T(1,128)}, u32[]{:S(2)}) copy-start(f32[1,512]{1,0:T(1,128)} %get-tuple-element.183) | copy-start | bytes 6148
  380.4 248.9 %all-reduce.14.cloned.1.call-start = ((), (), s32[]{:S(2)}) async-start(), calls=%async_computation.7 | async-start | bytes 12582912 | tf_op jit(solution)/shard_map/psum | solution.py:246
  381.0 25.1 %slice-start.2 = ((s8[8388608]{0:T(1024)(128)(4,1)}), s8[4194304]{0:T(1024)(128)(4,1)S(1)}, s32[]{:S(2)}) async-start(s8[8388608]{0:T(1024)(128)(4,1)} %bitcast.188), calls=%async_computation.10 | async-start | bytes 8388608
  381.1 27.5 %slice-start.4 = ((s8[6291456]{0:T(1024)(128)(4,1)}), s8[4194304]{0:T(1024)(128)(4,1)S(1)}, s32[]{:S(2)}) async-start(s8[6291456]{0:T(1024)(128)(4,1)} %bitcast.218), calls=%async_computation.12 | async-start | bytes 8388608
  392.7 13.5 %slice-start.3 = ((s8[8388608]{0:T(1024)(128)(4,1)}), s8[4194304]{0:T(1024)(128)(4,1)S(1)}, s32[]{:S(2)}) async-start(s8[8388608]{0:T(1024)(128)(4,1)} %bitcast.188), calls=%async_computation.11 | async-start | bytes 8388608
  392.7 13.5 %copy-start.10 = (bf16[2,2048,256]{2,1,0:T(8,128)(2,1)S(1)}, bf16[2,2048,256]{2,1,0:T(8,128)(2,1)}, u32[]{:S(2)}) copy-start(bf16[2,2048,256]{2,1,0:T(8,128)(2,1)} %get-tuple-element.76) | copy-start | bytes 6291460
  392.7 15.8 %slice-start.5 = ((s8[6291456]{0:T(1024)(128)(4,1)}), s8[2097152]{0:T(1024)(128)(4,1)S(1)}, s32[]{:S(2)}) async-start(s8[6291456]{0:T(1024)(128)(4,1)} %bitcast.218), calls=%async_computation.13 | async-start | bytes 4194304
  418.5 6.1 copy-start.54
  418.5 6.1 copy-start.55
  418.5 51.6 %copy-start.42 = (f32[4096]{0:T(1024)S(1)}, f32[4096]{0:T(1024)}, u32[]{:S(2)}) copy-start(f32[4096]{0:T(1024)} %copy-done.41) | copy-start | bytes 49156
  470.1 6.3 copy-start.47
  470.1 6.3 copy-start.56
  470.1 6.3 copy-start.57
  480.6 148.6 %copy-start.14 = (f32[256,512]{1,0:T(8,128)S(1)}, f32[256,512]{1,0:T(8,128)}, u32[]{:S(2)}) copy-start(f32[256,512]{1,0:T(8,128)} %param.28) | copy-start | bytes 1572868
  480.6 148.6 %copy-start.30 = (f32[256,512]{1,0:T(8,128)S(1)}, f32[256,512]{1,0:T(8,128)}, u32[]{:S(2)}) copy-start(f32[256,512]{1,0:T(8,128)} %param.33) | copy-start | bytes 1572868
  632.3 5.9 copy-start.17
  632.3 5.9 copy-start.18
  632.4 5.9 copy-start.19
  632.4 6.0 copy-start.24
  638.4 5.1 copy-start.21
  638.4 5.1 copy-start.22
  638.4 5.2 copy-start.23
  (35 other events, 103.1 us)
Sparse Core Ops, SparseCore 0:
  9.6 15.6 all-gather.2
  92.2 29.6 all-reduce.7
  123.5 14.1 all-gather.4
  195.9 29.6 all-reduce.9
  357.0 29.5 all-reduce.11
  388.9 13.1 reduce-scatter.1
  414.1 215.1 all-reduce.13
where the time goes:
time: 660 us; the launch traced here: 656 us
  waiting for transfers between devices  219 us (33%)
  matrix products  162 us (25%)
  other arithmetic  111 us (17%)
  local copies, waits for them, and re-layouts  87.4 us (13%)
  blocking collectives  45.5 us (7%)
  between operations  18.3 us (3%)
  loops' own time  10.7 us (2%)
    psum x1, waiting for transfers between devices, body(): summed = lax.psum((grad_qkv, grad_out, grad_up, grad_down, grad_ln), 'dp')  144 us
    dot_general x1, matrix products, body(): jnp.einsum('sd,fd->sf', grad_mlp, down_low, preferred_element_type=jnp.fl...  46.6 us
    psum x1, blocking collectives, body(): summed = lax.psum((grad_qkv, grad_out, grad_up, grad_down, grad_ln), 'dp')  45.5 us
    psum x1, waiting for transfers between devices, body(): lax.psum(jnp.einsum('sf,df->sd', grad_up_proj, up_low, preferred_element_...  29.7 us
    psum x1, waiting for transfers between devices, body(): lax.psum(attn_part.astype(jnp.bfloat16), 'head').astype(jnp.float32)  28.6 us
    reduce_sum x3, other arithmetic, layer_norm(): return centered * lax.rsqrt(row_var + epsilon_norm) * gain_vec + bias_vec  19.7 us
    convert_element_type x4, other arithmetic, body(): new_weights[kind_index].astype(jnp.bfloat16)  18.9 us
    all_gather x1, waiting for transfers between devices, body(): lax.all_gather(tokens, 'head', axis=1, tiled=True)  15.8 us
  transfers between devices with their start and end apart: 7, of which 4 were waited for; matrix products, arithmetic and copies ran while one was open for 14% of the time, Pallas kernels for 0%

commit v1 on v0

v1 whole, which is shorter than its diff:
```python
import functools

import jax
import jax.numpy as jnp
import numpy as np
from jax import lax
from jax.experimental import pallas as pl
from jax.experimental.pallas import tpu as pltpu
from jax.sharding import PartitionSpec as P

D = 512
HALF = 256
HEAD_DIM = 64
FF = 2048
SPAN = 128
SEQ = 2048
STEP = 5
ROWS = 16
PAIRS = 4
TILE = 512
TILES = SEQ // TILE
SPANS_TILE = TILE // SPAN

epsilon_norm = 1e-05
epsilon_adam = 1e-08
beta_one = 0.5
beta_two = 0.5
decay_rate = 0.1
masked_score = -1e30

bf16 = jnp.bfloat16
f32 = jnp.float32

NN = (((1,), (0,)), ((), ()))
NT = (((1,), (1,)), ((), ()))
TN = (((0,), (0,)), ((), ()))


def mm(left, right, dims=NN):
    return lax.dot_general(left, right, dims, preferred_element_type=f32)


def join_columns(head, own, other):
    low = jnp.where(head == 0, own, other)
    high = jnp.where(head == 0, other, own)
    return jnp.concatenate([low, high], axis=1)


def norm_stats(values):
    mean = jnp.mean(values, axis=1, keepdims=True)
    centered = values - mean
    rstd = lax.rsqrt(jnp.mean(centered * centered, axis=1, keepdims=True) + epsilon_norm)
    return centered * rstd, rstd


def head_stack(pair, low_lanes, high_lanes):
    return jnp.concatenate([pair * low_lanes, pair * high_lanes], axis=0)


def lane_masks(dtype):
    lane = lax.broadcasted_iota(jnp.int32, (1, 2 * HEAD_DIM), 1)
    low = (lane < HEAD_DIM).astype(f32)
    return low.astype(dtype), (1.0 - low).astype(dtype)


def pair_columns(pair):
    base = 3 * HALF * (pair // 2) + 2 * HEAD_DIM * (pair % 2)
    return base, base + HALF, base + 2 * HALF


def unstack_transposed(product):
    joined = jnp.concatenate(
        [product[:HEAD_DIM, :SPAN], product[HEAD_DIM:, SPAN:]], axis=0
    )
    return joined.T


def forward_attention(
    table, x_own, x_other, ln, w_own, w_other, causal, qkv, bars, probs, ctx, run_sum, normed
):
    head = lax.axis_index("head")
    step = pl.program_id(0)

    @pl.when(step == 0)
    def _():
        run_sum[...] = jnp.zeros_like(run_sum)

    for row in range(0, TILE, 128):
        rows = pl.ds(row, 128)
        x = join_columns(head, x_own[rows, :].astype(f32), x_other[rows, :].astype(f32))
        xhat, _ = norm_stats(x)
        normed[rows, :] = (xhat * ln[0:1, :] + ln[1:2, :]).astype(bf16)
    for side, w in enumerate((w_own, w_other)):
        for part in range(3):
            value = mm(normed[...], w[part])
            if part == 0:
                value = value * float(HEAD_DIM) ** (-0.5)
            base = side * 3 * HALF + part * HALF
            qkv[:, base : base + HALF] = value.astype(bf16)
    low_lanes, high_lanes = lane_masks(bf16)
    for span in range(SPANS_TILE):
        rows = pl.ds(span * SPAN, SPAN)
        row_id = step * SPANS_TILE + span
        inverse = table[0, row_id]
        shift = table[1, row_id]
        for pair in range(PAIRS):
            at_q, at_k, at_v = pair_columns(pair)
            lanes = pl.ds(pair * 128, 128)
            lanes_v = pl.ds(512 + pair * 128, 128)
            key = qkv[rows, at_k : at_k + 128]
            value = qkv[rows, at_v : at_v + 128]
            key_bar = (run_sum[:, lanes] * inverse).astype(bf16)
            value_bar = (run_sum[:, lanes_v] * inverse).astype(bf16)
            run_sum[:, lanes] += key.astype(f32)
            run_sum[:, lanes_v] += value.astype(f32)
            bars[rows, lanes] = key_bar
            bars[rows, lanes_v] = value_bar
            query = head_stack(qkv[rows, at_q : at_q + 128], low_lanes, high_lanes)
            direct = mm(key, query, NT) + causal[...]
            summary = mm(key_bar, query, NT) + shift
            top = jnp.maximum(
                jnp.max(direct, axis=0, keepdims=True), jnp.max(summary, axis=0, keepdims=True)
            )
            direct = jnp.exp(direct - top)
            summary = jnp.exp(summary - top)
            total = jnp.sum(direct, axis=0, keepdims=True) + jnp.sum(
                summary, axis=0, keepdims=True
            )
            scale = 1.0 / total
            direct = (direct * scale).astype(bf16)
            summary = (summary * scale).astype(bf16)
            slot = span * PAIRS + pair
            probs[slot, :SPAN, :] = direct
            probs[slot, SPAN:, :] = summary
            values = jnp.concatenate([value, value_bar], axis=0)
            both = jnp.concatenate([direct, summary], axis=0)
            ctx[rows, lanes] = unstack_transposed(mm(values, both, TN)).astype(bf16)


def gelu_parts(u):
    size = jnp.abs(u)
    bell = jnp.exp(u * u * -0.5)
    denom = 1.0 + (0.3275911 * 0.7071067811865476) * size
    t = 1.0 / denom
    poly = t * (
        0.5 * 0.254829592
        + t
        * (
            0.5 * -0.284496736
            + t * (0.5 * 1.421413741 + t * (0.5 * -1.453152027 + t * (0.5 * 1.061405429)))
        )
    )
    tail = poly * bell
    share = jnp.where(u >= 0.0, 1.0 - tail, tail)
    return u * share, share + u * bell * 0.3989422804014327


def mlp_both_ways(
    lengths,
    x_own,
    x_other,
    dy_own,
    dy_other,
    ln,
    ctx,
    out_own,
    out_other,
    up_own,
    up_other,
    down_own,
    down_other,
    y_own,
    y_other,
    grad_res,
    grad_ctx,
    g_out,
    g_up,
    g_down,
    g_ln,
    acc_out,
    acc_up,
    acc_down,
    acc_ln,
    res,
    xhat,
    rstd_at,
    normed,
    gm,
    mlp,
    grad_n,
    hid,
    slope,
    act,
    grad_hid,
    gu,
    ga,
):
    head = lax.axis_index("head")
    step = pl.program_id(0)
    used = lengths[head]

    @pl.when(step == 0)
    def _():
        acc_out[...] = jnp.zeros_like(acc_out)
        acc_up[...] = jnp.zeros_like(acc_up)
        acc_down[...] = jnp.zeros_like(acc_down)
        acc_ln[...] = jnp.zeros_like(acc_ln)

    def valid_rows(row, count):
        ids = lax.broadcasted_iota(jnp.int32, (count, 1), 0) + (step * TILE + row)
        return (ids < used).astype(f32)

    res[...] = mm(ctx[:, :HALF], out_own[...]) + mm(ctx[:, HALF:], out_other[...])
    for row in range(0, TILE, 128):
        rows = pl.ds(row, 128)
        valid = valid_rows(row, 128)
        x = join_columns(head, x_own[rows, :].astype(f32), x_other[rows, :].astype(f32))
        h = x + valid * res[rows, :]
        res[rows, :] = h
        hat, rstd = norm_stats(h)
        xhat[rows, :] = hat
        rstd_at[rows, :] = rstd
        normed[rows, :] = (hat * ln[2:3, :] + ln[3:4, :]).astype(bf16)
        dy = join_columns(head, dy_own[rows, :].astype(f32), dy_other[rows, :].astype(f32))
        gm[rows, :] = (valid * dy).astype(bf16)
    chunk = 512
    for index in range(FF // chunk):
        up_w, down_w = ((up_own, down_own), (up_other, down_other))[index // 2]
        cut = (index % 2) * chunk
        up_c = up_w[:, cut : cut + chunk]
        down_c = down_w[cut : cut + chunk, :]
        at = index * chunk
        slot = index % 2
        hid[slot] = mm(normed[...], up_c)
        grad_hid[slot] = mm(gm[...], down_c, NT)
        for row in range(0, TILE, 16):
            rows = pl.ds(row, 16)
            a, da = gelu_parts(hid[slot, rows, :])
            act[slot, rows, :] = a.astype(bf16)
            gu[slot, rows, :] = (grad_hid[slot, rows, :] * da).astype(bf16)
        part_m = mm(act[slot], down_c)
        part_n = mm(gu[slot], up_c, NT)
        if index == 0:
            mlp[...] = part_m
            grad_n[...] = part_n
        else:
            mlp[...] += part_m
            grad_n[...] += part_n
        acc_down[at : at + chunk, :] += mm(act[slot], gm[...], TN)
        acc_up[:, at : at + chunk] += mm(normed[...], gu[slot], TN)
    for row in range(0, TILE, 128):
        rows = pl.ds(row, 128)
        valid = valid_rows(row, 128)
        y = res[rows, :] + valid * mlp[rows, :]
        low, high = y[:, :HALF], y[:, HALF:]
        y_own[rows, :] = jnp.where(head == 0, low, high).astype(bf16)
        y_other[rows, :] = jnp.where(head == 0, high, low).astype(bf16)
        gn = grad_n[rows, :]
        hat = xhat[rows, :]
        acc_ln[0:1, :] += jnp.sum(gn * hat, axis=0, keepdims=True)
        acc_ln[1:2, :] += jnp.sum(gn, axis=0, keepdims=True)
        scaled = gn * ln[2:3, :]
        back = rstd_at[rows, :] * (
            scaled
            - jnp.mean(scaled, axis=1, keepdims=True)
            - hat * jnp.mean(scaled * hat, axis=1, keepdims=True)
        )
        dy = join_columns(head, dy_own[rows, :].astype(f32), dy_other[rows, :].astype(f32))
        gh = dy + back
        grad_res[rows, :] = gh
        ga[rows, :] = (valid * gh).astype(bf16)
    acc_out[...] += mm(ctx[...], ga[...], TN)
    grad_ctx[:, :HALF] = mm(ga[...], out_own[...], NT).astype(bf16)
    grad_ctx[:, HALF:] = mm(ga[...], out_other[...], NT).astype(bf16)

    @pl.when(step == TILES - 1)
    def _():
        g_out[...] = acc_out[...].astype(bf16)
        g_up[0] = acc_up[:, : FF // 2].astype(bf16)
        g_up[1] = acc_up[:, FF // 2 :].astype(bf16)
        g_down[...] = acc_down[...].astype(bf16)
        g_ln[...] = acc_ln[...]


def backward_attention(
    table,
    x_own,
    x_other,
    ln,
    w_own,
    w_other,
    qkv,
    bars,
    probs,
    grad_ctx,
    grad_res,
    gx_own,
    gx_other,
    g_qkv,
    g_ln,
    acc_qkv,
    acc_ln,
    after,
    grad_qkv,
    normed,
    grad_n,
):
    head = lax.axis_index("head")
    step = pl.program_id(0)

    @pl.when(step == 0)
    def _():
        acc_qkv[...] = jnp.zeros_like(acc_qkv)
        acc_ln[...] = jnp.zeros_like(acc_ln)
        after[...] = jnp.zeros_like(after)

    low_lanes, high_lanes = lane_masks(bf16)
    scale_factor = float(HEAD_DIM) ** (-0.5)
    for span in reversed(range(SPANS_TILE)):
        rows = pl.ds(span * SPAN, SPAN)
        row_id = (TILES - 1 - step) * SPANS_TILE + span
        inverse = table[0, row_id]
        for pair in range(PAIRS):
            at_q, at_k, at_v = pair_columns(pair)
            lanes = pl.ds(pair * 128, 128)
            lanes_v = pl.ds(512 + pair * 128, 128)
            keys = jnp.concatenate([qkv[rows, at_k : at_k + 128], bars[rows, lanes]], axis=0)
            values = jnp.concatenate([qkv[rows, at_v : at_v + 128], bars[rows, lanes_v]], axis=0)
            query = head_stack(qkv[rows, at_q : at_q + 128], low_lanes, high_lanes)
            grad = head_stack(grad_ctx[rows, lanes], low_lanes, high_lanes)
            prob = probs[span * PAIRS + pair]
            prob_f = prob.astype(f32)
            weighted = mm(values, grad, NT)
            weighted = weighted * prob_f
            delta = jnp.sum(weighted, axis=0, keepdims=True)
            score = (weighted - prob_f * delta).astype(bf16)
            grad_q = unstack_transposed(mm(keys, score, TN)) * scale_factor
            grad_k = mm(score, query)
            grad_v = mm(prob, grad)
            grad_qkv[rows, at_q : at_q + 128] = grad_q.astype(bf16)
            grad_qkv[rows, at_k : at_k + 128] = (grad_k[:SPAN] + after[:, lanes]).astype(bf16)
            grad_qkv[rows, at_v : at_v + 128] = (grad_v[:SPAN] + after[:, lanes_v]).astype(bf16)
            after[:, lanes] += grad_k[SPAN:] * inverse
            after[:, lanes_v] += grad_v[SPAN:] * inverse
    for row in range(0, TILE, 128):
        rows = pl.ds(row, 128)
        x = join_columns(head, x_own[rows, :].astype(f32), x_other[rows, :].astype(f32))
        hat, _ = norm_stats(x)
        normed[rows, :] = (hat * ln[0:1, :] + ln[1:2, :]).astype(bf16)
    for side, w in enumerate((w_own, w_other)):
        for part in range(3):
            at = side * 3 * HALF + part * HALF
            piece = grad_qkv[:, at : at + HALF]
            acc_qkv[side, part] += mm(normed[...], piece, TN)
            back = mm(piece, w[part], NT)
            if side == 0 and part == 0:
                grad_n[...] = back
            else:
                grad_n[...] += back
    for row in range(0, TILE, 128):
        rows = pl.ds(row, 128)
        x = join_columns(head, x_own[rows, :].astype(f32), x_other[rows, :].astype(f32))
        hat, rstd = norm_stats(x)
        gn = grad_n[rows, :]
        acc_ln[0:1, :] += jnp.sum(gn * hat, axis=0, keepdims=True)
        acc_ln[1:2, :] += jnp.sum(gn, axis=0, keepdims=True)
        scaled = gn * ln[0:1, :]
        back = rstd * (
            scaled
            - jnp.mean(scaled, axis=1, keepdims=True)
            - hat * jnp.mean(scaled * hat, axis=1, keepdims=True)
        )
        gx = grad_res[rows, :] + back
        low, high = gx[:, :HALF], gx[:, HALF:]
        gx_own[rows, :] = jnp.where(head == 0, low, high).astype(bf16)
        gx_other[rows, :] = jnp.where(head == 0, high, low).astype(bf16)

    @pl.when(step == TILES - 1)
    def _():
        g_qkv[...] = acc_qkv[...].astype(bf16)
        g_ln[...] = acc_ln[...]


def rows_spec(width, back=False):
    if back:
        return pl.BlockSpec((TILE, width), lambda i: (TILES - 1 - i, 0))
    return pl.BlockSpec((TILE, width), lambda i: (i, 0))


def probs_spec(back=False):
    shape = (SPANS_TILE * PAIRS, 2 * SPAN, 2 * SPAN)
    if back:
        return pl.BlockSpec(shape, lambda i: (TILES - 1 - i, 0, 0))
    return pl.BlockSpec(shape, lambda i: (i, 0, 0))


def whole_spec(shape):
    rank = len(shape)
    return pl.BlockSpec(shape, lambda i: (0,) * rank, pipeline_mode=pl.Buffered(1))


def shaped(shape, dtype=bf16):
    return jax.ShapeDtypeStruct(shape, dtype)


smem_spec = pl.BlockSpec(memory_space=pltpu.SMEM)
limits = pltpu.CompilerParams(vmem_limit_bytes=60 * 1024 * 1024)


def span_table():
    ids = np.arange(ROWS)
    inverse = 1.0 / np.maximum(ids, 1)
    shift = np.where(ids >= 1, np.log(np.maximum(ids, 1)), masked_score)
    return jnp.asarray(np.stack([inverse, shift]).astype(np.float32))


def causal_bias():
    key = np.arange(SPAN)[:, None]
    query = np.arange(2 * SPAN)[None, :] % SPAN
    return jnp.asarray(np.where(key <= query, 0.0, masked_score).astype(np.float32))


def layer_local(x_own, x_other, dy_own, dy_other, lengths, ln_params, weights):
    qkv_own, qkv_other, out_own, out_other, up_own, up_other, down_own, down_other = weights
    table = span_table()
    qkv, bars, probs, ctx = pl.pallas_call(
        forward_attention,
        grid=(TILES,),
        in_specs=[
            smem_spec,
            rows_spec(HALF),
            rows_spec(HALF),
            whole_spec((4, D)),
            whole_spec((3, D, HALF)),
            whole_spec((3, D, HALF)),
            whole_spec((SPAN, 2 * SPAN)),
        ],
        out_specs=[rows_spec(3 * D), rows_spec(2 * D), probs_spec(), rows_spec(D)],
        out_shape=[
            shaped((SEQ, 3 * D)),
            shaped((SEQ, 2 * D)),
            shaped((ROWS * PAIRS, 2 * SPAN, 2 * SPAN)),
            shaped((SEQ, D)),
        ],
        scratch_shapes=[pltpu.VMEM((SPAN, 2 * D), f32), pltpu.VMEM((TILE, D), bf16)],
        compiler_params=limits,
        name="forward_attention",
    )(table, x_own, x_other, ln_params, qkv_own, qkv_other, causal_bias())
    y_own, y_other, grad_res, grad_ctx, g_out, g_up, g_down, g_ln_two = pl.pallas_call(
        mlp_both_ways,
        grid=(TILES,),
        in_specs=[
            smem_spec,
            rows_spec(HALF),
            rows_spec(HALF),
            rows_spec(HALF),
            rows_spec(HALF),
            whole_spec((4, D)),
            rows_spec(D),
            whole_spec((HALF, D)),
            whole_spec((HALF, D)),
            whole_spec((D, FF // 2)),
            whole_spec((D, FF // 2)),
            whole_spec((FF // 2, D)),
            whole_spec((FF // 2, D)),
        ],
        out_specs=[
            rows_spec(HALF),
            rows_spec(HALF),
            rows_spec(D),
            rows_spec(D),
            whole_spec((D, D)),
            whole_spec((2, D, FF // 2)),
            whole_spec((FF, D)),
            whole_spec((2, D)),
        ],
        out_shape=[
            shaped((SEQ, HALF)),
            shaped((SEQ, HALF)),
            shaped((SEQ, D), f32),
            shaped((SEQ, D)),
            shaped((D, D)),
            shaped((2, D, FF // 2)),
            shaped((FF, D)),
            shaped((2, D), f32),
        ],
        scratch_shapes=[
            pltpu.VMEM((D, D), f32),
            pltpu.VMEM((D, FF), f32),
            pltpu.VMEM((FF, D), f32),
            pltpu.VMEM((2, D), f32),
            pltpu.VMEM((TILE, D), f32),
            pltpu.VMEM((TILE, D), f32),
            pltpu.VMEM((TILE, 1), f32),
            pltpu.VMEM((TILE, D), bf16),
            pltpu.VMEM((TILE, D), bf16),
            pltpu.VMEM((TILE, D), f32),
            pltpu.VMEM((TILE, D), f32),
            pltpu.VMEM((2, TILE, 512), f32),
            pltpu.VMEM((8, 128), f32),
            pltpu.VMEM((2, TILE, 512), bf16),
            pltpu.VMEM((2, TILE, 512), f32),
            pltpu.VMEM((2, TILE, 512), bf16),
            pltpu.VMEM((TILE, D), bf16),
        ],
        compiler_params=limits,
        name="mlp_both_ways",
    )(
        lengths,
        x_own,
        x_other,
        dy_own,
        dy_other,
        ln_params,
        ctx,
        out_own,
        out_other,
        up_own,
        up_other,
        down_own,
        down_other,
    )
    gx_own, gx_other, g_qkv, g_ln_one = pl.pallas_call(
        backward_attention,
        grid=(TILES,),
        in_specs=[
            smem_spec,
            rows_spec(HALF, True),
            rows_spec(HALF, True),
            whole_spec((4, D)),
            whole_spec((3, D, HALF)),
            whole_spec((3, D, HALF)),
            rows_spec(3 * D, True),
            rows_spec(2 * D, True),
            probs_spec(True),
            rows_spec(D, True),
            rows_spec(D, True),
        ],
        out_specs=[
            rows_spec(HALF, True),
            rows_spec(HALF, True),
            whole_spec((2, 3, D, HALF)),
            whole_spec((2, D)),
        ],
        out_shape=[
            shaped((SEQ, HALF)),
            shaped((SEQ, HALF)),
            shaped((2, 3, D, HALF)),
            shaped((2, D), f32),
        ],
        scratch_shapes=[
            pltpu.VMEM((2, 3, D, HALF), f32),
            pltpu.VMEM((2, D), f32),
            pltpu.VMEM((SPAN, 2 * D), f32),
            pltpu.VMEM((TILE, 3 * D), bf16),
            pltpu.VMEM((TILE, D), bf16),
            pltpu.VMEM((TILE, D), f32),
        ],
        compiler_params=limits,
        name="backward_attention",
    )(table, x_own, x_other, ln_params, qkv_own, qkv_other, qkv, bars, probs, grad_ctx, grad_res)
    return (
        (y_own, y_other),
        (gx_own, gx_other),
        g_qkv,
        g_out.reshape(2, HALF, D),
        g_up,
        g_down.reshape(2, FF // 2, D),
        jnp.concatenate([g_ln_one, g_ln_two], axis=0),
    )


def swap_heads(value):
    return lax.ppermute(value, "head", [(0, 1), (1, 0)])


def adam_step(gradient, weight, moment_one, moment_two, step_rate):
    first_new = beta_one * moment_one + (1.0 - beta_one) * gradient
    second_new = beta_two * moment_two + (1.0 - beta_two) * gradient * gradient
    first_hat = first_new / (1.0 - beta_one**STEP)
    second_hat = second_new / (1.0 - beta_two**STEP)
    weight_new = weight - step_rate * (
        first_hat / (jnp.sqrt(second_hat) + epsilon_adam) + decay_rate * weight
    )
    return (weight_new, first_new, second_new)


def gather_inputs(tokens, cotangent, w_qkv, w_out, w_up, w_down):
    head = lax.axis_index("head")

    def both(array):
        halves = array.reshape(2, SEQ, HALF)
        own = lax.dynamic_index_in_dim(halves, head, 0, keepdims=False)
        other = lax.dynamic_index_in_dim(halves, 1 - head, 0, keepdims=False)
        return own, swap_heads(other)

    x_own, x_other = both(tokens)
    qkv_own = w_qkv.transpose(1, 0, 2).astype(bf16)
    out_own = w_out.astype(bf16)
    up_own = w_up.astype(bf16)
    down_own = w_down.astype(bf16)
    qkv_other = swap_heads(qkv_own)
    dy_own, dy_other = both(cotangent)
    weights = (
        qkv_own,
        qkv_other,
        out_own,
        swap_heads(out_own),
        up_own,
        swap_heads(up_own),
        down_own,
        swap_heads(down_own),
    )
    return x_own, x_other, dy_own, dy_other, weights


def place_rows(pieces):
    head = lax.axis_index("head")
    own, away = pieces
    arrived = swap_heads(away)
    return jnp.concatenate(
        [jnp.where(head == 0, own, arrived), jnp.where(head == 0, arrived, own)], axis=0
    )


def body(
    tokens,
    cotangent,
    lengths,
    owners,
    w_qkv,
    w_out,
    w_up,
    w_down,
    ln_params,
    m_qkv,
    m_out,
    m_up,
    m_down,
    m_ln,
    v_qkv,
    v_out,
    v_up,
    v_down,
    v_ln,
):
    x_own, x_other, dy_own, dy_other, weights = gather_inputs(
        tokens, cotangent, w_qkv, w_out, w_up, w_down
    )
    y, gx, g_qkv, g_out, g_up, g_down, g_ln = layer_local(
        x_own, x_other, dy_own, dy_other, lengths, ln_params, weights
    )
    output_rows = place_rows(y)
    grad_input = place_rows(gx)
    halves = []
    for grad in (g_qkv, g_out, g_up, g_down):
        halves.append(grad[0].astype(f32) + swap_heads(grad[1]).astype(f32))
    summed = [lax.psum(half.astype(bf16), "dp").astype(f32) for half in halves]
    summed[0] = summed[0].transpose(1, 0, 2)
    summed.append(lax.psum(g_ln, ("dp", "head")))
    masters = (w_qkv, w_out, w_up, w_down, ln_params)
    firsts = (m_qkv, m_out, m_up, m_down, m_ln)
    seconds = (v_qkv, v_out, v_up, v_down, v_ln)
    rates = (
        float(D) ** (-0.5),
        4.0 * float(D) ** (-0.5),
        float(D) ** (-0.5),
        float(FF) ** (-0.5),
        0.7,
    )
    updated = [
        adam_step(
            summed[kind_index],
            masters[kind_index],
            firsts[kind_index],
            seconds[kind_index],
            rates[kind_index],
        )
        for kind_index in range(5)
    ]
    new_weights = tuple((entry[0] for entry in updated))
    new_firsts = tuple((entry[1] for entry in updated))
    new_seconds = tuple((entry[2] for entry in updated))
    device_index = lax.axis_index("dp")
    owned_grads = tuple(
        (
            jnp.where(owners[kind_index] == device_index, summed[kind_index], 0.0)[None]
            for kind_index in range(5)
        )
    )
    copies = tuple((new_weights[kind_index].astype(jnp.bfloat16) for kind_index in range(4)))
    return (
        (output_rows, grad_input)
        + owned_grads
        + tuple(new_weights)
        + tuple(new_firsts)
        + tuple(new_seconds)
        + copies
    )


PLACED = (
    (P("dp", "head"),) * 2
    + (P("dp"), P())
    + (P(None, None, "head"), P("head", None), P(None, "head"), P("head", None), P()) * 3
)
RESULTS = (
    (P("dp", "head"),) * 2
    + (
        P("dp", None, None, "head"),
        P("dp", "head", None),
        P("dp", None, "head"),
        P("dp", "head", None),
        P("dp", None, None),
    )
    + (P(None, None, "head"), P("head", None), P(None, "head"), P("head", None), P()) * 3
    + (P(None, None, "head"), P("head", None), P(None, "head"), P("head", None))
)


def solution(mesh):
    return jax.shard_map(
        body, mesh=mesh, in_specs=PLACED, out_specs=RESULTS, check_vma=False
    )
```

time: 660 us -> 324 us (0.49)
  matrix products: 162 us -> 0 us
  waiting for transfers between devices: 219 us -> 98 us
  Pallas kernels: 0 us -> 114 us
  other arithmetic: 111 us -> 33.6 us
  local copies, waits for them, and re-layouts: 87.4 us -> 11.1 us
  loops' own time: 10.7 us -> 0 us
    dot_general x26 -> x0, matrix products: 162 us -> none  [the longest x1 46.6 us: body(): jnp.einsum('sd,fd->sf', grad_mlp, down_low, preferred_element_type=jnp.fl...]
    pallas_call x0 -> x3, Pallas kernels: none -> 114 us  [the longest x1 49.5 us: layer_local(): pl.pallas_call(mlp_both_ways, grid=(TILES,), in_specs=[smem_spec, rows_sp...]
    psum x4 -> x1, waiting for transfers between devices: 202 us -> 95.8 us  [body(): summed = [lax.psum(half.astype(bf16), 'dp').astype(f32) for half in halves]]
    reduce_sum x12 -> x0, other arithmetic: 49.8 us -> none  [the longest x3 19.7 us: layer_norm(): return centered * lax.rsqrt(row_var + epsilon_norm) * gain_vec + bias_vec]
    dynamic_update_slice x10 -> x0, local copies, waits for them, and re-layouts: 21.1 us -> none  [the longest x4 13.5 us: body(): lax.map(attend_back, (seq_qkv, log_totals, grad_context.reshape(seq_count...]
    convert_element_type x9 -> x7, other arithmetic: 25 us -> 5.78 us  [the longest x3 3.44 us: body(): summed = [lax.psum(half.astype(bf16), 'dp').astype(f32) for half in halves]]
    while x29 -> x0, local copies, waits for them, and re-layouts: 16.8 us -> none  [the longest x1 8.71 us: body(): contexts, log_totals = lax.map(attend, seq_qkv)]
    all_gather x2 -> x0, waiting for transfers between devices: 15.8 us -> none  [the longest x1 15.8 us: body(): lax.all_gather(tokens, 'head', axis=1, tiled=True)]
  transfers between devices with their start and end apart: 7 -> 13, of which waited for: 4 -> 2; matrix products, arithmetic and copies ran while one was open for 14% -> 5% of each run, Pallas kernels for 0% -> 9%
where the time goes in v1:
time: 324 us; the launch traced here: 323 us
  Pallas kernels  114 us (35%)
  waiting for transfers between devices  98 us (30%)
  blocking collectives  44.7 us (14%)
  other arithmetic  33.6 us (10%)
  between operations  17.6 us (5%)
  local copies, waits for them, and re-layouts  11.1 us (3%)
  starting transfers between devices  4.33 us (1%)
    psum x1, waiting for transfers between devices, body(): summed = [lax.psum(half.astype(bf16), 'dp').astype(f32) for half in halves]  95.8 us
    pallas_call x1, Pallas kernels, layer_local(): pl.pallas_call(mlp_both_ways, grid=(TILES,), in_specs=[smem_spec, rows_sp...  49.5 us
    psum x1, blocking collectives, body(): summed.append(lax.psum(g_ln, ('dp', 'head')))  44.7 us
    pallas_call x1, Pallas kernels, layer_local(): pl.pallas_call(backward_attention, grid=(TILES,), in_specs=[smem_spec, ro...  36.5 us
    pallas_call x1, Pallas kernels, layer_local(): pl.pallas_call(forward_attention, grid=(TILES,), in_specs=[smem_spec, row...  27.9 us
    convert_element_type x4, other arithmetic, body(): new_weights[kind_index].astype(jnp.bfloat16)  20.1 us
  transfers between devices with their start and end apart: 13, of which 2 were waited for; matrix products, arithmetic and copies ran while one was open for 5% of the time, Pallas kernels for 9%

profile of v1, /device:TPU:0, one launch (start us, length us, event | category | flops | bytes accessed | tf_op | source)
XLA Modules:
  0.0 323.4 jit_solution(5221665111669163427)
XLA Ops:
  7.2 0.0 all-reduce.3.cloned.1.call-start
  7.3 2.8 dynamic-slice_bitcast_fusion.2
  10.0 0.5 collective-permute-start
  10.5 0.1 convert_bitcast_fusion.w_own
  10.6 0.1 collective-permute-start.2
  10.7 1.1 copy-done.10
  11.8 1.5 dynamic-slice_bitcast_fusion
  13.2 0.6 collective-permute-start.1
  13.8 0.3 copy-done.2
  14.1 1.1 convert_element_type.81.up_own
  15.3 0.6 collective-permute-start.4
  15.8 1.1 convert_element_type.82.down_own
  17.0 0.0 copy-start.19
  17.0 0.6 collective-permute-start.3
  17.6 0.3 copy-done.7
  17.9 1.0 copy-done
  18.9 27.9 %forward_attention.1 = (bf16[2048,1536]{1,0:T(8,128)(2,1)}, bf16[2048,1024]{1,0:T(8,128)(2,1)}, bf16[64,256,256]{2,1,0:T(8,128)(2,1)}, bf16[2048,512]{1,0:T(8,128)(2,1)}) custom-call(f32[2,16]{1,0:T(2,128)} %constant.74.clone.table, bf16[2048,256]{1,0:T(8,128)(2,1)} %get-tuple-element.88.x_own, bf16[2048,256]{1,0:T(8,128)(2,1)} %copy-done, f32[4,512]{1,0:T(4,128)} %ln.5, ...), custom_call_target="tpu_custom_call" | custom-call | tf_op jit(solution)/shard_map/forward_attention/pallas_call | solution.py:426
  46.9 49.5 %mlp_both_ways.1 = (bf16[2048,256]{1,0:T(8,128)(2,1)}, bf16[2048,256]{1,0:T(8,128)(2,1)}, f32[2048,512]{1,0:T(8,128)}, bf16[2048,512]{1,0:T(8,128)(2,1)}, bf16[5...) custom-call(s32[2]{0:T(128)} %lengths.1, ...), custom_call_target="tpu_custom_call" | custom-call | tf_op jit(solution)/shard_map/mlp_both_ways/pallas_call | solution.py:449
  96.4 36.5 %backward_attention.1 = (bf16[2048,256]{1,0:T(8,128)(2,1)}, bf16[2048,256]{1,0:T(8,128)(2,1)}, bf16[2,3,512,256]{3,2,1,0:T(8,128)(2,1)}, f32[2,512]{1,0:T(2,128)}) custom-call(f32[2,16]{1,0:T(2,128)} %constant.74.clone.table, bf16[2048,256]{1,0:T(8,128)(2,1)} %get-tuple-element.88.x_own, bf16[2048,256]{1,0:T(8,128)(2,1)} %copy-done, f32[4,512]{1,0:T(4,128)} %ln.5, ...), custom_call_target="tpu_custom_call" | custom-call | tf_op jit(solution)/shard_map/backward_attention/pallas_call | solution.py:523
  132.9 1.3 slice_bitcast_fusion.1
  134.3 0.6 collective-permute-start.8
  134.9 1.3 slice.54
  136.2 0.1 collective-permute-start.11
  136.3 0.5 collective-permute-start.9
  136.8 0.1 slice_bitcast_fusion
  136.9 0.1 collective-permute-start.10
  137.0 0.5 collective-permute-start.7
  137.5 2.1 collective-permute-done.9
  139.6 0.8 add_convert_fusion.1
  140.4 1.1 fusion.11
  141.5 1.3 add_convert_fusion
  142.8 1.4 fusion.7
  144.2 0.0 all-reduce.3.cloned.1.call-update
  144.3 0.6 copy-done.26
  144.9 0.6 fusion.29
  148.7 0.2 collective-permute-start.6
  148.9 44.7 %psum.39 = f32[4,512]{1,0:T(4,128)S(1)} all-reduce(f32[4,512]{1,0:T(4,128)S(1)} %pad_maximum_fusion.2), channel_id=1, replica_groups=mesh['dp'=16,'head'=2] {'dp','head'}, use_global_device_ids=true, to_apply=%region_4.5 | all-reduce | flops 2048 | bytes 16384 | tf_op jit(solution)/shard_map/psum | solution.py:660
  193.6 0.6 multiply_subtract_fusion.4
  194.2 1.7 broadcast_select_fusion.1
  195.9 1.5 pad_maximum_fusion.1
  197.4 0.2 copy-done.17
  197.6 1.4 broadcast_select_fusion.3
  198.9 1.5 pad_maximum_fusion
  200.4 95.8 %all-reduce.3.cloned.1.call-done = (bf16[512,3,256]{2,0,1:T(8,128)(2,1)}, bf16[256,512]{1,0:T(8,128)(2,1)}, bf16[512,1024]{1,0:T(8,128)(2,1)}, bf16[1024,512]{1,0:T(8,128)(2,1)}) async-done(((bf16[512,3,256]{2,0,1:T(8,128)(2,1)}, bf16[256,512]{1,0:T(8,128)(2,1)}, bf16[512,1024]{1,0:T(8,128)(2,1)}, bf16[1024,512]{1,0:T(8,128)(2,1)}), (bf16[512,3,256]{2,0,1:T(8,128)(2,1)}, bf16[256,512]{1,0:T(8,128)(2,1)}, ...) | async-done | bytes 3145744 | tf_op jit(solution)/shard_map/psum | solution.py:658
  296.2 8.2 %fusion.16 = (bf16[1024,512]{1,0:T(8,128)(2,1)}, f32[1024,512]{1,0:T(8,128)}, f32[1024,512]{1,0:T(8,128)}, f32[1024,512]{1,0:T(8,128)}, f32[1,1024,512]{2,1,0:T(8,128)}) fusion(f32[1024,512]{1,0:T(8,128)S(1)} %copy-done.1, bf16[1024,512]{1,0:T(8,128)(2,1)} %get-tuple-element.61, f32[1024,512]{1,0:T(8,128)} %param.33, f32[1024,512]{1,0:T(8,128)} %param.38, ...), kind=kLoop, calls=%fused_computation.54 | loop fusion | flops 8912896 | bytes 16777216 | tf_op jit(solution)/shard_map/convert_element_type | solution.py:691
  304.6 5.7 %fusion.19 = (bf16[512,1024]{1,0:T(8,128)(2,1)}, f32[512,1024]{1,0:T(8,128)}, f32[512,1024]{1,0:T(8,128)}, f32[512,1024]{1,0:T(8,128)}, f32[1,512,1024]{2,1,0:T(8,128)}) fusion(f32[512,1024]{1,0:T(8,128)S(1)} %copy-done.3, bf16[512,1024]{1,0:T(8,128)(2,1)S(1)} %copy-done.18, f32[512,1024]{1,0:T(8,128)S(1)} %copy-done.8, f32[512,1024]{1,0:T(8,128)S(1)} %copy-done.9, ...), kind=kLoop, calls=%fused_computation.55 | loop fusion | flops 8912896 | bytes 16777216 | tf_op jit(solution)/shard_map/convert_element_type | solution.py:691
  310.3 4.3 %fusion.25 = (bf16[512,3,256]{2,0,1:T(8,128)(2,1)}, f32[512,3,256]{2,0,1:T(8,128)}, f32[512,3,256]{2,0,1:T(8,128)}, f32[512,3,256]{2,0,1:T(8,128)}, f32[1,512,3,256]{3,1,2,0:T(8,128)}) fusion(f32[512,3,256]{2,0,1:T(8,128)S(1)} %copy-done.6, bf16[512,3,256]{2,0,1:T(8,128)(2,1)S(1)} %copy-done.20, f32[512,3,256]{2,0,1:T(8,128)S(1)} %copy-done.14, ...), kind=kLoop, calls=%fused_computation.57 | loop fusion | flops 6684672 | bytes 12582913 | tf_op jit(solution)/shard_map/convert_element_type | solution.py:691
  314.6 1.9 fusion.22
  (70 shorter events, 0.2 us)
Async XLA Ops:
  7.2 289.0 %all-reduce.3.cloned.1.call-start = ((), (), s32[]{:S(2)}) async-start(), calls=%async_computation | async-start | bytes 6291456 | tf_op jit(solution)/shard_map/psum | solution.py:658
  7.3 3.2 %copy-start.5 = (f32[512,3,256]{2,0,1:T(8,128)S(1)}, f32[512,3,256]{2,0,1:T(8,128)}, u32[]{:S(2)}) copy-start(f32[512,3,256]{2,0,1:T(8,128)} %param.25) | copy-start | bytes 4718596
  10.0 1.8 copy-start.10
  10.0 7.6 %collective-permute-start = (bf16[2048,256]{1,0:T(8,128)(2,1)S(1)}, bf16[2048,256]{1,0:T(8,128)(2,1)S(1)}, u32[]{:S(2)}, u32[]{:S(2)}) collective-permute-start(bf16[2048,256]{1,0:T(8,128)(2,1)S(1)} %get-tuple-element.87), channel_id=1, source_target_pairs={{0,1},{1,0},{2,3},{3,2},{4,5},{5,4},{6,7},{7,6},{8,9},{9,8},{10,11... | collective-permute-start | bytes 3145736 | tf_op jit(solution)/shard_map/ppermute | solution.py:574
  10.6 2.7 copy-start.4
  10.6 6.4 %collective-permute-start.2 = (bf16[3,512,256]{2,1,0:T(8,128)(2,1)S(1)}, bf16[3,512,256]{2,1,0:T(8,128)(2,1)S(1)}, u32[]{:S(2)}, u32[]{:S(2)}) collective-permute-start(bf16[3,512,256]{2,1,0:T(8,128)(2,1)S(1)} %convert_bitcast_fusion.w_own), channel_id=1, source_target_pairs={{0,1},{1,0},{2,3},{3,2},{4,5},{5,4},{6,7},{7,6},{8,9},{9,8},{10,11... | collective-permute-start | bytes 2359304 | tf_op jit(solution)/shard_map/ppermute | solution.py:574
  11.8 2.3 copy-start.2
  13.2 2.6 copy-start.1
  13.2 33.6 %collective-permute-start.1 = (bf16[2048,256]{1,0:T(8,128)(2,1)}, bf16[2048,256]{1,0:T(8,128)(2,1)}, u32[]{:S(2)}, u32[]{:S(2)}) collective-permute-start(bf16[2048,256]{1,0:T(8,128)(2,1)} %get-tuple-element.85), channel_id=1, source_target_pairs={{0,1},{1,0},{2,3},{3,2},{4,5},{5,4},{6,7},{7,6},{8,9},{9,8},{10,11... | collective-permute-start | bytes 3145736 | tf_op jit(solution)/shard_map/ppermute | solution.py:574
  15.3 1.7 copy-start.13
  15.3 31.6 %collective-permute-start.4 = (bf16[512,1024]{1,0:T(8,128)(2,1)}, bf16[512,1024]{1,0:T(8,128)(2,1)}, u32[]{:S(2)}, u32[]{:S(2)}) collective-permute-start(bf16[512,1024]{1,0:T(8,128)(2,1)} %convert_element_type.81.up_own), channel_id=1, source_target_pairs={{0,1},{1,0},{2,3},{3,2},{4,5},{5,4},{6,7},{7,6},{8,9},{9,8},{10,11... | collective-permute-start | bytes 3145736 | tf_op jit(solution)/shard_map/ppermute | solution.py:574
  16.9 29.9 %collective-permute-start.5 = (bf16[1024,512]{1,0:T(8,128)(2,1)}, bf16[1024,512]{1,0:T(8,128)(2,1)}, u32[]{:S(2)}, u32[]{:S(2)}) collective-permute-start(bf16[1024,512]{1,0:T(8,128)(2,1)} %convert_element_type.82.down_own), channel_id=1, source_target_pairs={{0,1},{1,0},{2,3},{3,2},{4,5},{5,4},{6,7},{7,6},{8,9},{9,8},{10,11... | collective-permute-start | bytes 3145736 | tf_op jit(solution)/shard_map/ppermute | solution.py:574
  17.0 29.9 %copy-start.19 = (bf16[256,512]{1,0:T(8,128)(2,1)}, bf16[256,512]{1,0:T(8,128)(2,1)S(1)}, u32[]{:S(2)}) copy-start(bf16[256,512]{1,0:T(8,128)(2,1)S(1)} %convert_element_type.80.out_own) | copy-start | bytes 786436
  17.0 0.9 copy-start.7
  17.0 29.8 %collective-permute-start.3 = (bf16[256,512]{1,0:T(8,128)(2,1)S(1)}, bf16[256,512]{1,0:T(8,128)(2,1)}, u32[]{:S(2)}, u32[]{:S(2)}) collective-permute-start(bf16[256,512]{1,0:T(8,128)(2,1)S(1)} %convert_element_type.80.out_own), channel_id=1, source_target_pairs={{0,1},{1,0},{2,3},{3,2},{4,5},{5,4},{6,7},{7,6},{8,9},{9,8},{10,11... | collective-permute-start | bytes 786440 | tf_op jit(solution)/shard_map/ppermute | solution.py:574
  17.9 1.0 copy-start
  132.9 3.4 %copy-start.23 = (bf16[512,512]{1,0:T(8,128)(2,1)S(1)}, bf16[512,512]{1,0:T(8,128)(2,1)}, u32[]{:S(2)}) copy-start(bf16[512,512]{1,0:T(8,128)(2,1)} %get-tuple-element.53) | copy-start | bytes 1572868
  132.9 3.9 %copy-start.11 = (bf16[2,512,1024]{2,1,0:T(8,128)(2,1)S(1)}, bf16[2,512,1024]{2,1,0:T(8,128)(2,1)}, u32[]{:S(2)}) copy-start(bf16[2,512,1024]{2,1,0:T(8,128)(2,1)} %get-tuple-element.54) | copy-start | bytes 6291460
  134.3 6.1 %collective-permute-start.8 = (bf16[3,512,256]{2,1,0:T(8,128)(2,1)S(1)}, bf16[3,512,256]{2,1,0:T(8,128)(2,1)S(1)}, u32[]{:S(2)}, u32[]{:S(2)}) collective-permute-start(bf16[3,512,256]{2,1,0:T(8,128)(2,1)S(1)} %slice_bitcast_fusion.1), channel_id=1, source_target_pairs={{0,1},{1,0},{2,3},{3,2},{4,5},{5,4},{6,7},{7,6},{8,9},{9,8},{10,11... | collective-permute-start | bytes 2359304 | tf_op jit(solution)/shard_map/ppermute | solution.py:574
  136.2 4.3 %copy-start.16 = (bf16[2,3,512,256]{3,2,1,0:T(8,128)(2,1)S(1)}, bf16[2,3,512,256]{3,2,1,0:T(8,128)(2,1)}, u32[]{:S(2)}) copy-start(bf16[2,3,512,256]{3,2,1,0:T(8,128)(2,1)} %get-tuple-element.52) | copy-start | bytes 4718596
  136.2 5.3 %collective-permute-start.11 = (bf16[1024,512]{1,0:T(8,128)(2,1)S(1)}, bf16[1024,512]{1,0:T(8,128)(2,1)S(1)}, u32[]{:S(2)}, u32[]{:S(2)}) collective-permute-start(bf16[1024,512]{1,0:T(8,128)(2,1)S(1)} %slice.54), channel_id=1, source_target_pairs={{0,1},{1,0},{2,3},{3,2},{4,5},{5,4},{6,7},{7,6},{8,9},{9,8},{10,11... | collective-permute-start | bytes 3145736 | tf_op jit(solution)/shard_map/ppermute | solution.py:574
  136.3 3.4 %collective-permute-start.9 = (bf16[256,512]{1,0:T(8,128)(2,1)S(1)}, bf16[256,512]{1,0:T(8,128)(2,1)S(1)}, u32[]{:S(2)}, u32[]{:S(2)}) collective-permute-start(bf16[256,512]{1,0:T(8,128)(2,1)S(1)} %slice.48), channel_id=1, source_target_pairs={{0,1},{1,0},{2,3},{3,2},{4,5},{5,4},{6,7},{7,6},{8,9},{9,8},{10,11... | collective-permute-start | bytes 786440 | tf_op jit(solution)/shard_map/ppermute | solution.py:574
  136.9 4.6 %copy-start.12 = (bf16[2048,512]{1,0:T(8,128)(2,1)S(1)}, bf16[2048,512]{1,0:T(8,128)(2,1)}, u32[]{:S(2)}) copy-start(bf16[2048,512]{1,0:T(8,128)(2,1)} %get-tuple-element.55) | copy-start | bytes 6291460
  136.9 5.9 %collective-permute-start.10 = (bf16[512,1024]{1,0:T(8,128)(2,1)S(1)}, bf16[512,1024]{1,0:T(8,128)(2,1)S(1)}, u32[]{:S(2)}, u32[]{:S(2)}) collective-permute-start(bf16[512,1024]{1,0:T(8,128)(2,1)S(1)} %slice_bitcast_fusion), channel_id=1, source_target_pairs={{0,1},{1,0},{2,3},{3,2},{4,5},{5,4},{6,7},{7,6},{8,9},{9,8},{10,11... | collective-permute-start | bytes 3145736 | tf_op jit(solution)/shard_map/ppermute | solution.py:574
  137.0 57.2 %collective-permute-start.7 = (bf16[2048,256]{1,0:T(8,128)(2,1)}, bf16[2048,256]{1,0:T(8,128)(2,1)}, u32[]{:S(2)}, u32[]{:S(2)}) collective-permute-start(bf16[2048,256]{1,0:T(8,128)(2,1)} %get-tuple-element.51), channel_id=1, source_target_pairs={{0,1},{1,0},{2,3},{3,2},{4,5},{5,4},{6,7},{7,6},{8,9},{9,8},{10,11... | collective-permute-start | bytes 3145736 | tf_op jit(solution)/shard_map/ppermute | solution.py:574
  144.2 0.7 copy-start.26
  144.2 4.7 %copy-start.29 = (f32[2,512]{1,0:T(2,128)S(1)}, f32[2,512]{1,0:T(2,128)}, u32[]{:S(2)}) copy-start(f32[2,512]{1,0:T(2,128)} %get-tuple-element.57) | copy-start | bytes 12292
  144.2 4.7 %copy-start.30 = (f32[2,512]{1,0:T(2,128)S(1)}, f32[2,512]{1,0:T(2,128)}, u32[]{:S(2)}) copy-start(f32[2,512]{1,0:T(2,128)} %get-tuple-element.56) | copy-start | bytes 12292
  144.2 49.4 %copy-start.25 = (f32[4,512]{1,0:T(4,128)S(1)}, f32[4,512]{1,0:T(4,128)}, u32[]{:S(2)}) copy-start(f32[4,512]{1,0:T(4,128)} %ln.5) | copy-start | bytes 24580
  144.2 49.4 %copy-start.27 = (f32[4,512]{1,0:T(4,128)S(1)}, f32[4,512]{1,0:T(4,128)}, u32[]{:S(2)}) copy-start(f32[4,512]{1,0:T(4,128)} %param.34) | copy-start | bytes 24580
  144.2 49.4 %copy-start.28 = (f32[4,512]{1,0:T(4,128)S(1)}, f32[4,512]{1,0:T(4,128)}, u32[]{:S(2)}) copy-start(f32[4,512]{1,0:T(4,128)} %param.39) | copy-start | bytes 24580
  148.7 48.7 %collective-permute-start.6 = (bf16[2048,256]{1,0:T(8,128)(2,1)}, bf16[2048,256]{1,0:T(8,128)(2,1)}, u32[]{:S(2)}, u32[]{:S(2)}) collective-permute-start(bf16[2048,256]{1,0:T(8,128)(2,1)} %get-tuple-element.44), channel_id=1, source_target_pairs={{0,1},{1,0},{2,3},{3,2},{4,5},{5,4},{6,7},{7,6},{8,9},{9,8},{10,11... | collective-permute-start | bytes 3145736 | tf_op jit(solution)/shard_map/ppermute | solution.py:574
  195.9 1.7 copy-start.17
  296.2 8.3 %copy-start.3 = (f32[512,1024]{1,0:T(8,128)S(1)}, f32[512,1024]{1,0:T(8,128)}, u32[]{:S(2)}) copy-start(f32[512,1024]{1,0:T(8,128)} %param.27) | copy-start | bytes 6291460
  296.2 8.3 %copy-start.8 = (f32[512,1024]{1,0:T(8,128)S(1)}, f32[512,1024]{1,0:T(8,128)}, u32[]{:S(2)}) copy-start(f32[512,1024]{1,0:T(8,128)} %param.32) | copy-start | bytes 6291460
  296.2 8.3 %copy-start.9 = (f32[512,1024]{1,0:T(8,128)S(1)}, f32[512,1024]{1,0:T(8,128)}, u32[]{:S(2)}) copy-start(f32[512,1024]{1,0:T(8,128)} %param.37) | copy-start | bytes 6291460
  296.2 8.3 %copy-start.18 = (bf16[512,1024]{1,0:T(8,128)(2,1)S(1)}, bf16[512,1024]{1,0:T(8,128)(2,1)}, u32[]{:S(2)}) copy-start(bf16[512,1024]{1,0:T(8,128)(2,1)} %get-tuple-element.60) | copy-start | bytes 3145732
  304.5 5.7 %copy-start.6 = (f32[512,3,256]{2,0,1:T(8,128)S(1)}, f32[512,3,256]{2,0,1:T(8,128)}, u32[]{:S(2)}) copy-start(f32[512,3,256]{2,0,1:T(8,128)} %param.25) | copy-start | bytes 4718596
  304.5 5.7 %copy-start.14 = (f32[512,3,256]{2,0,1:T(8,128)S(1)}, f32[512,3,256]{2,0,1:T(8,128)}, u32[]{:S(2)}) copy-start(f32[512,3,256]{2,0,1:T(8,128)} %param.30) | copy-start | bytes 4718596
  304.5 5.7 %copy-start.15 = (f32[512,3,256]{2,0,1:T(8,128)S(1)}, f32[512,3,256]{2,0,1:T(8,128)}, u32[]{:S(2)}) copy-start(f32[512,3,256]{2,0,1:T(8,128)} %param.35) | copy-start | bytes 4718596
  304.5 5.7 %copy-start.20 = (bf16[512,3,256]{2,0,1:T(8,128)(2,1)S(1)}, bf16[512,3,256]{2,0,1:T(8,128)(2,1)}, u32[]{:S(2)}) copy-start(bf16[512,3,256]{2,0,1:T(8,128)(2,1)} %get-tuple-element.58) | copy-start | bytes 2359300
  310.3 4.4 %copy-start.21 = (f32[256,512]{1,0:T(8,128)S(1)}, f32[256,512]{1,0:T(8,128)}, u32[]{:S(2)}) copy-start(f32[256,512]{1,0:T(8,128)} %param.31) | copy-start | bytes 1572868
  310.3 4.4 %copy-start.22 = (f32[256,512]{1,0:T(8,128)S(1)}, f32[256,512]{1,0:T(8,128)}, u32[]{:S(2)}) copy-start(f32[256,512]{1,0:T(8,128)} %param.36) | copy-start | bytes 1572868
  310.3 4.4 %copy-start.24 = (bf16[256,512]{1,0:T(8,128)(2,1)S(1)}, bf16[256,512]{1,0:T(8,128)(2,1)}, u32[]{:S(2)}) copy-start(bf16[256,512]{1,0:T(8,128)(2,1)} %get-tuple-element.59) | copy-start | bytes 786436
Sparse Core Ops, SparseCore 0:
  144.4 151.8 all-reduce.2

commit v2 on v1

--- a/solution.py
+++ b/solution.py
@@ -275,10 +275,15 @@
 
     @pl.when(step == TILES - 1)
     def _():
-        g_out[...] = acc_out[...].astype(bf16)
-        g_up[0] = acc_up[:, : FF // 2].astype(bf16)
-        g_up[1] = acc_up[:, FF // 2 :].astype(bf16)
-        g_down[...] = acc_down[...].astype(bf16)
+        for side in range(2):
+            for part in range(2):
+                lanes = slice(part * HALF, (part + 1) * HALF)
+                g_out[side, part] = acc_out[side * HALF : (side + 1) * HALF, lanes].astype(bf16)
+                g_down[side, part] = acc_down[side * 1024 : (side + 1) * 1024, lanes].astype(bf16)
+                for block in range(2):
+                    at = side * 1024 + block * D + part * HALF
+                    rows = slice(block * D, (block + 1) * D)
+                    g_up[side, part, rows] = acc_up[:, at : at + HALF].astype(bf16)
         g_ln[...] = acc_ln[...]
 
 
@@ -377,7 +382,12 @@
 
     @pl.when(step == TILES - 1)
     def _():
-        g_qkv[...] = acc_qkv[...].astype(bf16)
+        for side in range(2):
+            for part in range(2):
+                for kind in range(3):
+                    rows = slice(kind * HALF, (kind + 1) * HALF)
+                    half = slice(part * HALF, (part + 1) * HALF)
+                    g_qkv[side, part, rows] = acc_qkv[side, kind, half].astype(bf16)
         g_ln[...] = acc_ln[...]
 
 
@@ -469,9 +479,9 @@
             rows_spec(HALF),
             rows_spec(D),
             rows_spec(D),
-            whole_spec((D, D)),
-            whole_spec((2, D, FF // 2)),
-            whole_spec((FF, D)),
+            whole_spec((2, 2, HALF, HALF)),
+            whole_spec((2, 2, 1024, HALF)),
+            whole_spec((2, 2, 1024, HALF)),
             whole_spec((2, D)),
         ],
         out_shape=[
@@ -479,9 +489,9 @@
             shaped((SEQ, HALF)),
             shaped((SEQ, D), f32),
             shaped((SEQ, D)),
-            shaped((D, D)),
-            shaped((2, D, FF // 2)),
-            shaped((FF, D)),
+            shaped((2, 2, HALF, HALF)),
+            shaped((2, 2, 1024, HALF)),
+            shaped((2, 2, 1024, HALF)),
             shaped((2, D), f32),
         ],
         scratch_shapes=[
@@ -539,13 +549,13 @@
         out_specs=[
             rows_spec(HALF, True),
             rows_spec(HALF, True),
-            whole_spec((2, 3, D, HALF)),
+            whole_spec((2, 2, 3 * HALF, HALF)),
             whole_spec((2, D)),
         ],
         out_shape=[
             shaped((SEQ, HALF)),
             shaped((SEQ, HALF)),
-            shaped((2, 3, D, HALF)),
+            shaped((2, 2, 3 * HALF, HALF)),
             shaped((2, D), f32),
         ],
         scratch_shapes=[
@@ -563,26 +573,445 @@
         (y_own, y_other),
         (gx_own, gx_other),
         g_qkv,
-        g_out.reshape(2, HALF, D),
+        g_out,
         g_up,
-        g_down.reshape(2, FF // 2, D),
+        g_down,
         jnp.concatenate([g_ln_one, g_ln_two], axis=0),
     )
 
 
 def swap_heads(value):
     return lax.ppermute(value, "head", [(0, 1), (1, 0)])
+
+
+def chip_grid(count):
+    side = 1 << ((count.bit_length() - 1) // 3)
+    return (count // (side * side), side, side)
+
+
+class Lines:
+    def __init__(self, count):
+        self.sizes = chip_grid(count)
+        self.strides = (self.sizes[1] * self.sizes[2], self.sizes[2], 1)
+        self.chip = lax.axis_index("dp")
+        self.head = lax.axis_index("head")
+        self.places = [
+            lax.rem(self.chip // stride, size) for stride, size in zip(self.strides, self.sizes)
+        ]
+
+    def partner(self):
+        return (self.chip, 1 - self.head)
+
+    def member(self, axis, ahead):
+        size = self.sizes[axis]
+        place = lax.rem(self.places[axis] + ahead, size)
+        chip = self.chip + (place - self.places[axis]) * self.strides[axis]
+        return place, (chip, self.head)
+
+    def greet(self):
+        barrier = pltpu.get_barrier_semaphore()
+        others = [self.partner()]
+        for axis in range(3):
+            others += [self.member(axis, ahead)[1] for ahead in range(1, self.sizes[axis])]
+        for other in others:
+            pl.semaphore_signal(
+                barrier, inc=1, device_id=other, device_id_type=pl.DeviceIdType.MESH
+            )
+        pl.semaphore_wait(barrier, len(others))
+
+
+ORDERS = ((2, 1, 0), (1, 2, 0))
+
+
+def padded_rows(rows, count):
+    unit = 16 * count
+    return -(-rows // unit) * unit
+
+
+def chunk_rows(rows):
+    return next(chunk for chunk in (64, 48, 32, 16) if rows % chunk == 0)
+
+
+def sum_scratch(rows, count):
+    sizes = chip_grid(count)
+    shapes = [
+        pltpu.VMEM((2, rows, HALF), bf16),
+        pltpu.VMEM((2, rows, HALF), bf16),
+        pltpu.VMEM((2, rows, HALF), bf16),
+    ]
+    sems = [pltpu.SemaphoreType.DMA((2,))]
+    for order in ORDERS:
+        left = rows
+        for axis in order:
+            left //= sizes[axis]
+            shapes.append(pltpu.VMEM((sizes[axis] - 1, left, HALF), bf16))
+            sems.append(pltpu.SemaphoreType.DMA((2, 2, sizes[axis] - 1)))
+    return shapes + sems
+
+
+class DpSum:
+    def __init__(self, lines, grads, total, scratch):
+        self.lines = lines
+        self.grads = grads
+        self.total = total
+        self.rows = total.shape[1]
+        self.used = grads.shape[2]
+        self.work, self.arrived, self.final = scratch[:3]
+        self.slots = (scratch[3:6], scratch[6:9])
+        self.core_sem = scratch[9]
+        self.sems = (scratch[10:13], scratch[13:16])
+        self.base = [[0], [0]]
+        self.length = [self.rows, self.rows]
+
+    def remote(self, source, target, send_sem, recv_sem, device):
+        return pltpu.make_async_remote_copy(
+            src_ref=source,
+            dst_ref=target,
+            send_sem=send_sem,
+            recv_sem=recv_sem,
+            device_id=device,
+            device_id_type=pl.DeviceIdType.MESH,
+        )
+
+    def core_copy(self):
+        return self.remote(
+            self.grads.at[1],
+            self.arrived.at[:, pl.ds(0, self.used)],
+            self.core_sem.at[0],
+            self.core_sem.at[1],
+            self.lines.partner(),
+        )
+
+    def core_send(self):
+        self.core_copy().start()
+
+    def core_sum(self):
+        self.core_copy().wait()
+        chunk = chunk_rows(self.used)
+        for part in range(2):
+
+            def add(index, carry, part=part):
+                rows = pl.ds(pl.multiple_of(index * chunk, chunk), chunk)
+                own = self.grads[0, part, rows, :].astype(f32)
+                away = self.arrived[part, rows, :].astype(f32)
+                self.work[part, rows, :] = (own + away).astype(bf16)
+                return carry
+
+            lax.fori_loop(0, self.used // chunk, add, 0)
+
+    def spread_copies(self, part, stage):
+        axis = ORDERS[part][stage]
+        size = self.lines.sizes[axis]
+        base = self.base[part][stage]
+        piece = self.rows
+        for at in ORDERS[part][: stage + 1]:
+            piece //= self.lines.sizes[at]
+        copies = []
+        for ahead in range(1, size):
+            place, device = self.lines.member(axis, ahead)
+            start = pl.multiple_of(base + place * piece, 16)
+            copies.append(
+                self.remote(
+                    self.work.at[part, pl.ds(start, piece)],
+                    self.slots[part][stage].at[ahead - 1],
+                    self.sems[part][stage].at[0, 0, ahead - 1],
+                    self.sems[part][stage].at[0, 1, ahead - 1],
+                    device,
+                )
+            )
+        mine = base + self.lines.places[axis] * piece
+        return copies, mine, piece
+
+    def spread_send(self, part, stage):
+        copies, mine, _ = self.spread_copies(part, stage)
+        for copy in copies:
+            copy.start()
+        self.base[part] = self.base[part][: stage + 1] + [mine]
+
+    def spread_sum(self, part, stage):
+        copies, mine, piece = self.spread_copies(part, stage)
+        for copy in copies:
+            copy.wait()
+        slots = self.slots[part][stage]
+        target = self.final if stage == 2 else self.work
+        chunk = chunk_rows(piece)
+
+        def add(index, carry):
+            offset = pl.multiple_of(index * chunk, chunk)
+            rows = pl.ds(pl.multiple_of(mine + offset, 16), chunk)
+            value = self.work[part, rows, :].astype(f32)
+            for slot in range(len(copies)):
+                value = value + slots[slot, pl.ds(offset, chunk), :].astype(f32)
+            target[part, rows, :] = value.astype(bf16)
+            return carry
+
+        lax.fori_loop(0, piece // chunk, add, 0)
+
+    def gather_copies(self, part, stage):
+        axis = ORDERS[part][stage]
+        size = self.lines.sizes[axis]
+        piece = self.rows
+        for at in ORDERS[part][: stage + 1]:
+            piece //= self.lines.sizes[at]
+        mine = pl.multiple_of(self.base[part][stage + 1], 16)
+        rows = pl.ds(mine, piece)
+        copies = []
+        for ahead in range(1, size):
+            _, device = self.lines.member(axis, ahead)
+            copies.append(
+                self.remote(
+                    self.final.at[part, rows],
+                    self.final.at[part, rows],
+                    self.sems[part][stage].at[1, 0, ahead - 1],
+                    self.sems[part][stage].at[1, 1, ahead - 1],
+                    device,
+                )
+            )
+        return copies
+
+    def gather_send(self, part, stage):
+        for copy in self.gather_copies(part, stage):
+            copy.start()
+
+    def gather_wait(self, part, stage):
+        for copy in self.gather_copies(part, stage):
+            copy.wait()
+
+    def store(self):
+        self.total[...] = self.final[...]
+
+
+def both_parts(sums, action, stage):
+    for entry in sums:
+        for part in range(2):
+            getattr(entry, action)(part, stage)
+
+
+def ln_scratch(count):
+    return [
+        pltpu.VMEM((2, 4, D), f32),
+        pltpu.SemaphoreType.DMA((2,)),
+        *[pltpu.VMEM((size, 4, D), f32) for size in chip_grid(count)],
+        *[pltpu.SemaphoreType.DMA((2, max(size - 1, 1))) for size in chip_grid(count)],
+    ]
+
+
+class LnSum:
+    def __init__(self, lines, value, total, scratch):
+        self.lines = lines
+        self.value = value
+        self.total = total
+        self.core, self.core_sem = scratch[:2]
+        self.slots = scratch[2:5]
+        self.sems = scratch[5:8]
+
+    def stage_copies(self, stage):
+        lines = self.lines
+        if stage == 0:
+            mine = self.core.at[lines.head]
+            return [
+                pltpu.make_async_remote_copy(
+                    src_ref=mine,
+                    dst_ref=mine,
+                    send_sem=self.core_sem.at[0],
+                    recv_sem=self.core_sem.at[1],
+                    device_id=lines.partner(),
+                    device_id_type=pl.DeviceIdType.MESH,
+                )
+            ]
+        axis = stage - 1
+        mine = self.slots[axis].at[lines.places[axis]]
+        return [
+            pltpu.make_async_remote_copy(
+                src_ref=mine,
+                dst_ref=mine,
+                send_sem=self.sems[axis].at[0, ahead - 1],
+                recv_sem=self.sems[axis].at[1, ahead - 1],
+                device_id=lines.member(axis, ahead)[1],
+                device_id_type=pl.DeviceIdType.MESH,
+            )
+            for ahead in range(1, lines.sizes[axis])
+        ]
+
+    def send(self, stage):
+        if stage == 0:
+            self.core[self.lines.head] = self.value[...]
+        for copy in self.stage_copies(stage):
+            copy.start()
+
+    def finish(self, stage):
+        for copy in self.stage_copies(stage):
+            copy.wait()
+        slots = self.core if stage == 0 else self.slots[stage - 1]
+        value = slots[0]
+        for slot in range(1, slots.shape[0]):
+            value = value + slots[slot]
+        if stage == 3:
+            self.total[...] = value
+        else:
+            self.slots[stage][self.lines.places[stage]] = value
+
+
+def sum_kernel(count, kinds, *refs):
+    grads, ln = refs[:kinds], refs[kinds]
+    totals, ln_total = refs[kinds + 1 : 2 * kinds + 1], refs[2 * kinds + 1]
+    scratch = refs[2 * kinds + 2 :]
+    lines = Lines(count)
+    each = 16
+    sums = [
+        DpSum(lines, grads[kind], totals[kind], scratch[kind * each : (kind + 1) * each])
+        for kind in range(kinds)
+    ]
+    small = LnSum(lines, ln, ln_total, scratch[kinds * each :])
+    lines.greet()
+    for entry in sums:
+        entry.core_send()
+    small.send(0)
+    for entry in sums:
+        entry.core_sum()
+        both_parts([entry], "spread_send", 0)
+    small.finish(0)
+    small.send(1)
+    for stage in range(3):
+        for entry in sums:
+            both_parts([entry], "spread_sum", stage)
+            if stage < 2:
+                both_parts([entry], "spread_send", stage + 1)
+            else:
+                both_parts([entry], "gather_send", 2)
+        small.finish(stage + 1)
+        if stage < 2:
+            small.send(stage + 2)
+    for stage in reversed(range(3)):
+        for entry in sums:
+            both_parts([entry], "gather_wait", stage)
+            if stage > 0:
+                both_parts([entry], "gather_send", stage - 1)
+            else:
+                entry.store()
+
+
+def sum_over_all(grads, ln):
+    count = lax.axis_size("dp")
+    kinds = len(grads)
+    rows = [padded_rows(grad.shape[2], count) for grad in grads]
+    vmem = pl.BlockSpec(memory_space=pltpu.VMEM)
+    scratch = []
+    for count_rows in rows:
+        scratch += sum_scratch(count_rows, count)
+    scratch += ln_scratch(count)
+    return pl.pallas_call(
+        functools.partial(sum_kernel, count, kinds),
+        in_specs=[vmem] * (kinds + 1),
+        out_specs=[vmem] * (kinds + 1),
+        out_shape=[shaped((2, count_rows, HALF)) for count_rows in rows] + [shaped((4, D), f32)],
+        scratch_shapes=scratch,
+        compiler_params=pltpu.CompilerParams(
+            collective_id=0, has_side_effects=True, vmem_limit_bytes=60 * 1024 * 1024
+        ),
+        name="sum_over_all",
+    )(*grads, ln)
+
+
+RATES = (
+    float(D) ** (-0.5),
+    4.0 * float(D) ** (-0.5),
+    float(D) ** (-0.5),
+    float(FF) ** (-0.5),
+    0.7,
+)
 
 
 def adam_step(gradient, weight, moment_one, moment_two, step_rate):
     first_new = beta_one * moment_one + (1.0 - beta_one) * gradient
     second_new = beta_two * moment_two + (1.0 - beta_two) * gradient * gradient
-    first_hat = first_new / (1.0 - beta_one**STEP)
-    second_hat = second_new / (1.0 - beta_two**STEP)
+    first_hat = first_new * (1.0 / (1.0 - beta_one**STEP))
+    second_hat = second_new * (1.0 / (1.0 - beta_two**STEP))
     weight_new = weight - step_rate * (
         first_hat / (jnp.sqrt(second_hat) + epsilon_adam) + decay_rate * weight
     )
     return (weight_new, first_new, second_new)
+
+
+def kind_gradient(kind, ref):
+    if kind == 0:
+        return jnp.concatenate([ref[0, 0], ref[1, 0]], axis=0).astype(f32)[None]
+    if kind == 2:
+        blocks = [ref[part, block] for block in range(2) for part in range(2)]
+        return jnp.concatenate(blocks, axis=1).astype(f32)
+    return jnp.concatenate([ref[0], ref[1]], axis=1).astype(f32)
+
+
+BLOCKS = (
+    (3, (1, D, HALF), (2, 1, HALF, HALF)),
+    (1, (HALF, D), (2, HALF, HALF)),
+    (4, (128, 1024), (2, 2, 128, HALF)),
+    (4, (HALF, D), (2, HALF, HALF)),
+)
+
+
+def adam_kernel(kinds, owners, *refs):
+    step = pl.program_id(0)
+    chip = lax.axis_index("dp")
+    count = len(kinds)
+    first = 0
+    for index, kind in enumerate(kinds):
+        grad, weight, one, two = refs[index * 4 : index * 4 + 4]
+        owned, new, first_new, second_new, copy = refs[
+            count * 4 + index * 5 : count * 4 + index * 5 + 5
+        ]
+        steps = BLOCKS[kind][0]
+
+        @pl.when((step >= first) & (step < first + steps))
+        def _(kind=kind, grad=grad, weight=weight, one=one, two=two, owned=owned, new=new,
+              first_new=first_new, second_new=second_new, copy=copy):
+            gradient = kind_gradient(kind, grad)
+            results = adam_step(gradient, weight[...], one[...], two[...], RATES[kind])
+            owned[...] = jnp.where(owners[kind] == chip, gradient, 0.0)
+            new[...] = results[0]
+            first_new[...] = results[1]
+            second_new[...] = results[2]
+            copy[...] = results[0].astype(bf16)
+
+        first += steps
+
+
+def adam_update(kinds, owners, grads, weights, ones, twos):
+    in_specs, out_specs, out_shape, operands = [smem_spec], [], [], [owners]
+    first = 0
+    for index, kind in enumerate(kinds):
+        steps, block, grad_block = BLOCKS[kind]
+
+        def place(i, first=first, steps=steps):
+            return jnp.clip(i - first, 0, steps - 1)
+
+        def at(i, place=place, rank=len(block)):
+            return (place(i),) + (0,) * (rank - 1)
+
+        def grad_at(i, place=place, kind=kind):
+            if kind == 0:
+                return (0, place(i), 0, 0)
+            if kind == 2:
+                return (0, 0, place(i), 0)
+            return (0, place(i), 0)
+
+        spec = pl.BlockSpec(block, at)
+        in_specs += [pl.BlockSpec(grad_block, grad_at), spec, spec, spec]
+        out_specs += [spec] * 5
+        whole = weights[index].shape
+        out_shape += [shaped(whole, f32)] * 4 + [shaped(whole)]
+        operands += [grads[index], weights[index], ones[index], twos[index]]
+        first += steps
+    results = pl.pallas_call(
+        functools.partial(adam_kernel, kinds),
+        grid=(first,),
+        in_specs=in_specs,
+        out_specs=out_specs,
+        out_shape=out_shape,
+        compiler_params=limits,
+        name="adam_update",
+    )(*operands)
+    return [results[index * 5 : index * 5 + 5] for index in range(len(kinds))]
 
 
 def gather_inputs(tokens, cotangent, w_qkv, w_out, w_up, w_down):
@@ -652,51 +1081,33 @@
     )
     output_rows = place_rows(y)
     grad_input = place_rows(gx)
-    halves = []
-    for grad in (g_qkv, g_out, g_up, g_down):
-        halves.append(grad[0].astype(f32) + swap_heads(grad[1]).astype(f32))
-    summed = [lax.psum(half.astype(bf16), "dp").astype(f32) for half in halves]
-    summed[0] = summed[0].transpose(1, 0, 2)
-    summed.append(lax.psum(g_ln, ("dp", "head")))
-    masters = (w_qkv, w_out, w_up, w_down, ln_params)
-    firsts = (m_qkv, m_out, m_up, m_down, m_ln)
-    seconds = (v_qkv, v_out, v_up, v_down, v_ln)
-    rates = (
-        float(D) ** (-0.5),
-        4.0 * float(D) ** (-0.5),
-        float(D) ** (-0.5),
-        float(FF) ** (-0.5),
-        0.7,
+    totals = sum_over_all((g_down, g_up, g_out, g_qkv), g_ln)
+    t_down, t_up, t_out, t_qkv = [
+        total[:, :rows] for total, rows in zip(totals, (1024, 1024, HALF, 3 * HALF))
+    ]
+
+    def as_blocks(array):
+        return array.transpose(1, 0, 2)
+
+    t_ln = totals[4]
+    results = adam_update(
+        (0, 1, 2, 3),
+        owners,
+        (t_qkv.reshape(2, 3, HALF, HALF), t_out, t_up.reshape(2, 2, D, HALF), t_down),
+        (as_blocks(w_qkv), w_out, w_up, w_down),
+        (as_blocks(m_qkv), m_out, m_up, m_down),
+        (as_blocks(v_qkv), v_out, v_up, v_down),
     )
-    updated = [
-        adam_step(
-            summed[kind_index],
-            masters[kind_index],
-            firsts[kind_index],
-            seconds[kind_index],
-            rates[kind_index],
-        )
-        for kind_index in range(5)
+    results[0] = [as_blocks(array) for array in results[0]]
+    mine = owners[4] == lax.axis_index("dp")
+    ln_results = adam_step(t_ln, ln_params, m_ln, v_ln, RATES[4])
+    results.append([jnp.where(mine, t_ln, 0.0), *ln_results])
+    owned, new, first, second = [
+        tuple(results[kind][slot] for kind in range(5)) for slot in range(4)
     ]
-    new_weights = tuple((entry[0] for entry in updated))
-    new_firsts = tuple((entry[1] for entry in updated))
-    new_seconds = tuple((entry[2] for entry in updated))
-    device_index = lax.axis_index("dp")
-    owned_grads = tuple(
-        (
-            jnp.where(owners[kind_index] == device_index, summed[kind_index], 0.0)[None]
-            for kind_index in range(5)
-        )
-    )
-    copies = tuple((new_weights[kind_index].astype(jnp.bfloat16) for kind_index in range(4)))
-    return (
-        (output_rows, grad_input)
-        + owned_grads
-        + tuple(new_weights)
-        + tuple(new_firsts)
-        + tuple(new_seconds)
-        + copies
-    )
+    copies = tuple(results[kind][4] for kind in range(4))
+    owned = tuple(array[None] for array in owned)
+    return (output_rows, grad_input) + owned + new + first + second + copies
 
 
 PLACED = (

time: 324 us -> 249 us (0.77)
  Pallas kernels: 114 us -> 228 us
  waiting for transfers between devices: 98 us -> 0.02 us
  blocking collectives: 44.7 us -> 0 us
  other arithmetic: 33.6 us -> 9.9 us
  between operations: 17.6 us -> 1.55 us
  local copies, waits for them, and re-layouts: 11.1 us -> 6.52 us
    pallas_call x0 -> x2, Pallas kernels: none -> 114 us  [the longest x1 91.4 us: sum_over_all(): pl.pallas_call(functools.partial(sum_kernel, count, kinds), in_specs=[vme...]
    psum x1 -> x0, waiting for transfers between devices: 95.8 us -> none  [body(): summed = [lax.psum(half.astype(bf16), 'dp').astype(f32) for half in halves]]
    psum x1 -> x0, blocking collectives: 44.7 us -> none  [body(): summed.append(lax.psum(g_ln, ('dp', 'head')))]
    convert_element_type x7 -> x0, other arithmetic: 23.6 us -> none  [the longest x4 20.1 us: body(): new_weights[kind_index].astype(jnp.bfloat16)]
  transfers between devices with their start and end apart: 13 -> 8, of which waited for: 2 -> 0; matrix products, arithmetic and copies ran while one was open for 5% -> 4% of each run, Pallas kernels for 9% -> 72%
where the time goes in v2:
time: 249 us; the launch traced here: 248 us
  Pallas kernels  228 us (92%)
  other arithmetic  9.9 us (4%)
  local copies, waits for them, and re-layouts  6.52 us (3%)
  starting transfers between devices  2.51 us (1%)
    pallas_call x1, Pallas kernels, sum_over_all(): pl.pallas_call(functools.partial(sum_kernel, count, kinds), in_specs=[vme...  91.4 us
    pallas_call x1, Pallas kernels, layer_local(): pl.pallas_call(mlp_both_ways, grid=(TILES,), in_specs=[smem_spec, rows_sp...  49.6 us
    pallas_call x1, Pallas kernels, layer_local(): pl.pallas_call(backward_attention, grid=(TILES,), in_specs=[smem_spec, ro...  36.5 us
    pallas_call x1, Pallas kernels, layer_local(): pl.pallas_call(forward_attention, grid=(TILES,), in_specs=[smem_spec, row...  27.9 us
    pallas_call x1, Pallas kernels, adam_update(): pl.pallas_call(functools.partial(adam_kernel, kinds), grid=(first,), in_s...  22.3 us
  transfers between devices with their start and end apart: 8, of which 0 were waited for; matrix products, arithmetic and copies ran while one was open for 4% of the time, Pallas kernels for 72%

profile of v2, /device:TPU:0, one launch (start us, length us, event | category | flops | bytes accessed | tf_op | source)
XLA Modules:
  0.0 248.1 jit_solution(5855729729968044563)
XLA Ops:
  0.7 0.0 copy-start.2
  0.7 2.5 %bitcast_convert_fusion.w_own = bf16[3,512,256]{2,1,0:T(8,128)(2,1)} fusion(f32[512,3,256]{2,0,1:T(8,128)} %param.25), kind=kLoop, calls=%fused_computation.16 | loop fusion | flops 393216 | bytes 2359296 | tf_op jit(solution)/shard_map/convert_element_type | solution.py:1027
  3.2 0.5 collective-permute-start.2
  3.7 1.1 convert_element_type.15.down_own
  4.8 0.1 collective-permute-start.5
  4.8 0.0 copy-done.1
  4.8 1.1 convert_element_type.14.up_own
  6.0 0.8 collective-permute-start.4
  6.7 0.0 copy-done.3
  6.7 1.1 dynamic-slice_bitcast_fusion.2
  7.9 0.0 collective-permute-start
  7.9 0.9 copy-done.4
  8.7 1.5 dynamic-slice_bitcast_fusion
  10.2 0.0 collective-permute-start.1
  10.2 0.0 copy-start.10
  10.2 0.0 collective-permute-done.2.w_other
  10.2 0.6 collective-permute-start.3
  10.8 0.0 collective-permute-done.x_other
  10.8 1.0 copy-done
  11.8 27.9 %forward_attention.1 = (bf16[2048,1536]{1,0:T(8,128)(2,1)}, bf16[2048,1024]{1,0:T(8,128)(2,1)}, bf16[64,256,256]{2,1,0:T(8,128)(2,1)}, bf16[2048,512]{1,0:T(8,128)(2,1)}) custom-call(f32[2,16]{1,0:T(2,128)} %constant.41.clone.table, bf16[2048,256]{1,0:T(8,128)(2,1)} %get-tuple-element.118.x_own, bf16[2048,256]{1,0:T(8,128)(2,1)} %copy-done, f32[4,512]{1,0:T(4,128)} %ln.5, ...), custom_call_target="tpu_custom_call" | custom-call | tf_op jit(solution)/shard_map/forward_attention/pallas_call | solution.py:436
  39.6 0.0 collective-permute-done.3.out_other
  39.6 0.0 copy-start.11
  39.7 0.0 collective-permute-done.5.down_other
  39.7 0.0 copy-start.8
  39.7 0.0 copy-start.9
  39.7 0.6 copy-done.11
  40.4 0.4 copy-done.8
  40.7 0.3 copy-done.9
  41.1 49.6 %mlp_both_ways.1 = (bf16[2048,256]{1,0:T(8,128)(2,1)}, bf16[2048,256]{1,0:T(8,128)(2,1)}, f32[2048,512]{1,0:T(8,128)}, bf16[2048,512]{1,0:T(8,128)(2,1)}, bf16[2...) custom-call(s32[2]{0:T(128)} %lengths.1, ...), custom_call_target="tpu_custom_call" | custom-call | tf_op jit(solution)/shard_map/mlp_both_ways/pallas_call | solution.py:459
  90.7 0.1 collective-permute-start.6
  90.8 0.6 slice.3
  92.1 0.0 copy-start.16
  92.1 36.5 %backward_attention.1 = (bf16[2048,256]{1,0:T(8,128)(2,1)}, bf16[2048,256]{1,0:T(8,128)(2,1)}, bf16[2,2,768,256]{3,2,1,0:T(8,128)(2,1)}, f32[2,512]{1,0:T(2,128)}) custom-call(f32[2,16]{1,0:T(2,128)} %constant.41.clone.table, bf16[2048,256]{1,0:T(8,128)(2,1)} %get-tuple-element.118.x_own, bf16[2048,256]{1,0:T(8,128)(2,1)} %copy-done, f32[4,512]{1,0:T(4,128)} %ln.5, ...), custom_call_target="tpu_custom_call" | custom-call | tf_op jit(solution)/shard_map/backward_attention/pallas_call | solution.py:533
  128.6 0.5 collective-permute-start.7
  129.1 1.3 pad_maximum_fusion.2.refs_4_
  130.3 91.4 %sum_over_all.1 = (bf16[2,1024,256]{2,1,0:T(8,128)(2,1)}, bf16[2,1024,256]{2,1,0:T(8,128)(2,1)}, bf16[2,256,256]{2,1,0:T(8,128)(2,1)}, bf16[2,768,256]{2,1,0:T(8,128)(2,1)}, f32[4,512]{1,0:T(4,128)}) custom-call(bf16[2,2,1024,256]{3,2,1,0:T(8,128)(2,1)} %get-tuple-element.77.refs_0_, bf16[2,2,1024,256]{3,2,1,0:T(8,128)(2,1)} %get-tuple-element.78.refs_1_, ...), custom_call_target="tpu_custom_call" | custom-call | tf_op jit(solution)/shard_map/sum_over_all/pallas_call | solution.py:903
  221.7 0.0 copy-start.12
  221.7 0.0 copy-start.13
  221.7 0.0 copy-start.14
  221.8 0.0 copy-start.6
  221.8 22.3 %adam_update.1 = (f32[3,512,256]{2,1,0:T(8,128)}, f32[3,512,256]{2,1,0:T(8,128)}, f32[3,512,256]{2,1,0:T(8,128)}, f32[3,512,256]{2,1,0:T(8,128)}, bf16[3,512,256...) custom-call(s32[5]{0:T(128)} %owners.1, ...), custom_call_target="tpu_custom_call" | custom-call | tf_op jit(solution)/shard_map/adam_update/pallas_call | solution.py:1005
  244.1 0.6 multiply_subtract_fusion
  244.8 0.0 collective-permute-done.6
  244.8 0.1 broadcast_select_fusion.3
  244.9 1.5 pad_maximum_fusion
  246.4 0.1 copy-done.7
  246.5 0.1 broadcast_select_fusion.1
  246.7 1.5 pad_maximum_fusion.1
  (22 shorter events, 0.1 us)
Async XLA Ops:
  0.7 3.0 %copy-start.2 = (f32[1024,512]{1,0:T(8,128)S(1)}, f32[1024,512]{1,0:T(8,128)}, u32[]{:S(2)}) copy-start(f32[1024,512]{1,0:T(8,128)} %refs_13_.1) | copy-start | bytes 6291460
  3.2 1.6 copy-start.1
  3.2 7.0 %collective-permute-start.2 = (bf16[3,512,256]{2,1,0:T(8,128)(2,1)}, bf16[3,512,256]{2,1,0:T(8,128)(2,1)}, u32[]{:S(2)}, u32[]{:S(2)}) collective-permute-start(bf16[3,512,256]{2,1,0:T(8,128)(2,1)} %bitcast_convert_fusion.w_own), channel_id=1, source_target_pairs={{0,1},{1,0},{2,3},{3,2},{4,5},{5,4},{6,7},{7,6},{8,9},{9,8},{10,11... | collective-permute-start | bytes 2359304 | tf_op jit(solution)/shard_map/ppermute | solution.py:584
  4.8 2.0 copy-start.3
  4.8 34.9 %collective-permute-start.5 = (bf16[1024,512]{1,0:T(8,128)(2,1)}, bf16[1024,512]{1,0:T(8,128)(2,1)S(1)}, u32[]{:S(2)}, u32[]{:S(2)}) collective-permute-start(bf16[1024,512]{1,0:T(8,128)(2,1)} %convert_element_type.15.down_own), channel_id=1, source_target_pairs={{0,1},{1,0},{2,3},{3,2},{4,5},{5,4},{6,7},{7,6},{8,9},{9,8},{10,11... | collective-permute-start | bytes 3145736 | tf_op jit(solution)/shard_map/ppermute | solution.py:584
  6.0 33.7 %collective-permute-start.4 = (bf16[512,1024]{1,0:T(8,128)(2,1)}, bf16[512,1024]{1,0:T(8,128)(2,1)}, u32[]{:S(2)}, u32[]{:S(2)}) collective-permute-start(bf16[512,1024]{1,0:T(8,128)(2,1)} %convert_element_type.14.up_own), channel_id=1, source_target_pairs={{0,1},{1,0},{2,3},{3,2},{4,5},{5,4},{6,7},{7,6},{8,9},{9,8},{10,11... | collective-permute-start | bytes 3145736 | tf_op jit(solution)/shard_map/ppermute | solution.py:584
  6.7 2.0 copy-start.4
  7.9 3.0 %collective-permute-start = (bf16[2048,256]{1,0:T(8,128)(2,1)S(1)}, bf16[2048,256]{1,0:T(8,128)(2,1)S(1)}, u32[]{:S(2)}, u32[]{:S(2)}) collective-permute-start(bf16[2048,256]{1,0:T(8,128)(2,1)S(1)} %get-tuple-element.117), channel_id=1, source_target_pairs={{0,1},{1,0},{2,3},{3,2},{4,5},{5,4},{6,7},{7,6},{8,9},{9,8},{10,11... | collective-permute-start | bytes 3145736 | tf_op jit(solution)/shard_map/ppermute | solution.py:584
  8.7 1.5 copy-start.5
  10.2 29.5 %collective-permute-start.1 = (bf16[2048,256]{1,0:T(8,128)(2,1)}, bf16[2048,256]{1,0:T(8,128)(2,1)S(1)}, u32[]{:S(2)}, u32[]{:S(2)}) collective-permute-start(bf16[2048,256]{1,0:T(8,128)(2,1)} %get-tuple-element.115), channel_id=1, source_target_pairs={{0,1},{1,0},{2,3},{3,2},{4,5},{5,4},{6,7},{7,6},{8,9},{9,8},{10,11... | collective-permute-start | bytes 3145736 | tf_op jit(solution)/shard_map/ppermute | solution.py:584
  10.2 29.5 %copy-start.10 = (bf16[256,512]{1,0:T(8,128)(2,1)}, bf16[256,512]{1,0:T(8,128)(2,1)S(1)}, u32[]{:S(2)}) copy-start(bf16[256,512]{1,0:T(8,128)(2,1)S(1)} %convert_element_type.13.out_own) | copy-start | bytes 786436
  10.2 29.4 %collective-permute-start.3 = (bf16[256,512]{1,0:T(8,128)(2,1)S(1)}, bf16[256,512]{1,0:T(8,128)(2,1)S(1)}, u32[]{:S(2)}, u32[]{:S(2)}) collective-permute-start(bf16[256,512]{1,0:T(8,128)(2,1)S(1)} %convert_element_type.13.out_own), channel_id=1, source_target_pairs={{0,1},{1,0},{2,3},{3,2},{4,5},{5,4},{6,7},{7,6},{8,9},{9,8},{10,11... | collective-permute-start | bytes 786440 | tf_op jit(solution)/shard_map/ppermute | solution.py:584
  10.8 1.0 copy-start
  39.6 0.7 copy-start.11
  39.7 1.0 copy-start.8
  39.7 1.3 copy-start.9
  41.1 49.8 %copy-start.17 = (s32[5]{0:T(128)S(1)}, s32[5]{0:T(128)}, u32[]{:S(2)}) copy-start(s32[5]{0:T(128)} %owners.1) | copy-start | bytes 64
  90.7 154.1 %collective-permute-start.6 = (bf16[2048,256]{1,0:T(8,128)(2,1)}, bf16[2048,256]{1,0:T(8,128)(2,1)S(1)}, u32[]{:S(2)}, u32[]{:S(2)}) collective-permute-start(bf16[2048,256]{1,0:T(8,128)(2,1)} %get-tuple-element.69), channel_id=1, source_target_pairs={{0,1},{1,0},{2,3},{3,2},{4,5},{5,4},{6,7},{7,6},{8,9},{9,8},{10,11... | collective-permute-start | bytes 3145736 | tf_op jit(solution)/shard_map/ppermute | solution.py:584
  92.1 37.0 %copy-start.16 = (f32[2,512]{1,0:T(2,128)S(1)}, f32[2,512]{1,0:T(2,128)}, u32[]{:S(2)}) copy-start(f32[2,512]{1,0:T(2,128)} %get-tuple-element.82) | copy-start | bytes 12292
  128.6 117.8 %collective-permute-start.7 = (bf16[2048,256]{1,0:T(8,128)(2,1)}, bf16[2048,256]{1,0:T(8,128)(2,1)S(1)}, u32[]{:S(2)}, u32[]{:S(2)}) collective-permute-start(bf16[2048,256]{1,0:T(8,128)(2,1)} %get-tuple-element.76), channel_id=1, source_target_pairs={{0,1},{1,0},{2,3},{3,2},{4,5},{5,4},{6,7},{7,6},{8,9},{9,8},{10,11... | collective-permute-start | bytes 3145736 | tf_op jit(solution)/shard_map/ppermute | solution.py:584
  221.7 22.4 %copy-start.12 = (f32[4,512]{1,0:T(4,128)S(1)}, f32[4,512]{1,0:T(4,128)}, u32[]{:S(2)}) copy-start(f32[4,512]{1,0:T(4,128)} %ln.5) | copy-start | bytes 24580
  221.7 22.4 %copy-start.13 = (f32[4,512]{1,0:T(4,128)S(1)}, f32[4,512]{1,0:T(4,128)}, u32[]{:S(2)}) copy-start(f32[4,512]{1,0:T(4,128)} %param.34) | copy-start | bytes 24580
  221.7 22.4 %copy-start.14 = (f32[4,512]{1,0:T(4,128)S(1)}, f32[4,512]{1,0:T(4,128)}, u32[]{:S(2)}) copy-start(f32[4,512]{1,0:T(4,128)} %param.39) | copy-start | bytes 24580
  221.8 22.4 %copy-start.15 = (f32[4,512]{1,0:T(4,128)S(1)}, f32[4,512]{1,0:T(4,128)}, u32[]{:S(2)}) copy-start(f32[4,512]{1,0:T(4,128)} %get-tuple-element.91) | copy-start | bytes 24580
  221.8 23.0 %copy-start.6 = (bf16[2048,256]{1,0:T(8,128)(2,1)S(1)}, bf16[2048,256]{1,0:T(8,128)(2,1)}, u32[]{:S(2)}) copy-start(bf16[2048,256]{1,0:T(8,128)(2,1)} %get-tuple-element.68) | copy-start | bytes 3145732
  244.9 1.6 copy-start.7

commit v3 on v1

--- a/solution.py
+++ b/solution.py
@@ -275,14 +275,316 @@
 
     @pl.when(step == TILES - 1)
     def _():
-        g_out[...] = acc_out[...].astype(bf16)
-        g_up[0] = acc_up[:, : FF // 2].astype(bf16)
-        g_up[1] = acc_up[:, FF // 2 :].astype(bf16)
-        g_down[...] = acc_down[...].astype(bf16)
+        for side in range(2):
+            for part in range(2):
+                lanes = slice(part * HALF, (part + 1) * HALF)
+                g_out[side, part] = acc_out[side * HALF : (side + 1) * HALF, lanes].astype(bf16)
+                g_down[side, part] = acc_down[side * 1024 : (side + 1) * 1024, lanes].astype(bf16)
+                for block in range(2):
+                    at = side * 1024 + block * D + part * HALF
+                    rows = slice(block * D, (block + 1) * D)
+                    g_up[side, part, rows] = acc_up[:, at : at + HALF].astype(bf16)
         g_ln[...] = acc_ln[...]
 
 
+def swap_heads(value):
+    return lax.ppermute(value, "head", [(0, 1), (1, 0)])
+
+
+def chip_grid(count):
+    side = 1 << ((count.bit_length() - 1) // 3)
+    return (count // (side * side), side, side)
+
+
+class Lines:
+    def __init__(self, count):
+        self.sizes = chip_grid(count)
+        self.strides = (self.sizes[1] * self.sizes[2], self.sizes[2], 1)
+        self.chip = lax.axis_index("dp")
+        self.head = lax.axis_index("head")
+        self.places = [
+            lax.rem(self.chip // stride, size) for stride, size in zip(self.strides, self.sizes)
+        ]
+
+    def partner(self):
+        return (self.chip, 1 - self.head)
+
+    def member(self, axis, ahead):
+        size = self.sizes[axis]
+        place = lax.rem(self.places[axis] + ahead, size)
+        chip = self.chip + (place - self.places[axis]) * self.strides[axis]
+        return place, (chip, self.head)
+
+    def greet(self):
+        barrier = pltpu.get_barrier_semaphore()
+        others = [self.partner()]
+        for axis in range(3):
+            others += [self.member(axis, ahead)[1] for ahead in range(1, self.sizes[axis])]
+        for other in others:
+            pl.semaphore_signal(
+                barrier, inc=1, device_id=other, device_id_type=pl.DeviceIdType.MESH
+            )
+        pl.semaphore_wait(barrier, len(others))
+
+
+ORDERS = ((2, 1, 0), (1, 2, 0))
+
+
+def whole_slices(count):
+    return all(rows % (16 * count) == 0 for rows in PIECE_ROWS + (3 * HALF,))
+
+
+def chunk_rows(rows):
+    return next(chunk for chunk in (64, 48, 32, 16) if rows % chunk == 0)
+
+
+def sum_scratch(rows, count):
+    sizes = chip_grid(count)
+    shapes = [
+        pltpu.VMEM((2, rows, HALF), bf16),
+        pltpu.VMEM((2, rows, HALF), bf16),
+        pltpu.VMEM((2, rows, HALF), bf16),
+    ]
+    sems = [pltpu.SemaphoreType.DMA((2,))]
+    for order in ORDERS:
+        left = rows
+        for axis in order:
+            left //= sizes[axis]
+            shapes.append(pltpu.VMEM((sizes[axis] - 1, left, HALF), bf16))
+            sems.append(pltpu.SemaphoreType.DMA((2, 2, sizes[axis] - 1)))
+    return shapes + sems + [pltpu.SemaphoreType.DMA((1,))]
+
+
+class DpSum:
+    def __init__(self, lines, grads, total, scratch):
+        self.lines = lines
+        self.grads = grads
+        self.total = total
+        self.rows = grads.shape[2]
+        self.work, self.arrived, self.final = scratch[:3]
+        self.slots = (scratch[3:6], scratch[6:9])
+        self.core_sem = scratch[9]
+        self.sems = (scratch[10:13], scratch[13:16])
+        self.store_sem = scratch[16]
+        self.base = []
+        for order in ORDERS:
+            bases, piece = [0], self.rows
+            for axis in order:
+                piece //= lines.sizes[axis]
+                bases.append(bases[-1] + lines.places[axis] * piece)
+            self.base.append(bases)
+
+    def remote(self, source, target, send_sem, recv_sem, device):
+        return pltpu.make_async_remote_copy(
+            src_ref=source,
+            dst_ref=target,
+            send_sem=send_sem,
+            recv_sem=recv_sem,
+            device_id=device,
+            device_id_type=pl.DeviceIdType.MESH,
+        )
+
+    def core_copy(self):
+        return self.remote(
+            self.grads.at[1],
+            self.arrived,
+            self.core_sem.at[0],
+            self.core_sem.at[1],
+            self.lines.partner(),
+        )
+
+    def core_send(self):
+        self.core_copy().start()
+
+    def core_sum(self):
+        self.core_copy().wait()
+        chunk = chunk_rows(self.rows)
+        for part in range(2):
+
+            def add(index, carry, part=part):
+                rows = pl.ds(pl.multiple_of(index * chunk, chunk), chunk)
+                own = self.grads[0, part, rows, :].astype(f32)
+                away = self.arrived[part, rows, :].astype(f32)
+                self.work[part, rows, :] = (own + away).astype(bf16)
+                return carry
+
+            lax.fori_loop(0, self.rows // chunk, add, 0)
+
+    def spread_copies(self, part, stage):
+        axis = ORDERS[part][stage]
+        size = self.lines.sizes[axis]
+        base = self.base[part][stage]
+        piece = self.rows
+        for at in ORDERS[part][: stage + 1]:
+            piece //= self.lines.sizes[at]
+        copies = []
+        for ahead in range(1, size):
+            place, device = self.lines.member(axis, ahead)
+            start = pl.multiple_of(base + place * piece, 16)
+            copies.append(
+                self.remote(
+                    self.work.at[part, pl.ds(start, piece)],
+                    self.slots[part][stage].at[ahead - 1],
+                    self.sems[part][stage].at[0, 0, ahead - 1],
+                    self.sems[part][stage].at[0, 1, ahead - 1],
+                    device,
+                )
+            )
+        return copies, self.base[part][stage + 1], piece
+
+    def spread_send(self, part, stage):
+        for copy in self.spread_copies(part, stage)[0]:
+            copy.start()
+
+    def spread_sum(self, part, stage):
+        copies, mine, piece = self.spread_copies(part, stage)
+        for copy in copies:
+            copy.wait()
+        slots = self.slots[part][stage]
+        target = self.final if stage == 2 else self.work
+        chunk = chunk_rows(piece)
+
+        def add(index, carry):
+            offset = pl.multiple_of(index * chunk, chunk)
+            rows = pl.ds(pl.multiple_of(mine + offset, 16), chunk)
+            value = self.work[part, rows, :].astype(f32)
+            for slot in range(len(copies)):
+                value = value + slots[slot, pl.ds(offset, chunk), :].astype(f32)
+            target[part, rows, :] = value.astype(bf16)
+            return carry
+
+        lax.fori_loop(0, piece // chunk, add, 0)
+
+    def gather_copies(self, part, stage):
+        axis = ORDERS[part][stage]
+        size = self.lines.sizes[axis]
+        piece = self.rows
+        for at in ORDERS[part][: stage + 1]:
+            piece //= self.lines.sizes[at]
+        mine = pl.multiple_of(self.base[part][stage + 1], 16)
+        rows = pl.ds(mine, piece)
+        copies = []
+        for ahead in range(1, size):
+            _, device = self.lines.member(axis, ahead)
+            copies.append(
+                self.remote(
+                    self.final.at[part, rows],
+                    self.final.at[part, rows],
+                    self.sems[part][stage].at[1, 0, ahead - 1],
+                    self.sems[part][stage].at[1, 1, ahead - 1],
+                    device,
+                )
+            )
+        return copies
+
+    def gather_send(self, part, stage):
+        for copy in self.gather_copies(part, stage):
+            copy.start()
+
+    def gather_wait(self, part, stage):
+        for copy in self.gather_copies(part, stage):
+            copy.wait()
+
+    def store_copy(self):
+        return pltpu.make_async_copy(self.final, self.total, self.store_sem.at[0])
+
+    def event(self, index):
+        if index == 0:
+            self.core_send()
+        elif index == 1:
+            self.core_sum()
+        for part in range(2):
+            if 2 <= index <= 4:
+                self.spread_sum(part, index - 2)
+            elif index >= 5:
+                self.gather_wait(part, 7 - index)
+            if 1 <= index <= 3:
+                self.spread_send(part, index - 1)
+            elif 4 <= index <= 6:
+                self.gather_send(part, 6 - index)
+        if index == 7:
+            self.store_copy().start()
+
+    def finish(self):
+        self.store_copy().wait()
+
+
+EVENTS = 8
+
+
+def ln_scratch(count):
+    return [
+        pltpu.VMEM((2, 4, D), f32),
+        pltpu.SemaphoreType.DMA((2,)),
+        *[pltpu.VMEM((size, 4, D), f32) for size in chip_grid(count)],
+        *[pltpu.SemaphoreType.DMA((2, max(size - 1, 1))) for size in chip_grid(count)],
+    ]
+
+
+class LnSum:
+    def __init__(self, lines, value, total, scratch):
+        self.lines = lines
+        self.value = value
+        self.total = total
+        self.core, self.core_sem = scratch[:2]
+        self.slots = scratch[2:5]
+        self.sems = scratch[5:8]
+
+    def stage_copies(self, stage):
+        lines = self.lines
+        if stage == 0:
+            mine = self.core.at[lines.head]
+            return [
+                pltpu.make_async_remote_copy(
+                    src_ref=mine,
+                    dst_ref=mine,
+                    send_sem=self.core_sem.at[0],
+                    recv_sem=self.core_sem.at[1],
+                    device_id=lines.partner(),
+                    device_id_type=pl.DeviceIdType.MESH,
+                )
+            ]
+        axis = stage - 1
+        mine = self.slots[axis].at[lines.places[axis]]
+        return [
+            pltpu.make_async_remote_copy(
+                src_ref=mine,
+                dst_ref=mine,
+                send_sem=self.sems[axis].at[0, ahead - 1],
+                recv_sem=self.sems[axis].at[1, ahead - 1],
+                device_id=lines.member(axis, ahead)[1],
+                device_id_type=pl.DeviceIdType.MESH,
+            )
+            for ahead in range(1, lines.sizes[axis])
+        ]
+
+    def send(self, stage):
+        if stage == 0:
+            self.core[self.lines.head] = self.value[...]
+        for copy in self.stage_copies(stage):
+            copy.start()
+
+    def finish(self, stage):
+        for copy in self.stage_copies(stage):
+            copy.wait()
+        slots = self.core if stage == 0 else self.slots[stage - 1]
+        value = slots[0]
+        for slot in range(1, slots.shape[0]):
+            value = value + slots[slot]
+        if stage == 3:
+            self.total[...] = value
+        else:
+            self.slots[stage][self.lines.places[stage]] = value
+
+
+SCRATCH_EACH = 17
+PIECES = ((0, 0), (0, 512), (1, 0), (1, 512), (2, 0))
+PIECE_ROWS = (512, 512, 512, 512, HALF)
+SLOT_AT_HOOK = {0: 0, 1: 1, 3: 2, 4: 3, 6: 4, 7: 5, 9: 6, 10: 7}
+
+
 def backward_attention(
+    count,
     table,
     x_own,
     x_other,
@@ -294,19 +596,50 @@
     probs,
     grad_ctx,
     grad_res,
+    g_down,
+    g_up,
+    g_out,
+    g_ln_two,
     gx_own,
     gx_other,
-    g_qkv,
-    g_ln,
-    acc_qkv,
-    acc_ln,
-    after,
-    grad_qkv,
-    normed,
-    grad_n,
+    *refs,
 ):
+    summing = whole_slices(count)
+    kinds = len(PIECES) + 1 if summing else 1
+    totals, ln_total = refs[:kinds], refs[kinds]
+    acc_qkv, acc_ln, after, grad_qkv, normed, grad_n, g_qkv, ln_all = refs[kinds + 1 : kinds + 9]
+    scratch = refs[kinds + 9 :]
     head = lax.axis_index("head")
     step = pl.program_id(0)
+    sums = []
+    if summing:
+        lines = Lines(count)
+        sources = (g_down, g_up, g_out)
+        for index, (source, start) in enumerate(PIECES):
+            view = sources[source].at[:, :, pl.ds(start, PIECE_ROWS[index])]
+            part_scratch = scratch[index * SCRATCH_EACH : (index + 1) * SCRATCH_EACH]
+            sums.append(DpSum(lines, view, totals[index], part_scratch))
+        last = len(PIECES)
+        end = (last + 1) * SCRATCH_EACH
+        last_sum = DpSum(lines, g_qkv, totals[last], scratch[last * SCRATCH_EACH : end])
+        small = LnSum(lines, ln_all, ln_total, scratch[end:])
+
+    def run_slot(slot):
+        for index, entry in enumerate(sums):
+            if 0 <= slot - index < EVENTS:
+                entry.event(slot - index)
+
+    def hook(place):
+        for at in range(TILES if summing else 0):
+            slot = SLOT_AT_HOOK.get(at * 3 + place)
+            if slot is None:
+                continue
+
+            @pl.when(step == at)
+            def _(slot=slot):
+                if slot == 0:
+                    lines.greet()
+                run_slot(slot)
 
     @pl.when(step == 0)
     def _():
@@ -316,7 +649,8 @@
 
     low_lanes, high_lanes = lane_masks(bf16)
     scale_factor = float(HEAD_DIM) ** (-0.5)
-    for span in reversed(range(SPANS_TILE)):
+
+    def attention(span):
         rows = pl.ds(span * SPAN, SPAN)
         row_id = (TILES - 1 - step) * SPANS_TILE + span
         inverse = table[0, row_id]
@@ -342,6 +676,14 @@
             grad_qkv[rows, at_v : at_v + 128] = (grad_v[:SPAN] + after[:, lanes_v]).astype(bf16)
             after[:, lanes] += grad_k[SPAN:] * inverse
             after[:, lanes_v] += grad_v[SPAN:] * inverse
+
+    hook(0)
+    attention(3)
+    attention(2)
+    hook(1)
+    attention(1)
+    attention(0)
+    hook(2)
     for row in range(0, TILE, 128):
         rows = pl.ds(row, 128)
         x = join_columns(head, x_own[rows, :].astype(f32), x_other[rows, :].astype(f32))
@@ -377,8 +719,29 @@
 
     @pl.when(step == TILES - 1)
     def _():
-        g_qkv[...] = acc_qkv[...].astype(bf16)
-        g_ln[...] = acc_ln[...]
+        for side in range(2):
+            for part in range(2):
+                for kind in range(3):
+                    rows = slice(kind * HALF, (kind + 1) * HALF)
+                    half = slice(part * HALF, (part + 1) * HALF)
+                    g_qkv[side, part, rows] = acc_qkv[side, kind, half].astype(bf16)
+        ln_all[0:2, :] = acc_ln[...]
+        ln_all[2:4, :] = g_ln_two[...]
+        if not summing:
+            totals[0][...] = g_qkv[...]
+            ln_total[...] = ln_all[...]
+            return
+        late = len(SLOT_AT_HOOK)
+        for index in range(EVENTS):
+            last_sum.event(index)
+            if 1 <= index <= 4:
+                small.finish(index - 1)
+            if index <= 3:
+                small.send(index)
+            run_slot(late + index)
+        for entry in sums:
+            entry.finish()
+        last_sum.finish()
 
 
 def rows_spec(width, back=False):
@@ -469,9 +832,9 @@
             rows_spec(HALF),
             rows_spec(D),
             rows_spec(D),
-            whole_spec((D, D)),
-            whole_spec((2, D, FF // 2)),
-            whole_spec((FF, D)),
+            whole_spec((2, 2, HALF, HALF)),
+            whole_spec((2, 2, 1024, HALF)),
+            whole_spec((2, 2, 1024, HALF)),
             whole_spec((2, D)),
         ],
         out_shape=[
@@ -479,9 +842,9 @@
             shaped((SEQ, HALF)),
             shaped((SEQ, D), f32),
             shaped((SEQ, D)),
-            shaped((D, D)),
-            shaped((2, D, FF // 2)),
-            shaped((FF, D)),
+            shaped((2, 2, HALF, HALF)),
+            shaped((2, 2, 1024, HALF)),
+            shaped((2, 2, 1024, HALF)),
             shaped((2, D), f32),
         ],
         scratch_shapes=[
@@ -520,8 +883,21 @@
         down_own,
         down_other,
     )
-    gx_own, gx_other, g_qkv, g_ln_one = pl.pallas_call(
-        backward_attention,
+    count = lax.axis_size("dp")
+    summing = whole_slices(count)
+    sum_buffers, extra, total_specs, total_shapes = [], {}, [], []
+    if summing:
+        for rows in PIECE_ROWS + (3 * HALF,):
+            sum_buffers += sum_scratch(rows, count)
+            total_specs.append(pl.BlockSpec(memory_space=pl.ANY))
+            total_shapes.append(shaped((2, rows, HALF)))
+        sum_buffers += ln_scratch(count)
+        extra = dict(collective_id=0, has_side_effects=True)
+    else:
+        total_specs.append(whole_spec((2, 2, 3 * HALF, HALF)))
+        total_shapes.append(shaped((2, 2, 3 * HALF, HALF)))
+    gx_own, gx_other, *totals = pl.pallas_call(
+        functools.partial(backward_attention, count),
         grid=(TILES,),
         in_specs=[
             smem_spec,
@@ -535,19 +911,17 @@
             probs_spec(True),
             rows_spec(D, True),
             rows_spec(D, True),
-        ],
-        out_specs=[
-            rows_spec(HALF, True),
-            rows_spec(HALF, True),
-            whole_spec((2, 3, D, HALF)),
+            whole_spec((2, 2, 1024, HALF)),
+            whole_spec((2, 2, 1024, HALF)),
+            whole_spec((2, 2, HALF, HALF)),
             whole_spec((2, D)),
         ],
-        out_shape=[
-            shaped((SEQ, HALF)),
-            shaped((SEQ, HALF)),
-            shaped((2, 3, D, HALF)),
-            shaped((2, D), f32),
-        ],
+        out_specs=[rows_spec(HALF, True), rows_spec(HALF, True)]
+        + total_specs
+        + [whole_spec((4, D))],
+        out_shape=[shaped((SEQ, HALF)), shaped((SEQ, HALF))]
+        + total_shapes
+        + [shaped((4, D), f32)],
         scratch_shapes=[
             pltpu.VMEM((2, 3, D, HALF), f32),
             pltpu.VMEM((2, D), f32),
@@ -555,34 +929,145 @@
             pltpu.VMEM((TILE, 3 * D), bf16),
             pltpu.VMEM((TILE, D), bf16),
             pltpu.VMEM((TILE, D), f32),
-        ],
-        compiler_params=limits,
+            pltpu.VMEM((2, 2, 3 * HALF, HALF), bf16),
+            pltpu.VMEM((4, D), f32),
+        ]
+        + sum_buffers,
+        compiler_params=pltpu.CompilerParams(vmem_limit_bytes=60 * 1024 * 1024, **extra),
         name="backward_attention",
-    )(table, x_own, x_other, ln_params, qkv_own, qkv_other, qkv, bars, probs, grad_ctx, grad_res)
-    return (
-        (y_own, y_other),
-        (gx_own, gx_other),
-        g_qkv,
-        g_out.reshape(2, HALF, D),
+    )(
+        table,
+        x_own,
+        x_other,
+        ln_params,
+        qkv_own,
+        qkv_other,
+        qkv,
+        bars,
+        probs,
+        grad_ctx,
+        grad_res,
+        g_down,
         g_up,
-        g_down.reshape(2, FF // 2, D),
-        jnp.concatenate([g_ln_one, g_ln_two], axis=0),
+        g_out,
+        g_ln_two,
     )
-
-
-def swap_heads(value):
-    return lax.ppermute(value, "head", [(0, 1), (1, 0)])
+    if not summing:
+        g_qkv, g_ln = totals
+        grads = (g_down, g_up, g_out, g_qkv)
+        chips = [grad[0].astype(f32) + swap_heads(grad[1]).astype(f32) for grad in grads]
+        down, up, out, three = [lax.psum(chip.astype(bf16), "dp") for chip in chips]
+        ln_total = lax.psum(g_ln, ("dp", "head"))
+        totals = (down[:, :D], down[:, D:], up[:, :D], up[:, D:], out, three, ln_total)
+    return (y_own, y_other), (gx_own, gx_other), totals
+
+
+RATES = (
+    float(D) ** (-0.5),
+    4.0 * float(D) ** (-0.5),
+    float(D) ** (-0.5),
+    float(FF) ** (-0.5),
+    0.7,
+)
 
 
 def adam_step(gradient, weight, moment_one, moment_two, step_rate):
     first_new = beta_one * moment_one + (1.0 - beta_one) * gradient
     second_new = beta_two * moment_two + (1.0 - beta_two) * gradient * gradient
-    first_hat = first_new / (1.0 - beta_one**STEP)
-    second_hat = second_new / (1.0 - beta_two**STEP)
+    first_hat = first_new * (1.0 / (1.0 - beta_one**STEP))
+    second_hat = second_new * (1.0 / (1.0 - beta_two**STEP))
     weight_new = weight - step_rate * (
         first_hat / (jnp.sqrt(second_hat) + epsilon_adam) + decay_rate * weight
     )
     return (weight_new, first_new, second_new)
+
+
+def kind_gradient(kind, refs, step):
+    if kind == 0:
+        ref = refs[0]
+        return jnp.concatenate([ref[0, 0], ref[1, 0]], axis=0).astype(f32)[None]
+    sides = [jnp.concatenate([ref[0], ref[1]], axis=1) for ref in refs]
+    if kind == 2:
+        return jnp.concatenate(sides, axis=1).astype(f32)
+    if kind == 3:
+        return jnp.where(step < 2, sides[0].astype(f32), sides[1].astype(f32))
+    return sides[0].astype(f32)
+
+
+BLOCKS = (
+    (3, (1, D, HALF), (2, 1, HALF, HALF)),
+    (1, (HALF, D), (2, HALF, HALF)),
+    (4, (128, 1024), (2, 128, HALF)),
+    (4, (HALF, D), (2, HALF, HALF)),
+)
+GRADS = (1, 1, 2, 2)
+
+
+def adam_kernel(kinds, owners, *refs):
+    step = pl.program_id(0)
+    chip = lax.axis_index("dp")
+    ins = sum(GRADS[kind] + 3 for kind in kinds)
+    inputs, outputs = list(refs[:ins]), list(refs[ins:])
+    first = 0
+    for kind in kinds:
+        grads = [inputs.pop(0) for _ in range(GRADS[kind])]
+        weight, one, two = [inputs.pop(0) for _ in range(3)]
+        owned, new, first_new, second_new, copy = [outputs.pop(0) for _ in range(5)]
+        steps = BLOCKS[kind][0]
+
+        @pl.when((step >= first) & (step < first + steps))
+        def _(kind=kind, grads=grads, weight=weight, one=one, two=two, owned=owned, new=new,
+              first_new=first_new, second_new=second_new, copy=copy, first=first):
+            gradient = kind_gradient(kind, grads, step - first)
+            results = adam_step(gradient, weight[...], one[...], two[...], RATES[kind])
+            owned[...] = jnp.where(owners[kind] == chip, gradient, 0.0)
+            new[...] = results[0]
+            first_new[...] = results[1]
+            second_new[...] = results[2]
+            copy[...] = results[0].astype(bf16)
+
+        first += steps
+
+
+def adam_update(kinds, owners, grads, weights, ones, twos):
+    in_specs, out_specs, out_shape, operands = [smem_spec], [], [], [owners]
+    first = 0
+    for index, kind in enumerate(kinds):
+        steps, block, grad_block = BLOCKS[kind]
+
+        def place(i, first=first, steps=steps):
+            return jnp.clip(i - first, 0, steps - 1)
+
+        def at(i, place=place, rank=len(block)):
+            return (place(i),) + (0,) * (rank - 1)
+
+        for piece in range(GRADS[kind]):
+
+            def grad_at(i, place=place, kind=kind, piece=piece):
+                if kind == 0:
+                    return (0, place(i), 0, 0)
+                if kind == 3:
+                    return (0, jnp.clip(place(i) - 2 * piece, 0, 1), 0)
+                return (0, place(i), 0)
+
+            in_specs.append(pl.BlockSpec(grad_block, grad_at))
+        spec = pl.BlockSpec(block, at)
+        in_specs += [spec] * 3
+        out_specs += [spec] * 5
+        whole = weights[index].shape
+        out_shape += [shaped(whole, f32)] * 4 + [shaped(whole)]
+        operands += [*grads[index], weights[index], ones[index], twos[index]]
+        first += steps
+    results = pl.pallas_call(
+        functools.partial(adam_kernel, kinds),
+        grid=(first,),
+        in_specs=in_specs,
+        out_specs=out_specs,
+        out_shape=out_shape,
+        compiler_params=limits,
+        name="adam_update",
+    )(*operands)
+    return [results[index * 5 : index * 5 + 5] for index in range(len(kinds))]
 
 
 def gather_inputs(tokens, cotangent, w_qkv, w_out, w_up, w_down):
@@ -647,56 +1132,39 @@
     x_own, x_other, dy_own, dy_other, weights = gather_inputs(
         tokens, cotangent, w_qkv, w_out, w_up, w_down
     )
-    y, gx, g_qkv, g_out, g_up, g_down, g_ln = layer_local(
+    y, gx, totals = layer_local(
         x_own, x_other, dy_own, dy_other, lengths, ln_params, weights
     )
     output_rows = place_rows(y)
     grad_input = place_rows(gx)
-    halves = []
-    for grad in (g_qkv, g_out, g_up, g_down):
-        halves.append(grad[0].astype(f32) + swap_heads(grad[1]).astype(f32))
-    summed = [lax.psum(half.astype(bf16), "dp").astype(f32) for half in halves]
-    summed[0] = summed[0].transpose(1, 0, 2)
-    summed.append(lax.psum(g_ln, ("dp", "head")))
-    masters = (w_qkv, w_out, w_up, w_down, ln_params)
-    firsts = (m_qkv, m_out, m_up, m_down, m_ln)
-    seconds = (v_qkv, v_out, v_up, v_down, v_ln)
-    rates = (
-        float(D) ** (-0.5),
-        4.0 * float(D) ** (-0.5),
-        float(D) ** (-0.5),
-        float(FF) ** (-0.5),
-        0.7,
+    *pieces, t_ln = totals
+
+    def as_blocks(array):
+        return array.transpose(1, 0, 2)
+
+    results = adam_update(
+        (0, 1, 2, 3),
+        owners,
+        (
+            (pieces[5].reshape(2, 3, HALF, HALF),),
+            (pieces[4],),
+            (pieces[2], pieces[3]),
+            (pieces[0], pieces[1]),
+        ),
+        (as_blocks(w_qkv), w_out, w_up, w_down),
+        (as_blocks(m_qkv), m_out, m_up, m_down),
+        (as_blocks(v_qkv), v_out, v_up, v_down),
     )
-    updated = [
-        adam_step(
-            summed[kind_index],
-            masters[kind_index],
-            firsts[kind_index],
-            seconds[kind_index],
-            rates[kind_index],
-        )
-        for kind_index in range(5)
+    results[0] = [as_blocks(array) for array in results[0]]
+    mine = owners[4] == lax.axis_index("dp")
+    ln_results = adam_step(t_ln, ln_params, m_ln, v_ln, RATES[4])
+    results.append([jnp.where(mine, t_ln, 0.0), *ln_results])
+    owned, new, first, second = [
+        tuple(results[kind][slot] for kind in range(5)) for slot in range(4)
     ]
-    new_weights = tuple((entry[0] for entry in updated))
-    new_firsts = tuple((entry[1] for entry in updated))
-    new_seconds = tuple((entry[2] for entry in updated))
-    device_index = lax.axis_index("dp")
-    owned_grads = tuple(
-        (
-            jnp.where(owners[kind_index] == device_index, summed[kind_index], 0.0)[None]
-            for kind_index in range(5)
-        )
-    )
-    copies = tuple((new_weights[kind_index].astype(jnp.bfloat16) for kind_index in range(4)))
-    return (
-        (output_rows, grad_input)
-        + owned_grads
-        + tuple(new_weights)
-        + tuple(new_firsts)
-        + tuple(new_seconds)
-        + copies
-    )
+    copies = tuple(results[kind][4] for kind in range(4))
+    owned = tuple(array[None] for array in owned)
+    return (output_rows, grad_input) + owned + new + first + second + copies
 
 
 PLACED = (

time: 324 us -> 215 us (0.66)
  waiting for transfers between devices: 98 us -> 0.02 us
  Pallas kernels: 114 us -> 195 us
  blocking collectives: 44.7 us -> 0 us
  other arithmetic: 33.6 us -> 8.6 us
  between operations: 17.6 us -> 1.54 us
  local copies, waits for them, and re-layouts: 11.1 us -> 6.51 us
    psum x1 -> x0, waiting for transfers between devices: 95.8 us -> none  [body(): summed = [lax.psum(half.astype(bf16), 'dp').astype(f32) for half in halves]]
    pallas_call x1 -> x2, Pallas kernels: 36.5 us -> 118 us  [the longest x1 95 us: layer_local(): pl.pallas_call(functools.partial(backward_attention, count), grid=(TILES,...]
    psum x1 -> x0, blocking collectives: 44.7 us -> none  [body(): summed.append(lax.psum(g_ln, ('dp', 'head')))]
    convert_element_type x7 -> x0, other arithmetic: 23.6 us -> none  [the longest x4 20.1 us: body(): new_weights[kind_index].astype(jnp.bfloat16)]
  transfers between devices with their start and end apart: 13 -> 8, of which waited for: 2 -> 0; matrix products, arithmetic and copies ran while one was open for 5% -> 4% of each run, Pallas kernels for 9% -> 68%
where the time goes in v3:
time: 215 us; the launch traced here: 214 us
  Pallas kernels  195 us (91%)
  other arithmetic  8.6 us (4%)
  local copies, waits for them, and re-layouts  6.51 us (3%)
    pallas_call x1, Pallas kernels, layer_local(): pl.pallas_call(functools.partial(backward_attention, count), grid=(TILES,...  95 us
    pallas_call x1, Pallas kernels, layer_local(): pl.pallas_call(mlp_both_ways, grid=(TILES,), in_specs=[smem_spec, rows_sp...  49.6 us
    pallas_call x1, Pallas kernels, layer_local(): pl.pallas_call(forward_attention, grid=(TILES,), in_specs=[smem_spec, row...  27.9 us
    pallas_call x1, Pallas kernels, adam_update(): pl.pallas_call(functools.partial(adam_kernel, kinds), grid=(first,), in_s...  22.8 us
  transfers between devices with their start and end apart: 8, of which 0 were waited for; matrix products, arithmetic and copies ran while one was open for 4% of the time, Pallas kernels for 68%

profile of v3, /device:TPU:0, one launch (start us, length us, event | category | flops | bytes accessed | tf_op | source)
XLA Modules:
  0.0 214.0 jit_solution(17263553779577295493)
XLA Ops:
  0.7 0.0 copy-start.2
  0.7 2.5 %bitcast_convert_fusion.w_own = bf16[3,512,256]{2,1,0:T(8,128)(2,1)} fusion(f32[512,3,256]{2,0,1:T(8,128)} %param.25), kind=kLoop, calls=%fused_computation.15 | loop fusion | flops 393216 | bytes 2359296 | tf_op jit(solution)/shard_map/convert_element_type | solution.py:1083
  3.2 0.5 collective-permute-start.2
  3.7 1.1 convert_element_type.15.down_own
  4.8 0.1 collective-permute-start.5
  4.8 0.0 copy-done.1
  4.8 1.1 convert_element_type.14.up_own
  6.0 0.8 collective-permute-start.4
  6.7 0.0 copy-done.3
  6.7 1.1 dynamic-slice_bitcast_fusion.2
  7.9 0.0 collective-permute-start
  7.9 0.9 copy-done.4
  8.7 1.5 dynamic-slice_bitcast_fusion
  10.2 0.0 collective-permute-start.1
  10.2 0.0 copy-start.10
  10.2 0.0 collective-permute-done.2.w_other
  10.2 0.6 collective-permute-start.3
  10.8 0.0 collective-permute-done.x_other
  10.8 1.0 copy-done
  11.8 27.9 %forward_attention.1 = (bf16[2048,1536]{1,0:T(8,128)(2,1)}, bf16[2048,1024]{1,0:T(8,128)(2,1)}, bf16[64,256,256]{2,1,0:T(8,128)(2,1)}, bf16[2048,512]{1,0:T(8,128)(2,1)}) custom-call(f32[2,16]{1,0:T(2,128)} %constant.41.clone.table, bf16[2048,256]{1,0:T(8,128)(2,1)} %get-tuple-element.118.x_own, bf16[2048,256]{1,0:T(8,128)(2,1)} %copy-done, f32[4,512]{1,0:T(4,128)} %ln.5, ...), custom_call_target="tpu_custom_call" | custom-call | tf_op jit(solution)/shard_map/forward_attention/pallas_call | solution.py:789
  39.6 0.0 collective-permute-done.3.out_other
  39.6 0.0 copy-start.11
  39.7 0.0 collective-permute-done.5.down_other
  39.7 0.0 copy-start.7
  39.7 0.0 collective-permute-done.4.up_other
  39.7 0.0 collective-permute-done.1.dy_other
  39.7 0.0 copy-start.9
  39.7 0.6 copy-done.11
  40.4 0.4 copy-done.7
  40.7 0.3 copy-done.9
  41.1 49.6 %mlp_both_ways.1 = (bf16[2048,256]{1,0:T(8,128)(2,1)}, bf16[2048,256]{1,0:T(8,128)(2,1)}, f32[2048,512]{1,0:T(8,128)}, bf16[2048,512]{1,0:T(8,128)(2,1)}, bf16[2...) custom-call(s32[2]{0:T(128)} %lengths.1, ...), custom_call_target="tpu_custom_call" | custom-call | tf_op jit(solution)/shard_map/mlp_both_ways/pallas_call | solution.py:812
  90.7 0.1 collective-permute-start.6
  90.8 0.6 slice.3
  92.1 95.0 %backward_attention.1 = (bf16[2048,256]{1,0:T(8,128)(2,1)}, bf16[2048,256]{1,0:T(8,128)(2,1)}, bf16[2,512,256]{2,1,0:T(8,128)(2,1)}, bf16[2,512,256]{2,1,0:T(8,1...) custom-call(f32[2,16]{1,0:T(2,128)} %constant.41.clone.table, ...), custom_call_target="tpu_custom_call" | custom-call | tf_op jit(solution)/shard_map/backward_attention/pallas_call | solution.py:899
  187.0 0.1 collective-permute-start.7
  187.1 0.0 copy-start.12
  187.1 0.0 copy-start.13
  187.2 0.0 copy-start.14
  187.2 0.0 copy-start.6
  187.2 22.8 %adam_update.1 = (f32[3,512,256]{2,1,0:T(8,128)}, f32[3,512,256]{2,1,0:T(8,128)}, f32[3,512,256]{2,1,0:T(8,128)}, f32[3,512,256]{2,1,0:T(8,128)}, bf16[3,512,256...) custom-call(s32[5]{0:T(128)} %owners.1, ...), custom_call_target="tpu_custom_call" | custom-call | tf_op jit(solution)/shard_map/adam_update/pallas_call | solution.py:1061
  210.0 0.6 multiply_subtract_fusion
  210.7 0.0 collective-permute-done.6
  210.7 0.1 broadcast_select_fusion.3
  210.8 1.5 pad_maximum_fusion
  212.3 0.0 collective-permute-done.7
  212.3 0.1 copy-done.8
  212.4 0.1 broadcast_select_fusion.1
  212.6 1.5 pad_maximum_fusion.1
  (18 shorter events, 0.1 us)
Async XLA Ops:
  0.7 3.0 %copy-start.2 = (f32[1024,512]{1,0:T(8,128)S(1)}, f32[1024,512]{1,0:T(8,128)}, u32[]{:S(2)}) copy-start(f32[1024,512]{1,0:T(8,128)} %refs_15_.1) | copy-start | bytes 6291460
  3.2 1.6 copy-start.1
  3.2 7.0 %collective-permute-start.2 = (bf16[3,512,256]{2,1,0:T(8,128)(2,1)}, bf16[3,512,256]{2,1,0:T(8,128)(2,1)}, u32[]{:S(2)}, u32[]{:S(2)}) collective-permute-start(bf16[3,512,256]{2,1,0:T(8,128)(2,1)} %bitcast_convert_fusion.w_own), channel_id=1, source_target_pairs={{0,1},{1,0},{2,3},{3,2},{4,5},{5,4},{6,7},{7,6},{8,9},{9,8},{10,11... | collective-permute-start | bytes 2359304 | tf_op jit(solution)/shard_map/ppermute | solution.py:291
  4.8 2.0 copy-start.3
  4.8 34.9 %collective-permute-start.5 = (bf16[1024,512]{1,0:T(8,128)(2,1)}, bf16[1024,512]{1,0:T(8,128)(2,1)S(1)}, u32[]{:S(2)}, u32[]{:S(2)}) collective-permute-start(bf16[1024,512]{1,0:T(8,128)(2,1)} %convert_element_type.15.down_own), channel_id=1, source_target_pairs={{0,1},{1,0},{2,3},{3,2},{4,5},{5,4},{6,7},{7,6},{8,9},{9,8},{10,11... | collective-permute-start | bytes 3145736 | tf_op jit(solution)/shard_map/ppermute | solution.py:291
  6.0 33.7 %collective-permute-start.4 = (bf16[512,1024]{1,0:T(8,128)(2,1)}, bf16[512,1024]{1,0:T(8,128)(2,1)}, u32[]{:S(2)}, u32[]{:S(2)}) collective-permute-start(bf16[512,1024]{1,0:T(8,128)(2,1)} %convert_element_type.14.up_own), channel_id=1, source_target_pairs={{0,1},{1,0},{2,3},{3,2},{4,5},{5,4},{6,7},{7,6},{8,9},{9,8},{10,11... | collective-permute-start | bytes 3145736 | tf_op jit(solution)/shard_map/ppermute | solution.py:291
  6.7 2.0 copy-start.4
  7.9 3.0 %collective-permute-start = (bf16[2048,256]{1,0:T(8,128)(2,1)S(1)}, bf16[2048,256]{1,0:T(8,128)(2,1)S(1)}, u32[]{:S(2)}, u32[]{:S(2)}) collective-permute-start(bf16[2048,256]{1,0:T(8,128)(2,1)S(1)} %get-tuple-element.117), channel_id=1, source_target_pairs={{0,1},{1,0},{2,3},{3,2},{4,5},{5,4},{6,7},{7,6},{8,9},{9,8},{10,11... | collective-permute-start | bytes 3145736 | tf_op jit(solution)/shard_map/ppermute | solution.py:291
  8.7 1.5 copy-start.5
  10.2 29.5 %collective-permute-start.1 = (bf16[2048,256]{1,0:T(8,128)(2,1)}, bf16[2048,256]{1,0:T(8,128)(2,1)S(1)}, u32[]{:S(2)}, u32[]{:S(2)}) collective-permute-start(bf16[2048,256]{1,0:T(8,128)(2,1)} %get-tuple-element.115), channel_id=1, source_target_pairs={{0,1},{1,0},{2,3},{3,2},{4,5},{5,4},{6,7},{7,6},{8,9},{9,8},{10,11... | collective-permute-start | bytes 3145736 | tf_op jit(solution)/shard_map/ppermute | solution.py:291
  10.2 29.5 %copy-start.10 = (bf16[256,512]{1,0:T(8,128)(2,1)}, bf16[256,512]{1,0:T(8,128)(2,1)S(1)}, u32[]{:S(2)}) copy-start(bf16[256,512]{1,0:T(8,128)(2,1)S(1)} %convert_element_type.13.out_own) | copy-start | bytes 786436
  10.2 29.4 %collective-permute-start.3 = (bf16[256,512]{1,0:T(8,128)(2,1)S(1)}, bf16[256,512]{1,0:T(8,128)(2,1)S(1)}, u32[]{:S(2)}, u32[]{:S(2)}) collective-permute-start(bf16[256,512]{1,0:T(8,128)(2,1)S(1)} %convert_element_type.13.out_own), channel_id=1, source_target_pairs={{0,1},{1,0},{2,3},{3,2},{4,5},{5,4},{6,7},{7,6},{8,9},{9,8},{10,11... | collective-permute-start | bytes 786440 | tf_op jit(solution)/shard_map/ppermute | solution.py:291
  10.8 1.0 copy-start
  39.6 0.7 copy-start.11
  39.7 1.0 copy-start.7
  39.7 1.3 copy-start.9
  41.1 49.8 %copy-start.16 = (s32[5]{0:T(128)S(1)}, s32[5]{0:T(128)}, u32[]{:S(2)}) copy-start(s32[5]{0:T(128)} %owners.1) | copy-start | bytes 64
  90.7 120.0 %collective-permute-start.6 = (bf16[2048,256]{1,0:T(8,128)(2,1)}, bf16[2048,256]{1,0:T(8,128)(2,1)S(1)}, u32[]{:S(2)}, u32[]{:S(2)}) collective-permute-start(bf16[2048,256]{1,0:T(8,128)(2,1)} %get-tuple-element.69), channel_id=1, source_target_pairs={{0,1},{1,0},{2,3},{3,2},{4,5},{5,4},{6,7},{7,6},{8,9},{9,8},{10,11... | collective-permute-start | bytes 3145736 | tf_op jit(solution)/shard_map/ppermute | solution.py:291
  187.0 25.2 %collective-permute-start.7 = (bf16[2048,256]{1,0:T(8,128)(2,1)}, bf16[2048,256]{1,0:T(8,128)(2,1)S(1)}, u32[]{:S(2)}, u32[]{:S(2)}) collective-permute-start(bf16[2048,256]{1,0:T(8,128)(2,1)} %get-tuple-element.80), channel_id=1, source_target_pairs={{0,1},{1,0},{2,3},{3,2},{4,5},{5,4},{6,7},{7,6},{8,9},{9,8},{10,11... | collective-permute-start | bytes 3145736 | tf_op jit(solution)/shard_map/ppermute | solution.py:291
  187.1 22.9 %copy-start.12 = (f32[4,512]{1,0:T(4,128)S(1)}, f32[4,512]{1,0:T(4,128)}, u32[]{:S(2)}) copy-start(f32[4,512]{1,0:T(4,128)} %ln.5) | copy-start | bytes 24580
  187.1 22.9 %copy-start.13 = (f32[4,512]{1,0:T(4,128)S(1)}, f32[4,512]{1,0:T(4,128)}, u32[]{:S(2)}) copy-start(f32[4,512]{1,0:T(4,128)} %param.34) | copy-start | bytes 24580
  187.2 22.9 %copy-start.14 = (f32[4,512]{1,0:T(4,128)S(1)}, f32[4,512]{1,0:T(4,128)}, u32[]{:S(2)}) copy-start(f32[4,512]{1,0:T(4,128)} %param.39) | copy-start | bytes 24580
  187.2 22.9 %copy-start.15 = (f32[4,512]{1,0:T(4,128)S(1)}, f32[4,512]{1,0:T(4,128)}, u32[]{:S(2)}) copy-start(f32[4,512]{1,0:T(4,128)} %get-tuple-element.91) | copy-start | bytes 24580
  187.2 23.5 %copy-start.6 = (bf16[2048,256]{1,0:T(8,128)(2,1)S(1)}, bf16[2048,256]{1,0:T(8,128)(2,1)}, u32[]{:S(2)}) copy-start(bf16[2048,256]{1,0:T(8,128)(2,1)} %get-tuple-element.68) | copy-start | bytes 3145732
  210.8 1.6 copy-start.8

commit v4 on v3

v4 whole, which is shorter than its diff:
```python
import functools

import jax
import jax.numpy as jnp
import numpy as np
from jax import lax
from jax.experimental import pallas as pl
from jax.experimental.pallas import tpu as pltpu
from jax.sharding import PartitionSpec as P

D = 512
HALF = 256
HEAD_DIM = 64
FF = 2048
SPAN = 128
SEQ = 2048
STEP = 5
ROWS = 16
PAIRS = 4
TILE = 512
TILES = SEQ // TILE
SPANS_TILE = TILE // SPAN

epsilon_norm = 1e-05
epsilon_adam = 1e-08
beta_one = 0.5
beta_two = 0.5
decay_rate = 0.1
masked_score = -1e30

bf16 = jnp.bfloat16
f32 = jnp.float32

NN = (((1,), (0,)), ((), ()))
NT = (((1,), (1,)), ((), ()))
TN = (((0,), (0,)), ((), ()))


def mm(left, right, dims=NN):
    return lax.dot_general(left, right, dims, preferred_element_type=f32)


def join_columns(head, own, other):
    low = jnp.where(head == 0, own, other)
    high = jnp.where(head == 0, other, own)
    return jnp.concatenate([low, high], axis=1)


def norm_stats(values):
    mean = jnp.mean(values, axis=1, keepdims=True)
    centered = values - mean
    rstd = lax.rsqrt(jnp.mean(centered * centered, axis=1, keepdims=True) + epsilon_norm)
    return centered * rstd, rstd


def head_stack(pair, low_lanes, high_lanes):
    return jnp.concatenate([pair * low_lanes, pair * high_lanes], axis=0)


def lane_masks(dtype):
    lane = lax.broadcasted_iota(jnp.int32, (1, 2 * HEAD_DIM), 1)
    low = (lane < HEAD_DIM).astype(f32)
    return low.astype(dtype), (1.0 - low).astype(dtype)


def pair_columns(pair):
    base = 3 * HALF * (pair // 2) + 2 * HEAD_DIM * (pair % 2)
    return base, base + HALF, base + 2 * HALF


def unstack_transposed(product):
    joined = jnp.concatenate(
        [product[:HEAD_DIM, :SPAN], product[HEAD_DIM:, SPAN:]], axis=0
    )
    return joined.T


def forward_attention(
    table, x_own, x_other, ln, w_own, w_other, causal, qkv, bars, probs, ctx, run_sum, normed
):
    head = lax.axis_index("head")
    step = pl.program_id(0)

    @pl.when(step == 0)
    def _():
        run_sum[...] = jnp.zeros_like(run_sum)

    for row in range(0, TILE, 128):
        rows = pl.ds(row, 128)
        x = join_columns(head, x_own[rows, :].astype(f32), x_other[rows, :].astype(f32))
        xhat, _ = norm_stats(x)
        normed[rows, :] = (xhat * ln[0:1, :] + ln[1:2, :]).astype(bf16)
    for side, w in enumerate((w_own, w_other)):
        for part in range(3):
            value = mm(normed[...], w[part])
            if part == 0:
                value = value * float(HEAD_DIM) ** (-0.5)
            base = side * 3 * HALF + part * HALF
            qkv[:, base : base + HALF] = value.astype(bf16)
    low_lanes, high_lanes = lane_masks(bf16)

    def score_span(span):
        rows = pl.ds(span * SPAN, SPAN)
        row_id = step * SPANS_TILE + span
        inverse = table[0, row_id]
        shift = table[1, row_id]
        scores, stacked = [], []
        for pair in range(PAIRS):
            at_q, at_k, at_v = pair_columns(pair)
            lanes = pl.ds(pair * 128, 128)
            lanes_v = pl.ds(512 + pair * 128, 128)
            key = qkv[rows, at_k : at_k + 128]
            value = qkv[rows, at_v : at_v + 128]
            key_bar = (run_sum[:, lanes] * inverse).astype(bf16)
            value_bar = (run_sum[:, lanes_v] * inverse).astype(bf16)
            run_sum[:, lanes] += key.astype(f32)
            run_sum[:, lanes_v] += value.astype(f32)
            bars[rows, lanes] = key_bar
            bars[rows, lanes_v] = value_bar
            query = head_stack(qkv[rows, at_q : at_q + 128], low_lanes, high_lanes)
            scores.append((mm(key, query, NT) + causal[...], mm(key_bar, query, NT) + shift))
            stacked.append(jnp.concatenate([value, value_bar], axis=0))
        return scores, stacked

    def soft_span(span, scores):
        expo = []
        for direct, summary in scores:
            top = jnp.maximum(
                jnp.max(direct, axis=0, keepdims=True), jnp.max(summary, axis=0, keepdims=True)
            )
            expo.append((jnp.exp(direct - top), jnp.exp(summary - top)))
        both = []
        for pair, (direct, summary) in enumerate(expo):
            total = jnp.sum(direct, axis=0, keepdims=True) + jnp.sum(
                summary, axis=0, keepdims=True
            )
            scale = 1.0 / total
            prob = jnp.concatenate(
                [(direct * scale).astype(bf16), (summary * scale).astype(bf16)], axis=0
            )
            probs[span * PAIRS + pair] = prob
            both.append(prob)
        return both

    def context_span(span, stacked, both):
        rows = pl.ds(span * SPAN, SPAN)
        for pair in range(PAIRS):
            lanes = pl.ds(pair * 128, 128)
            ctx[rows, lanes] = unstack_transposed(mm(stacked[pair], both[pair], TN)).astype(bf16)

    ready = score_span(0)
    for span in range(SPANS_TILE):
        scores, stacked = ready
        if span + 1 < SPANS_TILE:
            ready = score_span(span + 1)
        both = soft_span(span, scores)
        context_span(span, stacked, both)


def gelu_parts(u):
    share = lax.erf(u * 0.7071067811865476) * 0.5 + 0.5
    bell = jnp.exp2((u * u) * -0.7213475204444817)
    return u * share, share + u * bell * 0.3989422804014327


def swap_heads(value):
    return lax.ppermute(value, "head", [(0, 1), (1, 0)])


def chip_grid(count):
    side = 1 << ((count.bit_length() - 1) // 3)
    return (count // (side * side), side, side)


class Lines:
    def __init__(self, count):
        self.sizes = chip_grid(count)
        self.strides = (self.sizes[1] * self.sizes[2], self.sizes[2], 1)
        self.chip = lax.axis_index("dp")
        self.head = lax.axis_index("head")
        self.places = [
            lax.rem(self.chip // stride, size) for stride, size in zip(self.strides, self.sizes)
        ]
        self.members = [
            [self.find(axis, ahead) for ahead in range(1, size)]
            for axis, size in enumerate(self.sizes)
        ]

    def partner(self):
        return (self.chip, 1 - self.head)

    def member(self, axis, ahead):
        return self.members[axis][ahead - 1]

    def find(self, axis, ahead):
        size = self.sizes[axis]
        place = 1 - self.places[axis]
        if size > 2:
            place = lax.rem(self.places[axis] + ahead, size)
        chip = self.chip + (place - self.places[axis]) * self.strides[axis]
        return place, (chip, self.head)

    def greet(self):
        barrier = pltpu.get_barrier_semaphore()
        others = [self.partner()]
        for axis in range(3):
            others += [self.member(axis, ahead)[1] for ahead in range(1, self.sizes[axis])]
        for other in others:
            pl.semaphore_signal(
                barrier, inc=1, device_id=other, device_id_type=pl.DeviceIdType.MESH
            )
        pl.semaphore_wait(barrier, len(others))


X_FIRST, Y_FIRST = (2, 1, 0), (1, 2, 0)


def whole_slices(count):
    return all(shape[1] % (16 * count) == 0 for shape, _ in PIECES)


def chunk_rows(rows):
    return next(chunk for chunk in (128, 96, 64, 48, 32, 16) if rows % chunk == 0)


def sum_scratch(shape, orders, count):
    parts, rows, lanes = shape
    sizes = chip_grid(count)
    shapes = [pltpu.VMEM(shape, bf16)]
    sems = [pltpu.SemaphoreType.DMA((3,))]
    for order in orders:
        left = rows
        for axis in order:
            left //= sizes[axis]
            shapes.append(pltpu.VMEM((sizes[axis] - 1, left, lanes), bf16))
            sems.append(pltpu.SemaphoreType.DMA((2, 2, sizes[axis] - 1)))
    return shapes + sems


class DpSum:
    def __init__(self, lines, orders, grads, total, scratch):
        self.lines = lines
        self.orders = orders
        self.parts = range(len(orders))
        self.grads = grads
        self.total = total
        self.rows = grads.shape[2]
        self.work, self.final = grads.at[0], scratch.pop(0)
        self.slots = [[scratch.pop(0) for _ in order] for order in orders]
        self.core_sem = scratch.pop(0)
        self.sems = [[scratch.pop(0) for _ in order] for order in orders]
        self.base = []
        for order in orders:
            bases, piece = [0], self.rows
            for axis in order:
                piece //= lines.sizes[axis]
                bases.append(bases[-1] + lines.places[axis] * piece)
            self.base.append(bases)

    def remote(self, source, target, send_sem, recv_sem, device):
        return pltpu.make_async_remote_copy(
            src_ref=source,
            dst_ref=target,
            send_sem=send_sem,
            recv_sem=recv_sem,
            device_id=device,
            device_id_type=pl.DeviceIdType.MESH,
        )

    def core_copy(self):
        return self.remote(
            self.grads.at[1],
            self.final,
            self.core_sem.at[0],
            self.core_sem.at[1],
            self.lines.partner(),
        )

    def core_send(self):
        self.core_copy().start()

    def core_sum(self):
        self.core_copy().wait()
        chunk = chunk_rows(self.rows)
        for part in self.parts:

            def add(index, carry, part=part):
                rows = pl.ds(pl.multiple_of(index * chunk, chunk), chunk)
                self.work[part, rows, :] = self.work[part, rows, :] + self.final[part, rows, :]
                return carry

            lax.fori_loop(0, self.rows // chunk, add, 0)

    def spread_copies(self, part, stage):
        axis = self.orders[part][stage]
        size = self.lines.sizes[axis]
        base = self.base[part][stage]
        piece = self.rows
        for at in self.orders[part][: stage + 1]:
            piece //= self.lines.sizes[at]
        copies = []
        for ahead in range(1, size):
            place, device = self.lines.member(axis, ahead)
            start = pl.multiple_of(base + place * piece, 16)
            copies.append(
                self.remote(
                    self.work.at[part, pl.ds(start, piece)],
                    self.slots[part][stage].at[ahead - 1],
                    self.sems[part][stage].at[0, 0, ahead - 1],
                    self.sems[part][stage].at[0, 1, ahead - 1],
                    device,
                )
            )
        return copies, self.base[part][stage + 1], piece

    def spread_send(self, part, stage):
        for copy in self.spread_copies(part, stage)[0]:
            copy.start()

    def spread_sum(self, part, stage):
        copies, mine, piece = self.spread_copies(part, stage)
        for copy in copies:
            copy.wait()
        slots = self.slots[part][stage]
        target = self.final if stage == 2 else self.work
        chunk = chunk_rows(piece)

        def add(index, carry):
            offset = pl.multiple_of(index * chunk, chunk)
            rows = pl.ds(pl.multiple_of(mine + offset, 16), chunk)
            value = self.work[part, rows, :]
            if len(copies) > 1:
                value = value.astype(f32)
            for slot in range(len(copies)):
                value = value + slots[slot, pl.ds(offset, chunk), :].astype(value.dtype)
            target[part, rows, :] = value.astype(bf16)
            return carry

        lax.fori_loop(0, piece // chunk, add, 0)

    def gather_copies(self, part, stage):
        axis = self.orders[part][stage]
        size = self.lines.sizes[axis]
        piece = self.rows
        for at in self.orders[part][: stage + 1]:
            piece //= self.lines.sizes[at]
        mine = pl.multiple_of(self.base[part][stage + 1], 16)
        rows = pl.ds(mine, piece)
        copies = []
        for ahead in range(1, size):
            _, device = self.lines.member(axis, ahead)
            copies.append(
                self.remote(
                    self.final.at[part, rows],
                    self.final.at[part, rows],
                    self.sems[part][stage].at[1, 0, ahead - 1],
                    self.sems[part][stage].at[1, 1, ahead - 1],
                    device,
                )
            )
        return copies

    def gather_send(self, part, stage):
        for copy in self.gather_copies(part, stage):
            copy.start()

    def gather_wait(self, part, stage):
        for copy in self.gather_copies(part, stage):
            copy.wait()

    def store_copy(self):
        return pltpu.make_async_copy(self.final, self.total, self.core_sem.at[2])

    def event(self, index):
        if index == 0:
            self.core_send()
        elif index == 1:
            self.core_sum()
        for part in self.parts:
            if 2 <= index <= 4:
                self.spread_sum(part, index - 2)
            elif index >= 5:
                self.gather_wait(part, 7 - index)
            if 1 <= index <= 3:
                self.spread_send(part, index - 1)
            elif 4 <= index <= 6:
                self.gather_send(part, 6 - index)
        if index == 7:
            self.store_copy().start()

    def finish(self):
        self.store_copy().wait()


EVENTS = 8


def ln_scratch(count):
    return [
        pltpu.VMEM((2, 4, D), f32),
        pltpu.SemaphoreType.DMA((2,)),
        *[pltpu.VMEM((size, 4, D), f32) for size in chip_grid(count)],
        *[pltpu.SemaphoreType.DMA((2, max(size - 1, 1))) for size in chip_grid(count)],
    ]


class LnSum:
    def __init__(self, lines, value, total, scratch):
        self.lines = lines
        self.value = value
        self.total = total
        self.core, self.core_sem = scratch[:2]
        self.slots = scratch[2:5]
        self.sems = scratch[5:8]

    def stage_copies(self, stage):
        lines = self.lines
        if stage == 0:
            mine = self.core.at[lines.head]
            return [
                pltpu.make_async_remote_copy(
                    src_ref=mine,
                    dst_ref=mine,
                    send_sem=self.core_sem.at[0],
                    recv_sem=self.core_sem.at[1],
                    device_id=lines.partner(),
                    device_id_type=pl.DeviceIdType.MESH,
                )
            ]
        axis = stage - 1
        mine = self.slots[axis].at[lines.places[axis]]
        return [
            pltpu.make_async_remote_copy(
                src_ref=mine,
                dst_ref=mine,
                send_sem=self.sems[axis].at[0, ahead - 1],
                recv_sem=self.sems[axis].at[1, ahead - 1],
                device_id=lines.member(axis, ahead)[1],
                device_id_type=pl.DeviceIdType.MESH,
            )
            for ahead in range(1, lines.sizes[axis])
        ]

    def send(self, stage):
        if stage == 0:
            self.core[self.lines.head] = self.value[...]
        for copy in self.stage_copies(stage):
            copy.start()

    def finish(self, stage):
        for copy in self.stage_copies(stage):
            copy.wait()
        slots = self.core if stage == 0 else self.slots[stage - 1]
        value = slots[0]
        for slot in range(1, slots.shape[0]):
            value = value + slots[slot]
        if stage == 3:
            self.total[...] = value
        else:
            self.slots[stage][self.lines.places[stage]] = value


PIECES = (
    ((2, 1024, HALF), (X_FIRST, Y_FIRST)),
    ((2, 1024, HALF), (X_FIRST, Y_FIRST)),
    ((1, HALF, D), (Y_FIRST,)),
    ((2, 3 * HALF, HALF), (X_FIRST, Y_FIRST)),
)
CHUNKS = FF // 512
CHUNK_STEP = TILES
POST_STEP = CHUNK_STEP + CHUNKS
ATT_STEP = POST_STEP + TILES
SPANS_STEP = 2
ATT_STEPS = ROWS // SPANS_STEP
LAST_STEP = ATT_STEP + ATT_STEPS
STEPS = LAST_STEP + TILES
EVENT_AT = (
    ((6, 0), (6, 1), (7, 1), (8, 0), (12, 0), (14, 0), (16, 0), (18, 0)),
    ((8, 0), (9, 0), (13, 0), (15, 0), (17, 0), (19, 0), (21, 0), (23, 0)),
    ((12, 0), (13, 0), (15, 0), (16, 0), (18, 0), (20, 0), (21, 0), (23, 0)),
    ((20, 0), (21, 0), (23, 0)),
)


def mlp_and_back(
    count,
    table,
    lengths,
    ln,
    x_own_at,
    x_other_at,
    dy_own_at,
    dy_other_at,
    ctx_at,
    qkv_at,
    bars_at,
    probs_at,
    out_own_at,
    out_other_at,
    w_own_at,
    w_other_at,
    up_own,
    up_other,
    down_own,
    down_other,
    y_own_at,
    y_other_at,
    gx_own_at,
    gx_other_at,
    *refs,
):
    summing = whole_slices(count)
    kinds = len(PIECES)
    totals, ln_total = refs[:kinds], refs[kinds]
    (x_own, x_other, dy_own, dy_other, ctx, qkv_two, bars_two, probs_two, out_own, out_other,
     w_own, w_other, up_all, down_all, load_sem, weight_sem, block_sem, store_sem, res, grad_qkv,
     normed_t, gm, mlp, grad_n, acc_one, acc_two, hid, grad_hid, after,
     acc_ln) = refs[kinds + 1 : kinds + 31]
    grads = refs[kinds + 31 : kinds + 31 + len(PIECES)]
    scratch = list(refs[kinds + 31 + len(PIECES) :])
    head = lax.axis_index("head")
    used = lengths[head]
    sums = []
    if summing:
        lines = Lines(count)
        for (_, orders), grad, total in zip(PIECES, grads, totals):
            sums.append(DpSum(lines, orders, grad, total, scratch))
        small = LnSum(lines, acc_ln, ln_total, scratch)

    def run_events(events):
        for index, event in events:
            sums[index].event(event)

    def hook(step, first, end, place=0):
        for at in range(first, end if summing else 0):
            events = [
                (index, event)
                for index, times in enumerate(EVENT_AT)
                for event, time in enumerate(times)
                if time == (at, place)
            ]
            if events:

                @pl.when(step == at)
                def _(events=events):
                    run_events(events)

    loads = [
        pltpu.make_async_copy(source, target, load_sem.at[index])
        for index, (source, target) in enumerate(
            (
                (ctx_at, ctx),
                (out_own_at, out_own),
                (out_other_at, out_other),
                (x_own_at, x_own),
                (x_other_at, x_other),
                (dy_own_at, dy_own),
                (dy_other_at, dy_other),
                (w_own_at, w_own),
                (w_other_at, w_other),
            )
        )
    ]
    weight_copies = []
    for chunk in range(CHUNKS):
        up_w, down_w = ((up_own, down_own), (up_other, down_other))[chunk % 2]
        cut = pl.ds(chunk // 2 * 512, 512)
        pairs = ((up_w.at[:, cut], up_all.at[chunk]), (down_w.at[cut], down_all.at[chunk]))
        for which, (source, target) in enumerate(pairs):
            sem = weight_sem.at[2 * chunk + which]
            weight_copies.append(pltpu.make_async_copy(source, target, sem))
    block_rows = SPANS_STEP * SPAN
    block_probs = SPANS_STEP * PAIRS

    def block_copies(index):
        block = ATT_STEPS - 1 - index
        slot = lax.rem(index, 2)
        rows = pl.ds(block * block_rows, block_rows)
        many = pl.ds(block * block_probs, block_probs)
        pairs = (
            (qkv_at.at[rows], qkv_two.at[slot]),
            (bars_at.at[rows], bars_two.at[slot]),
            (probs_at.at[many], probs_two.at[slot]),
        )
        return [
            pltpu.make_async_copy(source, target, block_sem.at[slot, which])
            for which, (source, target) in enumerate(pairs)
        ]

    stores = [
        pltpu.make_async_copy(source, target, store_sem.at[index])
        for index, (source, target) in enumerate(
            (
                (ctx.at[:, pl.ds(0, HALF)], y_own_at),
                (ctx.at[:, pl.ds(HALF, HALF)], y_other_at),
                (dy_own, gx_own_at),
                (dy_other, gx_other_at),
            )
        )
    ]

    def x_rows(rows):
        return join_columns(head, x_own[rows, :].astype(f32), x_other[rows, :].astype(f32))

    def dy_rows(rows):
        return join_columns(head, dy_own[rows, :].astype(f32), dy_other[rows, :].astype(f32))

    def valid_rows(first):
        ids = lax.broadcasted_iota(jnp.int32, (128, 1), 0) + first
        return (ids < used).astype(f32)

    def before_mlp(tile, carry):
        base = tile * TILE
        tokens = pl.ds(pl.multiple_of(base, TILE), TILE)
        res[tokens, :] = mm(ctx[tokens, :HALF], out_own[...]) + mm(
            ctx[tokens, HALF:], out_other[...]
        )
        mlp[tokens, :] = jnp.zeros((TILE, D), f32)
        grad_n[tokens, :] = jnp.zeros((TILE, D), f32)
        for row in range(0, TILE, 128):
            at = pl.ds(pl.multiple_of(base + row, 128), 128)
            valid = valid_rows(base + row)
            h = x_rows(at) + valid * res[at, :]
            res[at, :] = h
            hat, _ = norm_stats(h)
            n2 = (hat * ln[2:3, :] + ln[3:4, :]).astype(bf16)
            grad_qkv[at, :D] = n2
            normed_t[:, at] = n2.T
            gm[at, :] = (valid * dy_rows(at)).astype(bf16)
        return carry

    def chunk_in(chunk, tile):
        tokens = pl.ds(tile * TILE, TILE)
        hid[tile % 2] = mm(grad_qkv[tokens, :D], up_all[chunk])
        grad_hid[tile % 2] = mm(gm[tokens, :], down_all[chunk], NT)

    def act_rows(tile, row, size):
        return pl.ds(tile % 2 * TILE + row, size), pl.ds((2 + tile % 2) * TILE + row, size)

    def chunk_mid(tile):
        slot = tile % 2
        for row in range(0, TILE, 16):
            rows = pl.ds(row, 16)
            a, da = gelu_parts(hid[slot, rows, :])
            at_act, at_gu = act_rows(tile, row, 16)
            grad_qkv[at_act, D : 2 * D] = a.astype(bf16)
            grad_qkv[at_gu, D : 2 * D] = (grad_hid[slot, rows, :] * da).astype(bf16)

    def chunk_out(chunk, tile):
        tokens = pl.ds(tile * TILE, TILE)
        at_act, at_gu = act_rows(tile, 0, TILE)
        act = grad_qkv[at_act, D : 2 * D]
        gu = grad_qkv[at_gu, D : 2 * D]
        mlp[tokens, :] += mm(act, down_all[chunk])
        grad_n[tokens, :] += mm(gu, up_all[chunk], NT)
        part_down = mm(act, gm[tokens, :], TN)
        part_up = mm(normed_t[:, tokens], gu)
        if tile == 0:
            acc_one[...] = part_down
            acc_two[...] = part_up
        else:
            acc_one[...] += part_down
            acc_two[...] += part_up

    def chunk_tiles(chunk, first):
        chunk_in(chunk, first)
        chunk_in(chunk, first + 1)
        chunk_mid(first)
        chunk_out(chunk, first)
        chunk_mid(first + 1)
        chunk_out(chunk, first + 1)

    def hidden_chunk(chunk, carry):
        step = CHUNK_STEP + chunk
        hook(step, CHUNK_STEP, POST_STEP)
        chunk_tiles(chunk, 0)
        hook(step, CHUNK_STEP, POST_STEP, 1)
        chunk_tiles(chunk, 2)
        side = lax.rem(chunk, 2)

        for half in range(2):

            @pl.when(chunk // 2 == half)
            def _(half=half):
                for part in range(2):
                    lanes = slice(part * HALF, (part + 1) * HALF)
                    grads[half][side, part, :512] = acc_one[:, lanes].astype(bf16)
                    grads[half][side, part, 512:] = acc_two[:, lanes].astype(bf16)

        return carry

    def after_mlp(tile, carry):
        hook(POST_STEP + tile, POST_STEP, ATT_STEP)
        base = tile * TILE
        tokens = pl.ds(pl.multiple_of(base, TILE), TILE)
        for row in range(0, TILE, 128):
            at = pl.ds(pl.multiple_of(base + row, 128), 128)
            valid = valid_rows(base + row)
            h = res[at, :]
            mlp[at, :] = h + valid * mlp[at, :]
            gn = grad_n[at, :]
            hat, rstd = norm_stats(h)
            acc_ln[2:3, :] += jnp.sum(gn * hat, axis=0, keepdims=True)
            acc_ln[3:4, :] += jnp.sum(gn, axis=0, keepdims=True)
            scaled = gn * ln[2:3, :]
            back = rstd * (
                scaled
                - jnp.mean(scaled, axis=1, keepdims=True)
                - hat * jnp.mean(scaled * hat, axis=1, keepdims=True)
            )
            gh = dy_rows(at) + back
            res[at, :] = gh
            gm[at, :] = (valid * gh).astype(bf16)
        ga = gm[tokens, :]
        acc_one[...] += mm(ctx[tokens, :], ga, TN)
        low, high = mlp[tokens, :HALF], mlp[tokens, HALF:]
        ctx[tokens, :HALF] = jnp.where(head == 0, low, high).astype(bf16)
        ctx[tokens, HALF:] = jnp.where(head == 0, high, low).astype(bf16)
        grad_low = mm(ga, out_own[...], NT)
        grad_high = mm(ga, out_other[...], NT)
        gm[tokens, :HALF] = grad_low.astype(bf16)
        gm[tokens, HALF:] = grad_high.astype(bf16)
        return carry

    low_lanes, high_lanes = lane_masks(bf16)
    scale_factor = float(HEAD_DIM) ** (-0.5)

    def span_tokens(block, span):
        return pl.ds(pl.multiple_of(block * block_rows + span * SPAN, SPAN), SPAN)

    def attention_in(block, qkv, bars, span):
        rows = pl.ds(span * SPAN, SPAN)
        held = []
        for pair in range(PAIRS):
            _, _, at_v = pair_columns(pair)
            lanes = pl.ds(pair * 128, 128)
            lanes_v = pl.ds(512 + pair * 128, 128)
            values = jnp.concatenate([qkv[rows, at_v : at_v + 128], bars[rows, lanes_v]], axis=0)
            grad = head_stack(gm[span_tokens(block, span), lanes], low_lanes, high_lanes)
            held.append((grad, mm(values, grad, NT)))
        return held

    def attention_mid(probs, span, held):
        scores = []
        for pair in range(PAIRS):
            prob_f = probs[span * PAIRS + pair].astype(f32)
            weighted = held[pair][1] * prob_f
            delta = jnp.sum(weighted, axis=0, keepdims=True)
            scores.append((weighted - prob_f * delta).astype(bf16))
        return scores

    def attention_out(block, qkv, bars, probs, span, held, scores):
        rows = pl.ds(span * SPAN, SPAN)
        tokens = span_tokens(block, span)
        inverse = table[0, block * SPANS_STEP + span]
        for pair in range(PAIRS):
            at_q, at_k, at_v = pair_columns(pair)
            lanes = pl.ds(pair * 128, 128)
            lanes_v = pl.ds(512 + pair * 128, 128)
            keys = jnp.concatenate([qkv[rows, at_k : at_k + 128], bars[rows, lanes]], axis=0)
            query = head_stack(qkv[rows, at_q : at_q + 128], low_lanes, high_lanes)
            grad_q = unstack_transposed(mm(keys, scores[pair], TN)) * scale_factor
            grad_k = mm(scores[pair], query)
            grad_v = mm(probs[span * PAIRS + pair], held[pair][0])
            grad_qkv[tokens, at_q : at_q + 128] = grad_q.astype(bf16)
            grad_qkv[tokens, at_k : at_k + 128] = (grad_k[:SPAN] + after[:, lanes]).astype(bf16)
            grad_qkv[tokens, at_v : at_v + 128] = (grad_v[:SPAN] + after[:, lanes_v]).astype(bf16)
            after[:, lanes] += grad_k[SPAN:] * inverse
            after[:, lanes_v] += grad_v[SPAN:] * inverse

    def attention_block(index, carry):
        block = ATT_STEPS - 1 - index
        slot = lax.rem(index, 2)
        hook(ATT_STEP + index, ATT_STEP, LAST_STEP)
        for copy in block_copies(index):
            copy.wait()
        qkv, bars, probs = qkv_two.at[slot], bars_two.at[slot], probs_two.at[slot]
        for row in range(0, block_rows, 128):
            rows = pl.ds(pl.multiple_of(block * block_rows + row, 128), 128)
            hat, _ = norm_stats(x_rows(rows))
            normed_t[:, row : row + 128] = (hat * ln[0:1, :] + ln[1:2, :]).astype(bf16).T
        held_one = attention_in(block, qkv, bars, 1)
        held_two = attention_in(block, qkv, bars, 0)
        scores = attention_mid(probs, 1, held_one)
        attention_out(block, qkv, bars, probs, 1, held_one, scores)
        scores = attention_mid(probs, 0, held_two)
        attention_out(block, qkv, bars, probs, 0, held_two, scores)
        tokens = pl.ds(pl.multiple_of(block * block_rows, block_rows), block_rows)
        for side in range(2):
            for part in range(3):
                at = side * 3 * HALF + part * HALF
                rows = slice(part * D, (part + 1) * D)
                lanes = slice(side * HALF, (side + 1) * HALF)
                mlp[rows, lanes] += mm(
                    normed_t[:, :block_rows], grad_qkv[tokens, at : at + HALF]
                )


        @pl.when(index + 2 < ATT_STEPS)
        def _():
            for copy in block_copies(index + 2):
                copy.start()

        return carry

    def first_norm(tile, carry):
        hook(LAST_STEP + tile, LAST_STEP, STEPS)
        base = tile * TILE
        tokens = pl.ds(pl.multiple_of(base, TILE), TILE)
        for side, w in enumerate((w_own, w_other)):
            for part in range(3):
                at = side * 3 * HALF + part * HALF
                back = mm(grad_qkv[tokens, at : at + HALF], w[part], NT)
                if side == 0 and part == 0:
                    grad_n[:TILE, :] = back
                else:
                    grad_n[:TILE, :] += back
        for row in range(0, TILE, 128):
            at = pl.ds(pl.multiple_of(base + row, 128), 128)
            hat, rstd = norm_stats(x_rows(at))
            gn = grad_n[row : row + 128, :]
            acc_ln[0:1, :] += jnp.sum(gn * hat, axis=0, keepdims=True)
            acc_ln[1:2, :] += jnp.sum(gn, axis=0, keepdims=True)
            scaled = gn * ln[0:1, :]
            back = rstd * (
                scaled
                - jnp.mean(scaled, axis=1, keepdims=True)
                - hat * jnp.mean(scaled * hat, axis=1, keepdims=True)
            )
            gx = res[at, :] + back
            low, high = gx[:, :HALF], gx[:, HALF:]
            dy_own[at, :] = jnp.where(head == 0, low, high).astype(bf16)
            dy_other[at, :] = jnp.where(head == 0, high, low).astype(bf16)
        return carry

    for copy in loads + weight_copies + block_copies(0) + block_copies(1):
        copy.start()
    if summing:
        lines.greet()
    after[...] = jnp.zeros_like(after)
    acc_ln[...] = jnp.zeros_like(acc_ln)
    for copy in loads:
        copy.wait()
    lax.fori_loop(0, TILES, before_mlp, 0)
    for copy in weight_copies:
        copy.wait()
    lax.fori_loop(0, CHUNKS, hidden_chunk, 0)
    acc_one[...] = jnp.zeros_like(acc_one)
    lax.fori_loop(0, TILES, after_mlp, 0)
    for copy in stores[:2]:
        copy.start()
    for side in range(2):
        grads[2][side, 0] = acc_one[side * HALF : (side + 1) * HALF, :].astype(bf16)
    mlp[...] = jnp.zeros_like(mlp)
    lax.fori_loop(0, ATT_STEPS, attention_block, 0)
    for side in range(2):
        for part in range(2):
            for kind in range(3):
                rows = slice(kind * HALF, (kind + 1) * HALF)
                source = slice(kind * D + part * HALF, kind * D + (part + 1) * HALF)
                lanes = slice(side * HALF, (side + 1) * HALF)
                grads[3][side, part, rows] = mlp[source, lanes].astype(bf16)
    lax.fori_loop(0, TILES, first_norm, 0)
    for copy in stores[2:]:
        copy.start()
    if summing:
        small.send(0)
        for index in range(EVENTS):
            left = [
                (which, len(times) + index)
                for which, times in enumerate(EVENT_AT)
                if len(times) + index < EVENTS
            ]
            run_events(left)
            if index <= 3:
                small.finish(index)
            if index < 3:
                small.send(index + 1)
        for entry in sums:
            entry.finish()
    else:
        for total, grad in zip(totals, grads):
            total[...] = grad[...]
        ln_total[...] = acc_ln[...]
    for copy in stores:
        copy.wait()


def rows_spec(width):
    return pl.BlockSpec((TILE, width), lambda i: (i, 0))


def whole_spec(shape):
    rank = len(shape)
    return pl.BlockSpec(shape, lambda i: (0,) * rank, pipeline_mode=pl.Buffered(1))


def shaped(shape, dtype=bf16):
    return jax.ShapeDtypeStruct(shape, dtype)


smem_spec = pl.BlockSpec(memory_space=pltpu.SMEM)
limits = pltpu.CompilerParams(vmem_limit_bytes=60 * 1024 * 1024)


def span_table():
    ids = np.arange(ROWS)
    inverse = 1.0 / np.maximum(ids, 1)
    shift = np.where(ids >= 1, np.log(np.maximum(ids, 1)), masked_score)
    return jnp.asarray(np.stack([inverse, shift]).astype(np.float32))


def causal_bias():
    key = np.arange(SPAN)[:, None]
    query = np.arange(2 * SPAN)[None, :] % SPAN
    return jnp.asarray(np.where(key <= query, 0.0, masked_score).astype(np.float32))


def layer_local(x_own, x_other, dy_own, dy_other, lengths, ln_params, weights):
    qkv_own, qkv_other, out_own, out_other, up_own, up_other, down_own, down_other = weights
    table = span_table()
    qkv, bars, probs, ctx = pl.pallas_call(
        forward_attention,
        grid=(TILES,),
        in_specs=[
            smem_spec,
            rows_spec(HALF),
            rows_spec(HALF),
            whole_spec((4, D)),
            whole_spec((3, D, HALF)),
            whole_spec((3, D, HALF)),
            whole_spec((SPAN, 2 * SPAN)),
        ],
        out_specs=[
            rows_spec(3 * D),
            rows_spec(2 * D),
            pl.BlockSpec((SPANS_TILE * PAIRS, 2 * SPAN, 2 * SPAN), lambda i: (i, 0, 0)),
            rows_spec(D),
        ],
        out_shape=[
            shaped((SEQ, 3 * D)),
            shaped((SEQ, 2 * D)),
            shaped((ROWS * PAIRS, 2 * SPAN, 2 * SPAN)),
            shaped((SEQ, D)),
        ],
        scratch_shapes=[pltpu.VMEM((SPAN, 2 * D), f32), pltpu.VMEM((TILE, D), bf16)],
        compiler_params=limits,
        name="forward_attention",
    )(table, x_own, x_other, ln_params, qkv_own, qkv_other, causal_bias())
    count = lax.axis_size("dp")
    summing = whole_slices(count)
    sum_buffers, extra, total_specs, total_shapes = [], {}, [], []
    anywhere = pl.BlockSpec(memory_space=pl.ANY)
    if summing:
        for shape, orders in PIECES:
            sum_buffers += sum_scratch(shape, orders, count)
            total_specs.append(anywhere)
            total_shapes.append(shaped(shape))
        sum_buffers += ln_scratch(count)
        extra = dict(collective_id=0, has_side_effects=True)
    else:
        for shape, _ in PIECES:
            total_specs.append(pl.BlockSpec(memory_space=pltpu.VMEM))
            total_shapes.append(shaped((2, *shape)))
    block_rows = SPANS_STEP * SPAN
    vmem = pl.BlockSpec(memory_space=pltpu.VMEM)
    y_own, y_other, gx_own, gx_other, *totals = pl.pallas_call(
        functools.partial(mlp_and_back, count),
        in_specs=[smem_spec, smem_spec, vmem] + [anywhere] * 16,
        out_specs=[anywhere] * 4 + total_specs + [vmem],
        out_shape=[shaped((SEQ, HALF))] * 4 + total_shapes + [shaped((4, D), f32)],
        scratch_shapes=[
            pltpu.VMEM((SEQ, HALF), bf16),
            pltpu.VMEM((SEQ, HALF), bf16),
            pltpu.VMEM((SEQ, HALF), bf16),
            pltpu.VMEM((SEQ, HALF), bf16),
            pltpu.VMEM((SEQ, D), bf16),
            pltpu.VMEM((2, block_rows, 3 * D), bf16),
            pltpu.VMEM((2, block_rows, 2 * D), bf16),
            pltpu.VMEM((2, SPANS_STEP * PAIRS, 2 * SPAN, 2 * SPAN), bf16),
            pltpu.VMEM((HALF, D), bf16),
            pltpu.VMEM((HALF, D), bf16),
            pltpu.VMEM((3, D, HALF), bf16),
            pltpu.VMEM((3, D, HALF), bf16),
            pltpu.VMEM((CHUNKS, D, 512), bf16),
            pltpu.VMEM((CHUNKS, 512, D), bf16),
            pltpu.SemaphoreType.DMA((9,)),
            pltpu.SemaphoreType.DMA((2 * CHUNKS,)),
            pltpu.SemaphoreType.DMA((2, 3)),
            pltpu.SemaphoreType.DMA((4,)),
            pltpu.VMEM((SEQ, D), f32),
            pltpu.VMEM((SEQ, 3 * D), bf16),
            pltpu.VMEM((D, SEQ), bf16),
            pltpu.VMEM((SEQ, D), bf16),
            pltpu.VMEM((SEQ, D), f32),
            pltpu.VMEM((SEQ, D), f32),
            pltpu.VMEM((512, D), f32),
            pltpu.VMEM((D, 512), f32),
            pltpu.VMEM((2, TILE, 512), f32),
            pltpu.VMEM((2, TILE, 512), f32),
            pltpu.VMEM((SPAN, 2 * D), f32),
            pltpu.VMEM((4, D), f32),
        ]
        + [pltpu.VMEM((2, *shape), bf16) for shape, _ in PIECES]
        + sum_buffers,
        compiler_params=pltpu.CompilerParams(vmem_limit_bytes=63 * 1024 * 1024, **extra),
        name="mlp_and_back",
    )(
        table,
        lengths,
        ln_params,
        x_own,
        x_other,
        dy_own,
        dy_other,
        ctx,
        qkv,
        bars,
        probs,
        out_own,
        out_other,
        qkv_own,
        qkv_other,
        up_own,
        up_other,
        down_own,
        down_other,
    )
    if not summing:
        *grads, g_ln = totals
        chips = [grad[0].astype(f32) + swap_heads(grad[1]).astype(f32) for grad in grads]
        pieces = [lax.psum(chip.astype(bf16), "dp") for chip in chips]
        totals = (*pieces, lax.psum(g_ln, ("dp", "head")))
    return (y_own, y_other), (gx_own, gx_other), totals


RATES = (
    float(D) ** (-0.5),
    4.0 * float(D) ** (-0.5),
    float(D) ** (-0.5),
    float(FF) ** (-0.5),
    0.7,
)


def adam_step(gradient, weight, moment_one, moment_two, step_rate):
    first_new = beta_one * moment_one + (1.0 - beta_one) * gradient
    second_new = beta_two * moment_two + (1.0 - beta_two) * gradient * gradient
    first_hat = first_new * (1.0 / (1.0 - beta_one**STEP))
    second_hat = second_new * (1.0 / (1.0 - beta_two**STEP))
    weight_new = weight - step_rate * (
        first_hat / (jnp.sqrt(second_hat) + epsilon_adam) + decay_rate * weight
    )
    return (weight_new, first_new, second_new)


def kind_gradient(kind, refs, step):
    joined = [
        jnp.concatenate([ref[part] for part in range(ref.shape[0])], axis=0 if kind == 0 else 1)
        for ref in refs
    ]
    if kind == 0:
        return joined[0].astype(f32)[None]
    if kind == 2:
        return jnp.concatenate(joined, axis=1).astype(f32)
    if kind == 3:
        return jnp.where(step < 2, joined[0].astype(f32), joined[1].astype(f32))
    return joined[0].astype(f32)


BLOCKS = (
    (3, (1, D, HALF), ((3, (2, HALF, HALF), lambda i: (0, i, 0)),)),
    (1, (HALF, D), ((2, (1, HALF, D), lambda i: (0, i, 0)),)),
    (
        4,
        (128, 1024),
        (
            (0, (2, 128, HALF), lambda i: (0, 4 + i, 0)),
            (1, (2, 128, HALF), lambda i: (0, 4 + i, 0)),
        ),
    ),
    (
        4,
        (HALF, D),
        (
            (0, (2, HALF, HALF), lambda i: (0, jnp.minimum(i, 1), 0)),
            (1, (2, HALF, HALF), lambda i: (0, jnp.maximum(i - 2, 0), 0)),
        ),
    ),
)


def adam_kernel(kinds, owners, *refs):
    step = pl.program_id(0)
    chip = lax.axis_index("dp")
    ins = sum(len(BLOCKS[kind][2]) + 3 for kind in kinds)
    inputs, outputs = list(refs[:ins]), list(refs[ins:])
    first = 0
    for kind in kinds:
        grads = [inputs.pop(0) for _ in BLOCKS[kind][2]]
        weight, one, two = [inputs.pop(0) for _ in range(3)]
        owned, new, first_new, second_new, copy = [outputs.pop(0) for _ in range(5)]
        steps = BLOCKS[kind][0]

        @pl.when((step >= first) & (step < first + steps))
        def _(kind=kind, grads=grads, weight=weight, one=one, two=two, owned=owned, new=new,
              first_new=first_new, second_new=second_new, copy=copy, first=first):
            gradient = kind_gradient(kind, grads, step - first)
            results = adam_step(gradient, weight[...], one[...], two[...], RATES[kind])
            owned[...] = jnp.where(owners[kind] == chip, gradient, 0.0)
            new[...] = results[0]
            first_new[...] = results[1]
            second_new[...] = results[2]
            copy[...] = results[0].astype(bf16)

        first += steps


def adam_update(kinds, owners, pieces, weights, ones, twos):
    in_specs, out_specs, out_shape, operands = [smem_spec], [], [], [owners]
    first = 0
    for index, kind in enumerate(kinds):
        steps, block, sources = BLOCKS[kind]

        def place(i, first=first, steps=steps):
            return jnp.clip(i - first, 0, steps - 1)

        def at(i, place=place, rank=len(block)):
            return (place(i),) + (0,) * (rank - 1)

        for piece, grad_block, grad_place in sources:

            def grad_at(i, place=place, grad_place=grad_place):
                return grad_place(place(i))

            in_specs.append(pl.BlockSpec(grad_block, grad_at))
            operands.append(pieces[piece])
        spec = pl.BlockSpec(block, at)
        in_specs += [spec] * 3
        out_specs += [spec] * 5
        whole = weights[index].shape
        out_shape += [shaped(whole, f32)] * 4 + [shaped(whole)]
        operands += [weights[index], ones[index], twos[index]]
        first += steps
    results = pl.pallas_call(
        functools.partial(adam_kernel, kinds),
        grid=(first,),
        in_specs=in_specs,
        out_specs=out_specs,
        out_shape=out_shape,
        compiler_params=limits,
        name="adam_update",
    )(*operands)
    return [results[index * 5 : index * 5 + 5] for index in range(len(kinds))]


def gather_inputs(tokens, cotangent, w_qkv, w_out, w_up, w_down):
    head = lax.axis_index("head")

    def both(array):
        halves = array.reshape(2, SEQ, HALF)
        own = lax.dynamic_index_in_dim(halves, head, 0, keepdims=False)
        other = lax.dynamic_index_in_dim(halves, 1 - head, 0, keepdims=False)
        return own, swap_heads(other)

    x_own, x_other = both(tokens)
    qkv_own = w_qkv.transpose(1, 0, 2).astype(bf16)
    out_own = w_out.astype(bf16)
    up_own = w_up.astype(bf16)
    down_own = w_down.astype(bf16)
    qkv_other = swap_heads(qkv_own)
    dy_own, dy_other = both(cotangent)
    weights = (
        qkv_own,
        qkv_other,
        out_own,
        swap_heads(out_own),
        up_own,
        swap_heads(up_own),
        down_own,
        swap_heads(down_own),
    )
    return x_own, x_other, dy_own, dy_other, weights


def place_rows(pieces):
    head = lax.axis_index("head")
    own, away = pieces
    arrived = swap_heads(away)
    return jnp.concatenate(
        [jnp.where(head == 0, own, arrived), jnp.where(head == 0, arrived, own)], axis=0
    )


def body(
    tokens,
    cotangent,
    lengths,
    owners,
    w_qkv,
    w_out,
    w_up,
    w_down,
    ln_params,
    m_qkv,
    m_out,
    m_up,
    m_down,
    m_ln,
    v_qkv,
    v_out,
    v_up,
    v_down,
    v_ln,
):
    x_own, x_other, dy_own, dy_other, weights = gather_inputs(
        tokens, cotangent, w_qkv, w_out, w_up, w_down
    )
    y, gx, totals = layer_local(
        x_own, x_other, dy_own, dy_other, lengths, ln_params, weights
    )
    output_rows = place_rows(y)
    grad_input = place_rows(gx)
    *pieces, t_ln = totals

    def as_blocks(array):
        return array.transpose(1, 0, 2)

    results = adam_update(
        (0, 1, 2, 3),
        owners,
        pieces,
        (as_blocks(w_qkv), w_out, w_up, w_down),
        (as_blocks(m_qkv), m_out, m_up, m_down),
        (as_blocks(v_qkv), v_out, v_up, v_down),
    )
    results[0] = [as_blocks(array) for array in results[0]]
    mine = owners[4] == lax.axis_index("dp")
    ln_results = adam_step(t_ln, ln_params, m_ln, v_ln, RATES[4])
    results.append([jnp.where(mine, t_ln, 0.0), *ln_results])
    owned, new, first, second = [
        tuple(results[kind][slot] for kind in range(5)) for slot in range(4)
    ]
    copies = tuple(results[kind][4] for kind in range(4))
    owned = tuple(array[None] for array in owned)
    return (output_rows, grad_input) + owned + new + first + second + copies


PLACED = (
    (P("dp", "head"),) * 2
    + (P("dp"), P())
    + (P(None, None, "head"), P("head", None), P(None, "head"), P("head", None), P()) * 3
)
RESULTS = (
    (P("dp", "head"),) * 2
    + (
        P("dp", None, None, "head"),
        P("dp", "head", None),
        P("dp", None, "head"),
        P("dp", "head", None),
        P("dp", None, None),
    )
    + (P(None, None, "head"), P("head", None), P(None, "head"), P("head", None), P()) * 3
    + (P(None, None, "head"), P("head", None), P(None, "head"), P("head", None))
)


def solution(mesh):
    return jax.shard_map(
        body, mesh=mesh, in_specs=PLACED, out_specs=RESULTS, check_vma=False
    )
```

time: 215 us -> 181 us (0.84)
  Pallas kernels: 195 us -> 163 us
  other arithmetic: 8.6 us -> 5.78 us
    pallas_call x2 -> x1, Pallas kernels: 145 us -> 124 us  [layer_local(): pl.pallas_call(functools.partial(mlp_and_back, count), in_specs=[smem_spe...]
    pallas_call x1, Pallas kernels: 27.9 us -> 16.5 us  [layer_local(): pl.pallas_call(forward_attention, grid=(TILES,), in_specs=[smem_spec, row...]
  transfers between devices with their start and end apart: 8 -> 8, of which waited for: 0 -> 1; matrix products, arithmetic and copies ran while one was open for 4% -> 4% of each run, Pallas kernels for 68% -> 22%
where the time goes in v4:
time: 181 us
  Pallas kernels  163 us (90%)
  local copies, waits for them, and re-layouts  6.97 us (4%)
  other arithmetic  5.78 us (3%)
  starting transfers between devices  2.81 us (2%)
    pallas_call x1, Pallas kernels, layer_local(): pl.pallas_call(functools.partial(mlp_and_back, count), in_specs=[smem_spe...  124 us
    pallas_call x1, Pallas kernels, adam_update(): pl.pallas_call(functools.partial(adam_kernel, kinds), grid=(first,), in_s...  22.7 us
    pallas_call x1, Pallas kernels, layer_local(): pl.pallas_call(forward_attention, grid=(TILES,), in_specs=[smem_spec, row...  16.5 us
    squeeze x2, local copies, waits for them, and re-layouts, both(): other = lax.dynamic_index_in_dim(halves, 1 - head, 0, keepdims=False)  4.25 us
  transfers between devices with their start and end apart: 8, of which 1 were waited for; matrix products, arithmetic and copies ran while one was open for 4% of the time, Pallas kernels for 22%

profile of v4, /device:TPU:0, one launch (start us, length us, event | category | flops | bytes accessed | tf_op | source)
XLA Modules:
  0.0 181.0 jit_solution(10066575162698743029)
XLA Ops:
  0.7 0.0 copy-start.1
  0.7 1.6 bitcast_convert_fusion.w_own.w_own_at
  2.3 0.0 copy-start.2
  2.3 0.0 copy-start
  2.3 0.5 collective-permute-start.2
  2.9 0.0 copy-done.1
  2.9 0.1 convert_element_type.15.down_own
  3.0 0.0 copy-start.3
  3.0 0.4 collective-permute-start.5
  3.4 1.3 copy-done
  4.7 0.2 convert_element_type.14.up_own
  4.8 0.0 copy-done.2
  4.9 0.0 copy-start.4
  4.9 0.5 collective-permute-start.4
  5.4 2.8 %dynamic-slice_bitcast_fusion.2 = (bf16[2048,256]{1,0:T(8,128)(2,1)S(1)}, bf16[2048,256]{1,0:T(8,128)(2,1)}) fusion(bf16[2,2048,256]{2,1,0:T(8,128)(2,1)} %bitcast.28, s32[]{:T(128)S(6)} %select_n.39, s32[]{:T(128)S(6)} %select_n.38), kind=kLoop, calls=%fused_computation.4 | loop fusion | bytes 4194312 | tf_op jit(solution)/shard_map/jit(dynamic_index_in_dim)/squeeze | solution.py:1163
  8.2 0.0 copy-done.3
  8.2 0.0 copy-done.4
  8.2 0.2 collective-permute-start
  8.4 0.0 copy-done.5
  8.4 1.5 dynamic-slice_bitcast_fusion
  9.8 0.3 collective-permute-start.1
  10.2 0.0 copy-done.6
  10.2 0.0 copy-start.7
  10.2 0.0 collective-permute-done.2.w_other.w_other_at
  10.2 0.3 collective-permute-start.3
  10.5 0.5 collective-permute-done.x_other.x_other_at
  11.0 16.5 %forward_attention.1 = (bf16[2048,1536]{1,0:T(8,128)(2,1)}, bf16[2048,1024]{1,0:T(8,128)(2,1)}, bf16[64,256,256]{2,1,0:T(8,128)(2,1)}, bf16[2048,512]{1,0:T(8,128)(2,1)}) custom-call(f32[2,16]{1,0:T(2,128)} %constant.41.clone.table, bf16[2048,256]{1,0:T(8,128)(2,1)} %get-tuple-element.102.x_own.x_own_at, ...), custom_call_target="tpu_custom_call" | custom-call | tf_op jit(solution)/shard_map/forward_attention/pallas_call | solution.py:922
  27.5 0.0 collective-permute-done.3.out_other_at
  27.5 0.0 copy-start.10
  27.5 0.0 collective-permute-done.5.down_other
  27.6 0.0 collective-permute-done.4.up_other
  27.6 0.0 copy-done.7
  27.6 0.0 collective-permute-done.1.dy_other_at
  27.6 0.7 copy-done.10
  28.2 124.1 %mlp_and_back.1 = (bf16[2048,256]{1,0:T(8,128)(2,1)}, bf16[2048,256]{1,0:T(8,128)(2,1)}, bf16[2048,256]{1,0:T(8,128)(2,1)}, bf16[2048,256]{1,0:T(8,128)(2,1)}, b...) custom-call(f32[2,16]{1,0:T(2,128)} %constant.41.clone.table, ...), custom_call_target="tpu_custom_call" | custom-call | tf_op jit(solution)/shard_map/mlp_and_back/pallas_call | solution.py:967
  152.3 0.1 collective-permute-start.6
  152.4 0.0 copy-done.15
  152.4 0.6 slice.3
  153.6 0.5 collective-permute-start.7
  154.2 22.7 %adam_update.1 = (f32[3,512,256]{2,1,0:T(8,128)}, f32[3,512,256]{2,1,0:T(8,128)}, f32[3,512,256]{2,1,0:T(8,128)}, f32[3,512,256]{2,1,0:T(8,128)}, bf16[3,512,256...) custom-call(s32[5]{0:T(128)} %owners.1, ...), custom_call_target="tpu_custom_call" | custom-call | tf_op jit(solution)/shard_map/adam_update/pallas_call | solution.py:1145
  177.0 0.6 multiply_subtract_fusion
  177.6 0.0 collective-permute-done.6
  177.6 0.1 broadcast_select_fusion.3
  177.8 1.5 pad_maximum_fusion
  179.2 0.0 collective-permute-done.7
  179.2 0.1 copy-done.8
  179.4 0.1 broadcast_select_fusion.1
  179.5 1.5 pad_maximum_fusion.1
  (15 shorter events, 0.1 us)
Async XLA Ops:
  0.7 2.2 %copy-start.1 = (f32[1024,512]{1,0:T(8,128)S(1)}, f32[1024,512]{1,0:T(8,128)}, u32[]{:S(2)}) copy-start(f32[1024,512]{1,0:T(8,128)} %refs_15_.1) | copy-start | bytes 6291460
  2.3 2.5 %copy-start.2 = (bf16[3,512,256]{2,1,0:T(8,128)(2,1)}, bf16[3,512,256]{2,1,0:T(8,128)(2,1)S(1)}, u32[]{:S(2)}) copy-start(bf16[3,512,256]{2,1,0:T(8,128)(2,1)S(1)} %bitcast_convert_fusion.w_own.w_own_at) | copy-start | bytes 2359300
  2.3 2.4 %copy-start = (f32[512,1024]{1,0:T(8,128)S(1)}, f32[512,1024]{1,0:T(8,128)}, u32[]{:S(2)}) copy-start(f32[512,1024]{1,0:T(8,128)} %refs_10_.1) | copy-start | bytes 6291460
  2.3 7.9 %collective-permute-start.2 = (bf16[3,512,256]{2,1,0:T(8,128)(2,1)S(1)}, bf16[3,512,256]{2,1,0:T(8,128)(2,1)}, u32[]{:S(2)}, u32[]{:S(2)}) collective-permute-start(bf16[3,512,256]{2,1,0:T(8,128)(2,1)S(1)} %bitcast_convert_fusion.w_own.w_own_at), channel_id=1, source_target_pairs={{0,1},{1,0},{2,3},{3,2},{4,5},{5,4},{6,7},{7,6},{8,9},{9,8},{10,11... | collective-permute-start | bytes 2359304 | tf_op jit(solution)/shard_map/ppermute | solution.py:167
  3.0 5.2 %copy-start.3 = (bf16[1024,512]{1,0:T(8,128)(2,1)}, bf16[1024,512]{1,0:T(8,128)(2,1)S(1)}, u32[]{:S(2)}) copy-start(bf16[1024,512]{1,0:T(8,128)(2,1)S(1)} %convert_element_type.15.down_own) | copy-start | bytes 3145732
  3.0 24.5 %collective-permute-start.5 = (bf16[1024,512]{1,0:T(8,128)(2,1)S(1)}, bf16[1024,512]{1,0:T(8,128)(2,1)}, u32[]{:S(2)}, u32[]{:S(2)}) collective-permute-start(bf16[1024,512]{1,0:T(8,128)(2,1)S(1)} %convert_element_type.15.down_own), channel_id=1, source_target_pairs={{0,1},{1,0},{2,3},{3,2},{4,5},{5,4},{6,7},{7,6},{8,9},{9,8},{10,11... | collective-permute-start | bytes 3145736 | tf_op jit(solution)/shard_map/ppermute | solution.py:167
  4.9 3.3 %copy-start.4 = (bf16[512,1024]{1,0:T(8,128)(2,1)}, bf16[512,1024]{1,0:T(8,128)(2,1)S(1)}, u32[]{:S(2)}) copy-start(bf16[512,1024]{1,0:T(8,128)(2,1)S(1)} %convert_element_type.14.up_own) | copy-start | bytes 3145732
  4.9 22.7 %collective-permute-start.4 = (bf16[512,1024]{1,0:T(8,128)(2,1)S(1)}, bf16[512,1024]{1,0:T(8,128)(2,1)}, u32[]{:S(2)}, u32[]{:S(2)}) collective-permute-start(bf16[512,1024]{1,0:T(8,128)(2,1)S(1)} %convert_element_type.14.up_own), channel_id=1, source_target_pairs={{0,1},{1,0},{2,3},{3,2},{4,5},{5,4},{6,7},{7,6},{8,9},{9,8},{10,11... | collective-permute-start | bytes 3145736 | tf_op jit(solution)/shard_map/ppermute | solution.py:167
  5.4 3.0 %copy-start.5 = (bf16[4096,256]{1,0:T(8,128)(2,1)S(1)}, bf16[4096,256]{1,0:T(8,128)(2,1)}, u32[]{:S(2)}) copy-start(bf16[4096,256]{1,0:T(8,128)(2,1)} %param.22) | copy-start | bytes 6291460
  8.2 2.8 %collective-permute-start = (bf16[2048,256]{1,0:T(8,128)(2,1)S(1)}, bf16[2048,256]{1,0:T(8,128)(2,1)}, u32[]{:S(2)}, u32[]{:S(2)}) collective-permute-start(bf16[2048,256]{1,0:T(8,128)(2,1)S(1)} %get-tuple-element.101), channel_id=1, source_target_pairs={{0,1},{1,0},{2,3},{3,2},{4,5},{5,4},{6,7},{7,6},{8,9},{9,8},{10,11... | collective-permute-start | bytes 3145736 | tf_op jit(solution)/shard_map/ppermute | solution.py:167
  8.4 1.8 copy-start.6
  9.8 17.7 %collective-permute-start.1 = (bf16[2048,256]{1,0:T(8,128)(2,1)}, bf16[2048,256]{1,0:T(8,128)(2,1)}, u32[]{:S(2)}, u32[]{:S(2)}) collective-permute-start(bf16[2048,256]{1,0:T(8,128)(2,1)} %get-tuple-element.99), channel_id=1, source_target_pairs={{0,1},{1,0},{2,3},{3,2},{4,5},{5,4},{6,7},{7,6},{8,9},{9,8},{10,11... | collective-permute-start | bytes 3145736 | tf_op jit(solution)/shard_map/ppermute | solution.py:167
  10.2 17.4 %copy-start.7 = (bf16[256,512]{1,0:T(8,128)(2,1)}, bf16[256,512]{1,0:T(8,128)(2,1)S(1)}, u32[]{:S(2)}) copy-start(bf16[256,512]{1,0:T(8,128)(2,1)S(1)} %convert_element_type.13.out_own_at) | copy-start | bytes 786436
  10.2 17.3 %collective-permute-start.3 = (bf16[256,512]{1,0:T(8,128)(2,1)S(1)}, bf16[256,512]{1,0:T(8,128)(2,1)S(1)}, u32[]{:S(2)}, u32[]{:S(2)}) collective-permute-start(bf16[256,512]{1,0:T(8,128)(2,1)S(1)} %convert_element_type.13.out_own_at), channel_id=1, source_target_pairs={{0,1},{1,0},{2,3},{3,2},{4,5},{5,4},{6,7},{7,6},{8,9},{9,8},{10,11... | collective-permute-start | bytes 786440 | tf_op jit(solution)/shard_map/ppermute | solution.py:167
  27.5 0.7 copy-start.10
  28.2 124.2 %copy-start.15 = (s32[5]{0:T(128)S(1)}, s32[5]{0:T(128)}, u32[]{:S(2)}) copy-start(s32[5]{0:T(128)} %owners.1) | copy-start | bytes 64
  152.3 25.3 %collective-permute-start.6 = (bf16[2048,256]{1,0:T(8,128)(2,1)}, bf16[2048,256]{1,0:T(8,128)(2,1)S(1)}, u32[]{:S(2)}, u32[]{:S(2)}) collective-permute-start(bf16[2048,256]{1,0:T(8,128)(2,1)} %get-tuple-element.64), channel_id=1, source_target_pairs={{0,1},{1,0},{2,3},{3,2},{4,5},{5,4},{6,7},{7,6},{8,9},{9,8},{10,11... | collective-permute-start | bytes 3145736 | tf_op jit(solution)/shard_map/ppermute | solution.py:167
  153.6 25.6 %collective-permute-start.7 = (bf16[2048,256]{1,0:T(8,128)(2,1)}, bf16[2048,256]{1,0:T(8,128)(2,1)S(1)}, u32[]{:S(2)}, u32[]{:S(2)}) collective-permute-start(bf16[2048,256]{1,0:T(8,128)(2,1)} %get-tuple-element.66), channel_id=1, source_target_pairs={{0,1},{1,0},{2,3},{3,2},{4,5},{5,4},{6,7},{7,6},{8,9},{9,8},{10,11... | collective-permute-start | bytes 3145736 | tf_op jit(solution)/shard_map/ppermute | solution.py:167
  154.2 22.7 %copy-start.11 = (f32[4,512]{1,0:T(4,128)S(1)}, f32[4,512]{1,0:T(4,128)}, u32[]{:S(2)}) copy-start(f32[4,512]{1,0:T(4,128)} %ln.3) | copy-start | bytes 24580
  154.2 22.7 %copy-start.12 = (f32[4,512]{1,0:T(4,128)S(1)}, f32[4,512]{1,0:T(4,128)}, u32[]{:S(2)}) copy-start(f32[4,512]{1,0:T(4,128)} %param.34) | copy-start | bytes 24580
  154.2 22.8 %copy-start.13 = (f32[4,512]{1,0:T(4,128)S(1)}, f32[4,512]{1,0:T(4,128)}, u32[]{:S(2)}) copy-start(f32[4,512]{1,0:T(4,128)} %param.39) | copy-start | bytes 24580
  154.2 22.8 %copy-start.14 = (f32[4,512]{1,0:T(4,128)S(1)}, f32[4,512]{1,0:T(4,128)}, u32[]{:S(2)}) copy-start(f32[4,512]{1,0:T(4,128)} %get-tuple-element.75) | copy-start | bytes 24580
  154.2 23.4 %copy-start.9 = (bf16[2048,256]{1,0:T(8,128)(2,1)S(1)}, bf16[2048,256]{1,0:T(8,128)(2,1)}, u32[]{:S(2)}) copy-start(bf16[2048,256]{1,0:T(8,128)(2,1)} %get-tuple-element.63) | copy-start | bytes 3145732
  177.7 1.6 copy-start.8

commit v5 on v4

--- a/solution.py
+++ b/solution.py
@@ -76,7 +76,7 @@
 
 
 def forward_attention(
-    table, x_own, x_other, ln, w_own, w_other, causal, qkv, bars, probs, ctx, run_sum, normed
+    head_at, table, x_own, x_other, ln, w_own, w_other, causal, qkv, bars, probs, ctx, run_sum, normed
 ):
     head = lax.axis_index("head")
     step = pl.program_id(0)
@@ -475,10 +475,10 @@
 LAST_STEP = ATT_STEP + ATT_STEPS
 STEPS = LAST_STEP + TILES
 EVENT_AT = (
-    ((6, 0), (6, 1), (7, 1), (8, 0), (12, 0), (14, 0), (16, 0), (18, 0)),
-    ((8, 0), (9, 0), (13, 0), (15, 0), (17, 0), (19, 0), (21, 0), (23, 0)),
-    ((12, 0), (13, 0), (15, 0), (16, 0), (18, 0), (20, 0), (21, 0), (23, 0)),
-    ((20, 0), (21, 0), (23, 0)),
+    ((6, 0), (6, 1), (7, 1), (8, 0), (12, 0), (15, 0), (17, 0), (19, 0),),
+    ((8, 0), (9, 0), (13, 0), (16, 0), (19, 0),),
+    ((14, 0), (16, 0), (18, 0),),
+    ((20, 0), (22, 0),),
 )
 
 
@@ -545,6 +545,7 @@
                 def _(events=events):
                     run_events(events)
 
+    mine = pl.ds(head * SEQ, SEQ)
     loads = [
         pltpu.make_async_copy(source, target, load_sem.at[index])
         for index, (source, target) in enumerate(
@@ -552,10 +553,10 @@
                 (ctx_at, ctx),
                 (out_own_at, out_own),
                 (out_other_at, out_other),
-                (x_own_at, x_own),
-                (x_other_at, x_other),
-                (dy_own_at, dy_own),
-                (dy_other_at, dy_other),
+                (x_own_at.at[mine], x_own),
+                (x_other_at.at[mine], x_other),
+                (dy_own_at.at[mine], dy_own),
+                (dy_other_at.at[mine], dy_other),
                 (w_own_at, w_own),
                 (w_other_at, w_other),
             )
@@ -587,17 +588,28 @@
             for which, (source, target) in enumerate(pairs)
         ]
 
-    stores = [
-        pltpu.make_async_copy(source, target, store_sem.at[index])
-        for index, (source, target) in enumerate(
-            (
-                (ctx.at[:, pl.ds(0, HALF)], y_own_at),
-                (ctx.at[:, pl.ds(HALF, HALF)], y_other_at),
-                (dy_own, gx_own_at),
-                (dy_other, gx_other_at),
+    stores = []
+    for index, (source, target) in enumerate(
+        (
+            (ctx.at[:, pl.ds(0, HALF)], y_own_at),
+            (ctx.at[:, pl.ds(HALF, HALF)], y_other_at),
+            (dy_own, gx_own_at),
+            (dy_other, gx_other_at),
+        )
+    ):
+        if summing and index % 2 == 1:
+            stores.append(
+                pltpu.make_async_remote_copy(
+                    src_ref=source,
+                    dst_ref=target,
+                    send_sem=store_sem.at[index],
+                    recv_sem=store_sem.at[4 + index // 2],
+                    device_id=lines.partner(),
+                    device_id_type=pl.DeviceIdType.MESH,
+                )
             )
-        )
-    ]
+        else:
+            stores.append(pltpu.make_async_copy(source, target, store_sem.at[index]))
 
     def x_rows(rows):
         return join_columns(head, x_own[rows, :].astype(f32), x_other[rows, :].astype(f32))
@@ -887,12 +899,12 @@
 
 
 def rows_spec(width):
-    return pl.BlockSpec((TILE, width), lambda i: (i, 0))
+    return pl.BlockSpec((TILE, width), lambda i, *_: (i, 0))
 
 
 def whole_spec(shape):
     rank = len(shape)
-    return pl.BlockSpec(shape, lambda i: (0,) * rank, pipeline_mode=pl.Buffered(1))
+    return pl.BlockSpec(shape, lambda i, *_: (0,) * rank, pipeline_mode=pl.Buffered(1))
 
 
 def shaped(shape, dtype=bf16):
@@ -921,11 +933,13 @@
     table = span_table()
     qkv, bars, probs, ctx = pl.pallas_call(
         forward_attention,
+        grid_spec=pltpu.PrefetchScalarGridSpec(
+        num_scalar_prefetch=1,
         grid=(TILES,),
         in_specs=[
             smem_spec,
-            rows_spec(HALF),
-            rows_spec(HALF),
+            pl.BlockSpec((TILE, HALF), lambda i, head: (head[0] * TILES + i, 0)),
+            pl.BlockSpec((TILE, HALF), lambda i, head: (head[0] * TILES + i, 0)),
             whole_spec((4, D)),
             whole_spec((3, D, HALF)),
             whole_spec((3, D, HALF)),
@@ -934,19 +948,20 @@
         out_specs=[
             rows_spec(3 * D),
             rows_spec(2 * D),
-            pl.BlockSpec((SPANS_TILE * PAIRS, 2 * SPAN, 2 * SPAN), lambda i: (i, 0, 0)),
+            pl.BlockSpec((SPANS_TILE * PAIRS, 2 * SPAN, 2 * SPAN), lambda i, head: (i, 0, 0)),
             rows_spec(D),
         ],
+        scratch_shapes=[pltpu.VMEM((SPAN, 2 * D), f32), pltpu.VMEM((TILE, D), bf16)],
+        ),
         out_shape=[
             shaped((SEQ, 3 * D)),
             shaped((SEQ, 2 * D)),
             shaped((ROWS * PAIRS, 2 * SPAN, 2 * SPAN)),
             shaped((SEQ, D)),
         ],
-        scratch_shapes=[pltpu.VMEM((SPAN, 2 * D), f32), pltpu.VMEM((TILE, D), bf16)],
         compiler_params=limits,
         name="forward_attention",
-    )(table, x_own, x_other, ln_params, qkv_own, qkv_other, causal_bias())
+    )(lax.axis_index("head").reshape(1), table, x_own, x_other, ln_params, qkv_own, qkv_other, causal_bias())
     count = lax.axis_size("dp")
     summing = whole_slices(count)
     sum_buffers, extra, total_specs, total_shapes = [], {}, [], []
@@ -987,7 +1002,7 @@
             pltpu.SemaphoreType.DMA((9,)),
             pltpu.SemaphoreType.DMA((2 * CHUNKS,)),
             pltpu.SemaphoreType.DMA((2, 3)),
-            pltpu.SemaphoreType.DMA((4,)),
+            pltpu.SemaphoreType.DMA((6,)),
             pltpu.VMEM((SEQ, D), f32),
             pltpu.VMEM((SEQ, 3 * D), bf16),
             pltpu.VMEM((D, SEQ), bf16),
@@ -1031,6 +1046,7 @@
         chips = [grad[0].astype(f32) + swap_heads(grad[1]).astype(f32) for grad in grads]
         pieces = [lax.psum(chip.astype(bf16), "dp") for chip in chips]
         totals = (*pieces, lax.psum(g_ln, ("dp", "head")))
+        y_other, gx_other = swap_heads(y_other), swap_heads(gx_other)
     return (y_own, y_other), (gx_own, gx_other), totals
 
 
@@ -1054,114 +1070,168 @@
     return (weight_new, first_new, second_new)
 
 
-def kind_gradient(kind, refs, step):
-    joined = [
-        jnp.concatenate([ref[part] for part in range(ref.shape[0])], axis=0 if kind == 0 else 1)
-        for ref in refs
+KINDS = (
+    ((3 * D, HALF), 3, D),
+    ((HALF, D), 1, HALF),
+    ((D, FF // 2), 4, 128),
+    ((FF // 2, D), 4, HALF),
+)
+BLOCK_LIST = [(kind, block) for kind in (3, 2, 1, 0) for block in range(KINDS[kind][1])]
+STRIP = 32
+
+
+def strip_gradient(kind, block, strip, pieces):
+    def take(piece, part, start):
+        rows = pl.ds(pl.multiple_of(start + strip * STRIP, STRIP), STRIP)
+        return pieces[piece][part, rows, :].astype(f32)
+
+    if kind == 1:
+        return take(2, 0, 0)
+    if kind == 2:
+        start = 512 + block * 128
+        return jnp.concatenate(
+            [take(piece, part, start) for piece in range(2) for part in range(2)], axis=1
+        )
+    start = (block % 2) * HALF
+    return jnp.concatenate([take(block // 2, part, start) for part in range(2)], axis=1)
+
+
+def finish_step(owners, t_ln, ln, m_ln, v_ln, *refs):
+    refs = list(refs)
+
+    def some(count):
+        taken, refs[:] = refs[:count], refs[count:]
+        return taken
+
+    pieces_at, weights_at, ones_at, twos_at = some(4), some(4), some(4), some(4)
+    rows_at = some(4)
+    owned_at, new_at, first_at, second_at, copy_at = [some(4) for _ in range(5)]
+    y_at, gx_at = some(2)
+    ln_owned, ln_new, ln_first, ln_second = some(4)
+    pieces, weights, ones, twos, owned, copies = [some(4) for _ in range(6)]
+    row_buffer, piece_sem, in_sem, out_sem, row_sem = some(5)
+    head, chip = lax.axis_index("head"), lax.axis_index("dp")
+
+    def block_copies(index, arrays, buffers, sems, back):
+        kind, block = BLOCK_LIST[index]
+        rows = pl.ds(block * KINDS[kind][2], KINDS[kind][2])
+        result = []
+        for which, (array, buffer) in enumerate(zip(arrays, buffers)):
+            outside, inside = array[kind].at[rows], buffer[kind].at[rows]
+            pair = (inside, outside) if back else (outside, inside)
+            result.append(pltpu.make_async_copy(*pair, sems.at[index, which]))
+        return result
+
+    row_reads = [
+        pltpu.make_async_copy(rows_at[index], row_buffer.at[index], row_sem.at[0, index])
+        for index in range(4)
     ]
-    if kind == 0:
-        return joined[0].astype(f32)[None]
-    if kind == 2:
-        return jnp.concatenate(joined, axis=1).astype(f32)
-    if kind == 3:
-        return jnp.where(step < 2, joined[0].astype(f32), joined[1].astype(f32))
-    return joined[0].astype(f32)
-
-
-BLOCKS = (
-    (3, (1, D, HALF), ((3, (2, HALF, HALF), lambda i: (0, i, 0)),)),
-    (1, (HALF, D), ((2, (1, HALF, D), lambda i: (0, i, 0)),)),
-    (
-        4,
-        (128, 1024),
-        (
-            (0, (2, 128, HALF), lambda i: (0, 4 + i, 0)),
-            (1, (2, 128, HALF), lambda i: (0, 4 + i, 0)),
-        ),
-    ),
-    (
-        4,
-        (HALF, D),
-        (
-            (0, (2, HALF, HALF), lambda i: (0, jnp.minimum(i, 1), 0)),
-            (1, (2, HALF, HALF), lambda i: (0, jnp.maximum(i - 2, 0), 0)),
-        ),
-    ),
-)
-
-
-def adam_kernel(kinds, owners, *refs):
-    step = pl.program_id(0)
-    chip = lax.axis_index("dp")
-    ins = sum(len(BLOCKS[kind][2]) + 3 for kind in kinds)
-    inputs, outputs = list(refs[:ins]), list(refs[ins:])
-    first = 0
-    for kind in kinds:
-        grads = [inputs.pop(0) for _ in BLOCKS[kind][2]]
-        weight, one, two = [inputs.pop(0) for _ in range(3)]
-        owned, new, first_new, second_new, copy = [outputs.pop(0) for _ in range(5)]
-        steps = BLOCKS[kind][0]
-
-        @pl.when((step >= first) & (step < first + steps))
-        def _(kind=kind, grads=grads, weight=weight, one=one, two=two, owned=owned, new=new,
-              first_new=first_new, second_new=second_new, copy=copy, first=first):
-            gradient = kind_gradient(kind, grads, step - first)
-            results = adam_step(gradient, weight[...], one[...], two[...], RATES[kind])
-            owned[...] = jnp.where(owners[kind] == chip, gradient, 0.0)
-            new[...] = results[0]
-            first_new[...] = results[1]
-            second_new[...] = results[2]
-            copy[...] = results[0].astype(bf16)
-
-        first += steps
-
-
-def adam_update(kinds, owners, pieces, weights, ones, twos):
-    in_specs, out_specs, out_shape, operands = [smem_spec], [], [], [owners]
-    first = 0
-    for index, kind in enumerate(kinds):
-        steps, block, sources = BLOCKS[kind]
-
-        def place(i, first=first, steps=steps):
-            return jnp.clip(i - first, 0, steps - 1)
-
-        def at(i, place=place, rank=len(block)):
-            return (place(i),) + (0,) * (rank - 1)
-
-        for piece, grad_block, grad_place in sources:
-
-            def grad_at(i, place=place, grad_place=grad_place):
-                return grad_place(place(i))
-
-            in_specs.append(pl.BlockSpec(grad_block, grad_at))
-            operands.append(pieces[piece])
-        spec = pl.BlockSpec(block, at)
-        in_specs += [spec] * 3
-        out_specs += [spec] * 5
-        whole = weights[index].shape
-        out_shape += [shaped(whole, f32)] * 4 + [shaped(whole)]
-        operands += [weights[index], ones[index], twos[index]]
-        first += steps
+    row_writes = [
+        pltpu.make_async_copy(
+            row_buffer.at[index],
+            (y_at, gx_at)[index // 2].at[pl.ds((head if index % 2 == 0 else 1 - head) * SEQ, SEQ)],
+            row_sem.at[1, index],
+        )
+        for index in range(4)
+    ]
+    piece_copies = [
+        pltpu.make_async_copy(pieces_at[index], pieces[index], piece_sem.at[index])
+        for index in range(4)
+    ]
+    count = len(BLOCK_LIST)
+    reads = [
+        block_copies(index, (weights_at, ones_at, twos_at), (weights, ones, twos), in_sem, False)
+        for index in range(count)
+    ]
+    writes = [
+        block_copies(
+            index,
+            (owned_at, new_at, first_at, second_at, copy_at),
+            (owned, weights, ones, twos, copies),
+            out_sem,
+            True,
+        )
+        for index in range(count)
+    ]
+    for copy in piece_copies + [copy for block in reads for copy in block]:
+        copy.start()
+    for copy in row_reads:
+        copy.start()
+    gradient = t_ln[...]
+    results = adam_step(gradient, ln[...], m_ln[...], v_ln[...], RATES[4])
+    ln_owned[...] = jnp.where(owners[4] == chip, gradient, 0.0)
+    ln_new[...], ln_first[...], ln_second[...] = results
+    for copy in piece_copies:
+        copy.wait()
+    for index, (kind, block) in enumerate(BLOCK_LIST):
+        for copy in reads[index]:
+            copy.wait()
+        size = KINDS[kind][2]
+        mine = owners[kind] == chip
+
+        def update(rows, gradient, kind=kind, mine=mine):
+            results = adam_step(
+                gradient, weights[kind][rows], ones[kind][rows], twos[kind][rows], RATES[kind]
+            )
+            owned[kind][rows] = jnp.where(mine, gradient, 0.0)
+            weights[kind][rows], ones[kind][rows], twos[kind][rows] = results
+            copies[kind][rows] = results[0].astype(bf16)
+
+        def strips(strip, carry, kind=kind, block=block, size=size, update=update):
+            start = block * size + strip * STRIP
+            if kind == 0:
+                source = pl.ds(pl.multiple_of(block * HALF + strip * STRIP, STRIP), STRIP)
+                for part in range(2):
+                    rows = pl.ds(pl.multiple_of(start + part * HALF, STRIP), STRIP)
+                    update(rows, pieces[3][part, source, :].astype(f32))
+            else:
+                rows = pl.ds(pl.multiple_of(start, STRIP), STRIP)
+                update(rows, strip_gradient(kind, block, strip, pieces))
+            return carry
+
+        lax.fori_loop(0, (HALF if kind == 0 else size) // STRIP, strips, 0)
+        for copy in writes[index]:
+            copy.start()
+    for read, write in zip(row_reads, row_writes):
+        read.wait()
+        write.start()
+    for copy in row_writes + [copy for block in writes for copy in block]:
+        copy.wait()
+
+
+def update_all(owners, pieces, t_ln, ln_all, weights, ones, twos, rows):
+    anywhere = pl.BlockSpec(memory_space=pl.ANY)
+    vmem = pl.BlockSpec(memory_space=pltpu.VMEM)
+    shapes = [kind[0] for kind in KINDS]
+    whole = [shaped(shape, f32) for shape in shapes]
+    buffers = [pltpu.VMEM(shape, f32) for shape in shapes]
     results = pl.pallas_call(
-        functools.partial(adam_kernel, kinds),
-        grid=(first,),
-        in_specs=in_specs,
-        out_specs=out_specs,
-        out_shape=out_shape,
+        finish_step,
+        in_specs=[smem_spec] + [vmem] * 4 + [anywhere] * 20,
+        out_specs=[anywhere] * 22 + [vmem] * 4,
+        out_shape=whole * 4
+        + [shaped(shape) for shape in shapes]
+        + [shaped((2 * SEQ, HALF))] * 2
+        + [shaped((4, D), f32)] * 4,
+        scratch_shapes=[pltpu.VMEM(piece.shape, bf16) for piece in pieces]
+        + buffers * 4
+        + [pltpu.VMEM(shape, bf16) for shape in shapes]
+        + [
+            pltpu.VMEM((4, SEQ, HALF), bf16),
+            pltpu.SemaphoreType.DMA((4,)),
+            pltpu.SemaphoreType.DMA((len(BLOCK_LIST), 3)),
+            pltpu.SemaphoreType.DMA((len(BLOCK_LIST), 5)),
+            pltpu.SemaphoreType.DMA((2, 4)),
+        ],
         compiler_params=limits,
-        name="adam_update",
-    )(*operands)
-    return [results[index * 5 : index * 5 + 5] for index in range(len(kinds))]
+        name="update_all",
+    )(owners, t_ln, *ln_all, *pieces, *weights, *ones, *twos, *rows)
+    return results[:20], results[20:22], results[22:]
 
 
 def gather_inputs(tokens, cotangent, w_qkv, w_out, w_up, w_down):
-    head = lax.axis_index("head")
-
     def both(array):
-        halves = array.reshape(2, SEQ, HALF)
-        own = lax.dynamic_index_in_dim(halves, head, 0, keepdims=False)
-        other = lax.dynamic_index_in_dim(halves, 1 - head, 0, keepdims=False)
-        return own, swap_heads(other)
+        return array, swap_heads(array)
 
     x_own, x_other = both(tokens)
     qkv_own = w_qkv.transpose(1, 0, 2).astype(bf16)
@@ -1169,27 +1239,23 @@
     up_own = w_up.astype(bf16)
     down_own = w_down.astype(bf16)
     qkv_other = swap_heads(qkv_own)
-    dy_own, dy_other = both(cotangent)
+    later, _, _ = lax.optimization_barrier((cotangent, x_other, qkv_other))
+    dy_own, dy_other = cotangent, swap_heads(later)
+
+    def swap_later(value):
+        return swap_heads(lax.optimization_barrier((value, x_other, qkv_other))[0])
+
     weights = (
         qkv_own,
         qkv_other,
         out_own,
         swap_heads(out_own),
         up_own,
-        swap_heads(up_own),
+        swap_later(up_own),
         down_own,
-        swap_heads(down_own),
+        swap_later(down_own),
     )
     return x_own, x_other, dy_own, dy_other, weights
-
-
-def place_rows(pieces):
-    head = lax.axis_index("head")
-    own, away = pieces
-    arrived = swap_heads(away)
-    return jnp.concatenate(
-        [jnp.where(head == 0, own, arrived), jnp.where(head == 0, arrived, own)], axis=0
-    )
 
 
 def body(
@@ -1219,31 +1285,30 @@
     y, gx, totals = layer_local(
         x_own, x_other, dy_own, dy_other, lengths, ln_params, weights
     )
-    output_rows = place_rows(y)
-    grad_input = place_rows(gx)
     *pieces, t_ln = totals
 
-    def as_blocks(array):
-        return array.transpose(1, 0, 2)
-
-    results = adam_update(
-        (0, 1, 2, 3),
+    def as_rows(array):
+        return array.transpose(1, 0, 2).reshape(3 * D, HALF)
+
+    results, (output_rows, grad_input), ln_results = update_all(
         owners,
         pieces,
-        (as_blocks(w_qkv), w_out, w_up, w_down),
-        (as_blocks(m_qkv), m_out, m_up, m_down),
-        (as_blocks(v_qkv), v_out, v_up, v_down),
+        t_ln,
+        (ln_params, m_ln, v_ln),
+        (as_rows(w_qkv), w_out, w_up, w_down),
+        (as_rows(m_qkv), m_out, m_up, m_down),
+        (as_rows(v_qkv), v_out, v_up, v_down),
+        (*y, *gx),
     )
-    results[0] = [as_blocks(array) for array in results[0]]
-    mine = owners[4] == lax.axis_index("dp")
-    ln_results = adam_step(t_ln, ln_params, m_ln, v_ln, RATES[4])
-    results.append([jnp.where(mine, t_ln, 0.0), *ln_results])
-    owned, new, first, second = [
-        tuple(results[kind][slot] for kind in range(5)) for slot in range(4)
-    ]
-    copies = tuple(results[kind][4] for kind in range(4))
-    owned = tuple(array[None] for array in owned)
-    return (output_rows, grad_input) + owned + new + first + second + copies
+    groups = []
+    for slot in range(5):
+        group = list(results[slot * 4 : slot * 4 + 4])
+        group[0] = group[0].reshape(3, D, HALF).transpose(1, 0, 2)
+        if slot < 4:
+            group.append(ln_results[slot])
+        groups.append(tuple(group))
+    owned = tuple(array[None] for array in groups[0])
+    return (output_rows, grad_input) + owned + groups[1] + groups[2] + groups[3] + groups[4]
 
 
 PLACED = (

time: 181 us -> 166 us (0.917)
  Pallas kernels: 163 us -> 154 us
  local copies, waits for them, and re-layouts: 6.97 us -> 1.57 us
  waiting for transfers between devices: 0.52 us -> 3.16 us
    pallas_call x1, Pallas kernels: 124 us -> 116 us  [layer_local(): pl.pallas_call(functools.partial(mlp_and_back, count), in_specs=[smem_spe...]
    squeeze x2 -> x0, local copies, waits for them, and re-layouts: 4.25 us -> none  [both(): other = lax.dynamic_index_in_dim(halves, 1 - head, 0, keepdims=False)]
    concatenate x2 -> x0, other arithmetic: 2.91 us -> none  [place_rows(): jnp.concatenate([jnp.where(head == 0, own, arrived), jnp.where(head == 0,...]
    ppermute x8 -> x6, waiting for transfers between devices: 0.52 us -> 3.16 us  [swap_heads(): return lax.ppermute(value, 'head', [(0, 1), (1, 0)])]
  transfers between devices with their start and end apart: 8 -> 6, of which waited for: 1 -> 1; matrix products, arithmetic and copies ran while one was open for 4% -> 2% of each run, Pallas kernels for 22% -> 10%
where the time goes in v5:
time: 166 us
  Pallas kernels  154 us (93%)
  other arithmetic  4 us (2%)
  waiting for transfers between devices  3.16 us (2%)
  starting transfers between devices  1.86 us (1%)
    pallas_call x1, Pallas kernels, layer_local(): pl.pallas_call(functools.partial(mlp_and_back, count), in_specs=[smem_spe...  116 us
    pallas_call x1, Pallas kernels, update_all(): pl.pallas_call(finish_step, in_specs=[smem_spec] + [vmem] * 4 + [anywhere...  21.6 us
    pallas_call x1, Pallas kernels, layer_local(): pl.pallas_call(forward_attention, grid_spec=pltpu.PrefetchScalarGridSpec(...  16.6 us
  transfers between devices with their start and end apart: 6, of which 1 were waited for; matrix products, arithmetic and copies ran while one was open for 2% of the time, Pallas kernels for 10%

profile of v5, /device:TPU:0, one launch (start us, length us, event | category | flops | bytes accessed | tf_op | source)
XLA Modules:
  0.0 165.6 jit_solution(10856651876846092770)
XLA Ops:
  0.7 0.0 copy-start
  0.7 0.5 collective-permute-start
  1.2 1.6 bitcast_convert_fusion.w_own.w_own_at
  2.8 0.0 copy-start.3
  2.8 0.0 copy-start.1
  2.8 0.1 collective-permute-start.1
  3.0 3.2 %collective-permute-done.1.w_other.w_other_at = bf16[3,512,256]{2,1,0:T(8,128)(2,1)S(1)} collective-permute-done((bf16[3,512,256]{2,1,0:T(8,128)(2,1)S(1)}, bf16[3,512,256]{2,1,0:T(8,128)(2,1)S(1)}, u32[]{:S(2)}, u32[]{:S(2)}) %collective-permute-start.1) | collective-permute-done | bytes 786464 | tf_op jit(solution)/shard_map/ppermute | solution.py:167
  6.1 0.0 copy-start.4
  6.1 0.0 collective-permute-done.x_other.x_other_at
  6.1 0.9 copy-done.4
  7.0 0.0 copy-start.2
  7.0 0.4 collective-permute-start.2
  7.4 0.0 copy-done
  7.4 1.3 convert_element_type.14.up_own
  8.6 0.0 copy-done.1
  8.7 0.0 copy-start.5
  8.7 1.1 convert_element_type.15.down_own
  9.8 0.0 copy-done.3
  9.8 0.0 copy-done.2
  9.8 0.2 collective-permute-start.4
  10.0 0.3 collective-permute-start.5
  10.3 0.0 copy-done.5
  10.3 0.0 copy-start.6
  10.3 0.3 collective-permute-start.3
  10.6 16.6 %forward_attention.1 = (bf16[2048,1536]{1,0:T(8,128)(2,1)}, bf16[2048,1024]{1,0:T(8,128)(2,1)}, bf16[64,256,256]{2,1,0:T(8,128)(2,1)}, bf16[2048,512]{1,0:T(8,128)(2,1)}) custom-call(s32[1]{0:T(128)} %bitcast.1.head_at, f32[2,16]{1,0:T(2,128)} %constant.8.clone.table, bf16[4096,256]{1,0:T(8,128)(2,1)} %x_own_at.1, bf16[4096,256]{1,0:T(8,128)(2,1)} %copy-done.2, ...), custom_call_target="tpu_custom_call" | custom-call | tf_op jit(solution)/shard_map/forward_attention/pallas_call | solution.py:934
  27.2 0.0 copy-done.6
  27.2 0.0 collective-permute-done.3.out_other_at
  27.3 0.0 copy-start.7
  27.3 0.0 collective-permute-done.4.up_other
  27.3 0.0 collective-permute-done.5.down_other
  27.3 0.0 collective-permute-done.2.dy_other_at
  27.3 0.7 copy-done.7
  28.0 115.9 %mlp_and_back.1 = (bf16[2048,256]{1,0:T(8,128)(2,1)}, bf16[2048,256]{1,0:T(8,128)(2,1)}, bf16[2048,256]{1,0:T(8,128)(2,1)}, bf16[2048,256]{1,0:T(8,128)(2,1)}, b...) custom-call(f32[2,16]{1,0:T(2,128)} %constant.8.clone.table, ...), custom_call_target="tpu_custom_call" | custom-call | tf_op jit(solution)/shard_map/mlp_and_back/pallas_call | solution.py:982
  143.8 21.6 %update_all.1 = (f32[1536,256]{1,0:T(8,128)}, f32[256,512]{1,0:T(8,128)}, f32[512,1024]{1,0:T(8,128)}, f32[1024,512]{1,0:T(8,128)}, f32[1536,256]{1,0:T(8,128)},...) custom-call(s32[5]{0:T(128)} %owners.1, ...), custom_call_target="tpu_custom_call" | custom-call | tf_op jit(solution)/shard_map/update_all/pallas_call | solution.py:1208
  (1 shorter events, 0.0 us)
Async XLA Ops:
  0.7 6.7 %copy-start = (f32[512,1024]{1,0:T(8,128)S(1)}, f32[512,1024]{1,0:T(8,128)}, u32[]{:S(2)}) copy-start(f32[512,1024]{1,0:T(8,128)} %refs_6_.1) | copy-start | bytes 6291460
  0.7 5.4 %collective-permute-start = (bf16[4096,256]{1,0:T(8,128)(2,1)}, bf16[4096,256]{1,0:T(8,128)(2,1)S(1)}, u32[]{:S(2)}, u32[]{:S(2)}) collective-permute-start(bf16[4096,256]{1,0:T(8,128)(2,1)} %x_own_at.1), channel_id=1, source_target_pairs={{0,1},{1,0},{2,3},{3,2},{4,5},{5,4},{6,7},{7,6},{8,9},{9,8},{10,11... | collective-permute-start | bytes 6291464 | tf_op jit(solution)/shard_map/ppermute | solution.py:167
  2.8 7.0 %copy-start.3 = (bf16[3,512,256]{2,1,0:T(8,128)(2,1)}, bf16[3,512,256]{2,1,0:T(8,128)(2,1)S(1)}, u32[]{:S(2)}) copy-start(bf16[3,512,256]{2,1,0:T(8,128)(2,1)S(1)} %bitcast_convert_fusion.w_own.w_own_at) | copy-start | bytes 2359300
  2.8 5.8 %copy-start.1 = (f32[1024,512]{1,0:T(8,128)S(1)}, f32[1024,512]{1,0:T(8,128)}, u32[]{:S(2)}) copy-start(f32[1024,512]{1,0:T(8,128)} %refs_7_.1) | copy-start | bytes 6291460
  2.8 3.3 %collective-permute-start.1 = (bf16[3,512,256]{2,1,0:T(8,128)(2,1)S(1)}, bf16[3,512,256]{2,1,0:T(8,128)(2,1)S(1)}, u32[]{:S(2)}, u32[]{:S(2)}) collective-permute-start(bf16[3,512,256]{2,1,0:T(8,128)(2,1)S(1)} %bitcast_convert_fusion.w_own.w_own_at), channel_id=1, source_target_pairs={{0,1},{1,0},{2,3},{3,2},{4,5},{5,4},{6,7},{7,6},{8,9},{9,8},{10,11... | collective-permute-start | bytes 2359304 | tf_op jit(solution)/shard_map/ppermute | solution.py:167
  6.1 0.9 copy-start.4
  7.0 2.8 %copy-start.2 = (bf16[4096,256]{1,0:T(8,128)(2,1)}, bf16[4096,256]{1,0:T(8,128)(2,1)S(1)}, u32[]{:S(2)}) copy-start(bf16[4096,256]{1,0:T(8,128)(2,1)S(1)} %collective-permute-done.x_other.x_other_at) | copy-start | bytes 6291460
  7.0 20.3 %collective-permute-start.2 = (bf16[4096,256]{1,0:T(8,128)(2,1)}, bf16[4096,256]{1,0:T(8,128)(2,1)}, u32[]{:S(2)}, u32[]{:S(2)}) collective-permute-start(bf16[4096,256]{1,0:T(8,128)(2,1)} %dy_own_at.1), channel_id=1, source_target_pairs={{0,1},{1,0},{2,3},{3,2},{4,5},{5,4},{6,7},{7,6},{8,9},{9,8},{10,11... | collective-permute-start | bytes 6291464 | tf_op jit(solution)/shard_map/ppermute | solution.py:167
  8.7 1.6 copy-start.5
  9.8 17.5 %collective-permute-start.4 = (bf16[512,1024]{1,0:T(8,128)(2,1)}, bf16[512,1024]{1,0:T(8,128)(2,1)}, u32[]{:S(2)}, u32[]{:S(2)}) collective-permute-start(bf16[512,1024]{1,0:T(8,128)(2,1)} %convert_element_type.14.up_own), channel_id=1, source_target_pairs={{0,1},{1,0},{2,3},{3,2},{4,5},{5,4},{6,7},{7,6},{8,9},{9,8},{10,11... | collective-permute-start | bytes 3145736 | tf_op jit(solution)/shard_map/ppermute | solution.py:167
  10.0 17.3 %collective-permute-start.5 = (bf16[1024,512]{1,0:T(8,128)(2,1)}, bf16[1024,512]{1,0:T(8,128)(2,1)}, u32[]{:S(2)}, u32[]{:S(2)}) collective-permute-start(bf16[1024,512]{1,0:T(8,128)(2,1)} %convert_element_type.15.down_own), channel_id=1, source_target_pairs={{0,1},{1,0},{2,3},{3,2},{4,5},{5,4},{6,7},{7,6},{8,9},{9,8},{10,11... | collective-permute-start | bytes 3145736 | tf_op jit(solution)/shard_map/ppermute | solution.py:167
  10.3 16.9 %copy-start.6 = (bf16[256,512]{1,0:T(8,128)(2,1)}, bf16[256,512]{1,0:T(8,128)(2,1)S(1)}, u32[]{:S(2)}) copy-start(bf16[256,512]{1,0:T(8,128)(2,1)S(1)} %convert_element_type.13.out_own_at) | copy-start | bytes 786436
  10.3 16.9 %collective-permute-start.3 = (bf16[256,512]{1,0:T(8,128)(2,1)S(1)}, bf16[256,512]{1,0:T(8,128)(2,1)S(1)}, u32[]{:S(2)}, u32[]{:S(2)}) collective-permute-start(bf16[256,512]{1,0:T(8,128)(2,1)S(1)} %convert_element_type.13.out_own_at), channel_id=1, source_target_pairs={{0,1},{1,0},{2,3},{3,2},{4,5},{5,4},{6,7},{7,6},{8,9},{9,8},{10,11... | collective-permute-start | bytes 786440 | tf_op jit(solution)/shard_map/ppermute | solution.py:167
  27.3 0.7 copy-start.7

commit v6 on v5

--- a/solution.py
+++ b/solution.py
@@ -883,7 +883,7 @@
                 for which, times in enumerate(EVENT_AT)
                 if len(times) + index < EVENTS
             ]
-            run_events(left)
+            run_events(left[::-1])
             if index <= 3:
                 small.finish(index)
             if index < 3:

time: 166 us -> 164 us (0.988)
  Pallas kernels: 154 us -> 152 us
    pallas_call x1, Pallas kernels: 116 us -> 114 us  [layer_local(): pl.pallas_call(functools.partial(mlp_and_back, count), in_specs=[smem_spe...]
where the time goes in v6:
time: 164 us
  Pallas kernels  152 us (93%)
  other arithmetic  4 us (2%)
  waiting for transfers between devices  3.16 us (2%)
  starting transfers between devices  1.86 us (1%)
    pallas_call x1, Pallas kernels, layer_local(): pl.pallas_call(functools.partial(mlp_and_back, count), in_specs=[smem_spe...  114 us
    pallas_call x1, Pallas kernels, update_all(): pl.pallas_call(finish_step, in_specs=[smem_spec] + [vmem] * 4 + [anywhere...  21.6 us
    pallas_call x1, Pallas kernels, layer_local(): pl.pallas_call(forward_attention, grid_spec=pltpu.PrefetchScalarGridSpec(...  16.6 us
  transfers between devices with their start and end apart: 6, of which 1 were waited for; matrix products, arithmetic and copies ran while one was open for 2% of the time, Pallas kernels for 10%

profile of v6, /device:TPU:0, one launch (start us, length us, event | category | flops | bytes accessed | tf_op | source)
XLA Modules:
  0.0 163.5 jit_solution(14915842035779613901)
XLA Ops:
  0.7 0.0 copy-start
  0.7 0.5 collective-permute-start
  1.2 1.6 bitcast_convert_fusion.w_own.w_own_at
  2.8 0.0 copy-start.3
  2.8 0.0 copy-start.1
  2.8 0.1 collective-permute-start.1
  3.0 3.2 %collective-permute-done.1.w_other.w_other_at = bf16[3,512,256]{2,1,0:T(8,128)(2,1)S(1)} collective-permute-done((bf16[3,512,256]{2,1,0:T(8,128)(2,1)S(1)}, bf16[3,512,256]{2,1,0:T(8,128)(2,1)S(1)}, u32[]{:S(2)}, u32[]{:S(2)}) %collective-permute-start.1) | collective-permute-done | bytes 786464 | tf_op jit(solution)/shard_map/ppermute | solution.py:167
  6.1 0.0 copy-start.4
  6.1 0.0 collective-permute-done.x_other.x_other_at
  6.1 0.9 copy-done.4
  7.0 0.0 copy-start.2
  7.0 0.4 collective-permute-start.2
  7.4 0.0 copy-done
  7.4 1.3 convert_element_type.14.up_own
  8.6 0.0 copy-done.1
  8.7 0.0 copy-start.5
  8.7 1.1 convert_element_type.15.down_own
  9.8 0.0 copy-done.3
  9.8 0.0 copy-done.2
  9.8 0.2 collective-permute-start.4
  10.0 0.3 collective-permute-start.5
  10.3 0.0 copy-done.5
  10.3 0.0 copy-start.6
  10.3 0.3 collective-permute-start.3
  10.6 16.6 %forward_attention.1 = (bf16[2048,1536]{1,0:T(8,128)(2,1)}, bf16[2048,1024]{1,0:T(8,128)(2,1)}, bf16[64,256,256]{2,1,0:T(8,128)(2,1)}, bf16[2048,512]{1,0:T(8,128)(2,1)}) custom-call(s32[1]{0:T(128)} %bitcast.1.head_at, f32[2,16]{1,0:T(2,128)} %constant.8.clone.table, bf16[4096,256]{1,0:T(8,128)(2,1)} %x_own_at.1, bf16[4096,256]{1,0:T(8,128)(2,1)} %copy-done.2, ...), custom_call_target="tpu_custom_call" | custom-call | tf_op jit(solution)/shard_map/forward_attention/pallas_call | solution.py:934
  27.2 0.0 copy-done.6
  27.2 0.0 collective-permute-done.3.out_other_at
  27.3 0.0 copy-start.7
  27.3 0.0 collective-permute-done.4.up_other
  27.3 0.0 collective-permute-done.5.down_other
  27.3 0.0 collective-permute-done.2.dy_other_at
  27.3 0.7 copy-done.7
  28.0 113.8 %mlp_and_back.1 = (bf16[2048,256]{1,0:T(8,128)(2,1)}, bf16[2048,256]{1,0:T(8,128)(2,1)}, bf16[2048,256]{1,0:T(8,128)(2,1)}, bf16[2048,256]{1,0:T(8,128)(2,1)}, b...) custom-call(f32[2,16]{1,0:T(2,128)} %constant.8.clone.table, ...), custom_call_target="tpu_custom_call" | custom-call | tf_op jit(solution)/shard_map/mlp_and_back/pallas_call | solution.py:982
  141.8 21.6 %update_all.1 = (f32[1536,256]{1,0:T(8,128)}, f32[256,512]{1,0:T(8,128)}, f32[512,1024]{1,0:T(8,128)}, f32[1024,512]{1,0:T(8,128)}, f32[1536,256]{1,0:T(8,128)},...) custom-call(s32[5]{0:T(128)} %owners.1, ...), custom_call_target="tpu_custom_call" | custom-call | tf_op jit(solution)/shard_map/update_all/pallas_call | solution.py:1208
  (1 shorter events, 0.0 us)
Async XLA Ops:
  0.7 6.7 %copy-start = (f32[512,1024]{1,0:T(8,128)S(1)}, f32[512,1024]{1,0:T(8,128)}, u32[]{:S(2)}) copy-start(f32[512,1024]{1,0:T(8,128)} %refs_6_.1) | copy-start | bytes 6291460
  0.7 5.4 %collective-permute-start = (bf16[4096,256]{1,0:T(8,128)(2,1)}, bf16[4096,256]{1,0:T(8,128)(2,1)S(1)}, u32[]{:S(2)}, u32[]{:S(2)}) collective-permute-start(bf16[4096,256]{1,0:T(8,128)(2,1)} %x_own_at.1), channel_id=1, source_target_pairs={{0,1},{1,0},{2,3},{3,2},{4,5},{5,4},{6,7},{7,6},{8,9},{9,8},{10,11... | collective-permute-start | bytes 6291464 | tf_op jit(solution)/shard_map/ppermute | solution.py:167
  2.8 7.0 %copy-start.3 = (bf16[3,512,256]{2,1,0:T(8,128)(2,1)}, bf16[3,512,256]{2,1,0:T(8,128)(2,1)S(1)}, u32[]{:S(2)}) copy-start(bf16[3,512,256]{2,1,0:T(8,128)(2,1)S(1)} %bitcast_convert_fusion.w_own.w_own_at) | copy-start | bytes 2359300
  2.8 5.8 %copy-start.1 = (f32[1024,512]{1,0:T(8,128)S(1)}, f32[1024,512]{1,0:T(8,128)}, u32[]{:S(2)}) copy-start(f32[1024,512]{1,0:T(8,128)} %refs_7_.1) | copy-start | bytes 6291460
  2.8 3.3 %collective-permute-start.1 = (bf16[3,512,256]{2,1,0:T(8,128)(2,1)S(1)}, bf16[3,512,256]{2,1,0:T(8,128)(2,1)S(1)}, u32[]{:S(2)}, u32[]{:S(2)}) collective-permute-start(bf16[3,512,256]{2,1,0:T(8,128)(2,1)S(1)} %bitcast_convert_fusion.w_own.w_own_at), channel_id=1, source_target_pairs={{0,1},{1,0},{2,3},{3,2},{4,5},{5,4},{6,7},{7,6},{8,9},{9,8},{10,11... | collective-permute-start | bytes 2359304 | tf_op jit(solution)/shard_map/ppermute | solution.py:167
  6.1 0.9 copy-start.4
  7.0 2.8 %copy-start.2 = (bf16[4096,256]{1,0:T(8,128)(2,1)}, bf16[4096,256]{1,0:T(8,128)(2,1)S(1)}, u32[]{:S(2)}) copy-start(bf16[4096,256]{1,0:T(8,128)(2,1)S(1)} %collective-permute-done.x_other.x_other_at) | copy-start | bytes 6291460
  7.0 20.3 %collective-permute-start.2 = (bf16[4096,256]{1,0:T(8,128)(2,1)}, bf16[4096,256]{1,0:T(8,128)(2,1)}, u32[]{:S(2)}, u32[]{:S(2)}) collective-permute-start(bf16[4096,256]{1,0:T(8,128)(2,1)} %dy_own_at.1), channel_id=1, source_target_pairs={{0,1},{1,0},{2,3},{3,2},{4,5},{5,4},{6,7},{7,6},{8,9},{9,8},{10,11... | collective-permute-start | bytes 6291464 | tf_op jit(solution)/shard_map/ppermute | solution.py:167
  8.7 1.6 copy-start.5
  9.8 17.5 %collective-permute-start.4 = (bf16[512,1024]{1,0:T(8,128)(2,1)}, bf16[512,1024]{1,0:T(8,128)(2,1)}, u32[]{:S(2)}, u32[]{:S(2)}) collective-permute-start(bf16[512,1024]{1,0:T(8,128)(2,1)} %convert_element_type.14.up_own), channel_id=1, source_target_pairs={{0,1},{1,0},{2,3},{3,2},{4,5},{5,4},{6,7},{7,6},{8,9},{9,8},{10,11... | collective-permute-start | bytes 3145736 | tf_op jit(solution)/shard_map/ppermute | solution.py:167
  10.0 17.3 %collective-permute-start.5 = (bf16[1024,512]{1,0:T(8,128)(2,1)}, bf16[1024,512]{1,0:T(8,128)(2,1)}, u32[]{:S(2)}, u32[]{:S(2)}) collective-permute-start(bf16[1024,512]{1,0:T(8,128)(2,1)} %convert_element_type.15.down_own), channel_id=1, source_target_pairs={{0,1},{1,0},{2,3},{3,2},{4,5},{5,4},{6,7},{7,6},{8,9},{9,8},{10,11... | collective-permute-start | bytes 3145736 | tf_op jit(solution)/shard_map/ppermute | solution.py:167
  10.3 16.9 %copy-start.6 = (bf16[256,512]{1,0:T(8,128)(2,1)}, bf16[256,512]{1,0:T(8,128)(2,1)S(1)}, u32[]{:S(2)}) copy-start(bf16[256,512]{1,0:T(8,128)(2,1)S(1)} %convert_element_type.13.out_own_at) | copy-start | bytes 786436
  10.3 16.9 %collective-permute-start.3 = (bf16[256,512]{1,0:T(8,128)(2,1)S(1)}, bf16[256,512]{1,0:T(8,128)(2,1)S(1)}, u32[]{:S(2)}, u32[]{:S(2)}) collective-permute-start(bf16[256,512]{1,0:T(8,128)(2,1)S(1)} %convert_element_type.13.out_own_at), channel_id=1, source_target_pairs={{0,1},{1,0},{2,3},{3,2},{4,5},{5,4},{6,7},{7,6},{8,9},{9,8},{10,11... | collective-permute-start | bytes 786440 | tf_op jit(solution)/shard_map/ppermute | solution.py:167
  27.3 0.7 copy-start.7

commit v7 on v6

--- a/solution.py
+++ b/solution.py
@@ -1192,9 +1192,10 @@
         lax.fori_loop(0, (HALF if kind == 0 else size) // STRIP, strips, 0)
         for copy in writes[index]:
             copy.start()
-    for read, write in zip(row_reads, row_writes):
-        read.wait()
-        write.start()
+        if index == count - 3:
+            for read, write in zip(row_reads, row_writes):
+                read.wait()
+                write.start()
     for copy in row_writes + [copy for block in writes for copy in block]:
         copy.wait()
 

time: 164 us -> 164 us (level)
  no operation moved by 1% of the time
where the time goes in v7:
time: 164 us; the launch traced here: 163 us
  Pallas kernels  152 us (93%)
  other arithmetic  4 us (2%)
  waiting for transfers between devices  3.16 us (2%)
  starting transfers between devices  1.86 us (1%)
    pallas_call x1, Pallas kernels, layer_local(): pl.pallas_call(functools.partial(mlp_and_back, count), in_specs=[smem_spe...  114 us
    pallas_call x1, Pallas kernels, update_all(): pl.pallas_call(finish_step, in_specs=[smem_spec] + [vmem] * 4 + [anywhere...  21.5 us
    pallas_call x1, Pallas kernels, layer_local(): pl.pallas_call(forward_attention, grid_spec=pltpu.PrefetchScalarGridSpec(...  16.6 us
  transfers between devices with their start and end apart: 6, of which 1 were waited for; matrix products, arithmetic and copies ran while one was open for 2% of the time, Pallas kernels for 10%

profile of v7, /device:TPU:0, one launch (start us, length us, event | category | flops | bytes accessed | tf_op | source)
XLA Modules:
  0.0 163.4 jit_solution(8314766354100723745)
XLA Ops:
  0.7 0.0 copy-start
  0.7 0.5 collective-permute-start
  1.2 1.6 bitcast_convert_fusion.w_own.w_own_at
  2.8 0.0 copy-start.3
  2.8 0.0 copy-start.1
  2.8 0.1 collective-permute-start.1
  3.0 3.2 %collective-permute-done.1.w_other.w_other_at = bf16[3,512,256]{2,1,0:T(8,128)(2,1)S(1)} collective-permute-done((bf16[3,512,256]{2,1,0:T(8,128)(2,1)S(1)}, bf16[3,512,256]{2,1,0:T(8,128)(2,1)S(1)}, u32[]{:S(2)}, u32[]{:S(2)}) %collective-permute-start.1) | collective-permute-done | bytes 786464 | tf_op jit(solution)/shard_map/ppermute | solution.py:167
  6.1 0.0 copy-start.4
  6.1 0.0 collective-permute-done.x_other.x_other_at
  6.1 0.9 copy-done.4
  7.0 0.0 copy-start.2
  7.0 0.4 collective-permute-start.2
  7.4 0.0 copy-done
  7.4 1.3 convert_element_type.14.up_own
  8.6 0.0 copy-done.1
  8.7 0.0 copy-start.5
  8.7 1.1 convert_element_type.15.down_own
  9.8 0.0 copy-done.3
  9.8 0.0 copy-done.2
  9.8 0.2 collective-permute-start.4
  10.0 0.3 collective-permute-start.5
  10.3 0.0 copy-done.5
  10.3 0.0 copy-start.6
  10.3 0.3 collective-permute-start.3
  10.6 16.6 %forward_attention.1 = (bf16[2048,1536]{1,0:T(8,128)(2,1)}, bf16[2048,1024]{1,0:T(8,128)(2,1)}, bf16[64,256,256]{2,1,0:T(8,128)(2,1)}, bf16[2048,512]{1,0:T(8,128)(2,1)}) custom-call(s32[1]{0:T(128)} %bitcast.1.head_at, f32[2,16]{1,0:T(2,128)} %constant.8.clone.table, bf16[4096,256]{1,0:T(8,128)(2,1)} %x_own_at.1, bf16[4096,256]{1,0:T(8,128)(2,1)} %copy-done.2, ...), custom_call_target="tpu_custom_call" | custom-call | tf_op jit(solution)/shard_map/forward_attention/pallas_call | solution.py:934
  27.2 0.0 copy-done.6
  27.2 0.0 collective-permute-done.3.out_other_at
  27.3 0.0 copy-start.7
  27.3 0.0 collective-permute-done.4.up_other
  27.3 0.0 collective-permute-done.5.down_other
  27.3 0.0 collective-permute-done.2.dy_other_at
  27.3 0.7 copy-done.7
  28.0 113.8 %mlp_and_back.1 = (bf16[2048,256]{1,0:T(8,128)(2,1)}, bf16[2048,256]{1,0:T(8,128)(2,1)}, bf16[2048,256]{1,0:T(8,128)(2,1)}, bf16[2048,256]{1,0:T(8,128)(2,1)}, b...) custom-call(f32[2,16]{1,0:T(2,128)} %constant.8.clone.table, ...), custom_call_target="tpu_custom_call" | custom-call | tf_op jit(solution)/shard_map/mlp_and_back/pallas_call | solution.py:982
  141.8 21.5 %update_all.1 = (f32[1536,256]{1,0:T(8,128)}, f32[256,512]{1,0:T(8,128)}, f32[512,1024]{1,0:T(8,128)}, f32[1024,512]{1,0:T(8,128)}, f32[1536,256]{1,0:T(8,128)},...) custom-call(s32[5]{0:T(128)} %owners.1, ...), custom_call_target="tpu_custom_call" | custom-call | tf_op jit(solution)/shard_map/update_all/pallas_call | solution.py:1209
  (1 shorter events, 0.0 us)
Async XLA Ops:
  0.7 6.7 %copy-start = (f32[512,1024]{1,0:T(8,128)S(1)}, f32[512,1024]{1,0:T(8,128)}, u32[]{:S(2)}) copy-start(f32[512,1024]{1,0:T(8,128)} %refs_6_.1) | copy-start | bytes 6291460
  0.7 5.4 %collective-permute-start = (bf16[4096,256]{1,0:T(8,128)(2,1)}, bf16[4096,256]{1,0:T(8,128)(2,1)S(1)}, u32[]{:S(2)}, u32[]{:S(2)}) collective-permute-start(bf16[4096,256]{1,0:T(8,128)(2,1)} %x_own_at.1), channel_id=1, source_target_pairs={{0,1},{1,0},{2,3},{3,2},{4,5},{5,4},{6,7},{7,6},{8,9},{9,8},{10,11... | collective-permute-start | bytes 6291464 | tf_op jit(solution)/shard_map/ppermute | solution.py:167
  2.8 7.0 %copy-start.3 = (bf16[3,512,256]{2,1,0:T(8,128)(2,1)}, bf16[3,512,256]{2,1,0:T(8,128)(2,1)S(1)}, u32[]{:S(2)}) copy-start(bf16[3,512,256]{2,1,0:T(8,128)(2,1)S(1)} %bitcast_convert_fusion.w_own.w_own_at) | copy-start | bytes 2359300
  2.8 5.8 %copy-start.1 = (f32[1024,512]{1,0:T(8,128)S(1)}, f32[1024,512]{1,0:T(8,128)}, u32[]{:S(2)}) copy-start(f32[1024,512]{1,0:T(8,128)} %refs_7_.1) | copy-start | bytes 6291460
  2.8 3.3 %collective-permute-start.1 = (bf16[3,512,256]{2,1,0:T(8,128)(2,1)S(1)}, bf16[3,512,256]{2,1,0:T(8,128)(2,1)S(1)}, u32[]{:S(2)}, u32[]{:S(2)}) collective-permute-start(bf16[3,512,256]{2,1,0:T(8,128)(2,1)S(1)} %bitcast_convert_fusion.w_own.w_own_at), channel_id=1, source_target_pairs={{0,1},{1,0},{2,3},{3,2},{4,5},{5,4},{6,7},{7,6},{8,9},{9,8},{10,11... | collective-permute-start | bytes 2359304 | tf_op jit(solution)/shard_map/ppermute | solution.py:167
  6.1 0.9 copy-start.4
  7.0 2.8 %copy-start.2 = (bf16[4096,256]{1,0:T(8,128)(2,1)}, bf16[4096,256]{1,0:T(8,128)(2,1)S(1)}, u32[]{:S(2)}) copy-start(bf16[4096,256]{1,0:T(8,128)(2,1)S(1)} %collective-permute-done.x_other.x_other_at) | copy-start | bytes 6291460
  7.0 20.3 %collective-permute-start.2 = (bf16[4096,256]{1,0:T(8,128)(2,1)}, bf16[4096,256]{1,0:T(8,128)(2,1)}, u32[]{:S(2)}, u32[]{:S(2)}) collective-permute-start(bf16[4096,256]{1,0:T(8,128)(2,1)} %dy_own_at.1), channel_id=1, source_target_pairs={{0,1},{1,0},{2,3},{3,2},{4,5},{5,4},{6,7},{7,6},{8,9},{9,8},{10,11... | collective-permute-start | bytes 6291464 | tf_op jit(solution)/shard_map/ppermute | solution.py:167
  8.7 1.6 copy-start.5
  9.8 17.5 %collective-permute-start.4 = (bf16[512,1024]{1,0:T(8,128)(2,1)}, bf16[512,1024]{1,0:T(8,128)(2,1)}, u32[]{:S(2)}, u32[]{:S(2)}) collective-permute-start(bf16[512,1024]{1,0:T(8,128)(2,1)} %convert_element_type.14.up_own), channel_id=1, source_target_pairs={{0,1},{1,0},{2,3},{3,2},{4,5},{5,4},{6,7},{7,6},{8,9},{9,8},{10,11... | collective-permute-start | bytes 3145736 | tf_op jit(solution)/shard_map/ppermute | solution.py:167
  10.0 17.3 %collective-permute-start.5 = (bf16[1024,512]{1,0:T(8,128)(2,1)}, bf16[1024,512]{1,0:T(8,128)(2,1)}, u32[]{:S(2)}, u32[]{:S(2)}) collective-permute-start(bf16[1024,512]{1,0:T(8,128)(2,1)} %convert_element_type.15.down_own), channel_id=1, source_target_pairs={{0,1},{1,0},{2,3},{3,2},{4,5},{5,4},{6,7},{7,6},{8,9},{9,8},{10,11... | collective-permute-start | bytes 3145736 | tf_op jit(solution)/shard_map/ppermute | solution.py:167
  10.3 16.9 %copy-start.6 = (bf16[256,512]{1,0:T(8,128)(2,1)}, bf16[256,512]{1,0:T(8,128)(2,1)S(1)}, u32[]{:S(2)}) copy-start(bf16[256,512]{1,0:T(8,128)(2,1)S(1)} %convert_element_type.13.out_own_at) | copy-start | bytes 786436
  10.3 16.9 %collective-permute-start.3 = (bf16[256,512]{1,0:T(8,128)(2,1)S(1)}, bf16[256,512]{1,0:T(8,128)(2,1)S(1)}, u32[]{:S(2)}, u32[]{:S(2)}) collective-permute-start(bf16[256,512]{1,0:T(8,128)(2,1)S(1)} %convert_element_type.13.out_own_at), channel_id=1, source_target_pairs={{0,1},{1,0},{2,3},{3,2},{4,5},{5,4},{6,7},{7,6},{8,9},{9,8},{10,11... | collective-permute-start | bytes 786440 | tf_op jit(solution)/shard_map/ppermute | solution.py:167
  27.3 0.7 copy-start.7
